TPU v7x, 512 devices: a whole 4x8x8 slice. The times are simulated.
512 devices in a mesh: res: 64 (over y, z_lo, x), seq: 8 (over z_hi, core).
Axes of the slice: x: 4, y: 8, z: 8 (z_hi: 4, z_lo: 2; z = z_hi * 2 + z_lo), core: 2. Of those that a mesh axis runs over, the one named last changes fastest.
Arguments:
- aligned_chain_embedding: bfloat16 [512, 768, 256], P('seq', 'res'), may hold values from -6 to 6
- presence_indicator: int32 [512, 768], P('seq', 'res'), may hold values from 0 to 1, as said below
- outer_lhs_embedding: bfloat16 [256, 32], replicated, may hold values from -0.375 to 0.375
- outer_rhs_embedding: bfloat16 [256, 32], replicated, may hold values from -0.375 to 0.375
- final_projection_matrix: bfloat16 [1024, 128], replicated, may hold values from -1 to 1
- final_offset: float32 [128], replicated, may hold values from -3 to 3
Outputs:
- pair: float32 [768, 768, 128], P('res', 'seq')
Inputs may be any that keep to these rules, and one draw needn't show every extreme that they name: `presence_indicator`: 0 or 1 for each sequence and residue.
All inputs are finite; a program needn't handle non-finite values.
Results may differ from a plain program's by a relative error of at most 0.0075.
Values may be sent and summed in bfloat16 or wider, within the bound.
No kernel may reach another device: no remote copies, remote signals or barrier semaphores. Data moves between devices by JAX's collectives and lax.ppermute only.
A program may use at most 64 MiB of HBM per device.

v0:
```python
import jax
import jax.numpy as jnp
from jax import lax
from jax.sharding import PartitionSpec as P


def standardized_activations(aligned_chain_embedding):
    collected_entries = aligned_chain_embedding.astype(jnp.float32)
    center = jnp.mean(collected_entries, axis=-1, keepdims=True)
    spread = jnp.mean((collected_entries - center) ** 2, axis=-1, keepdims=True)
    return (collected_entries - center) * lax.rsqrt(spread + 1e-05)


def local(
    aligned_chain_embedding,
    presence_indicator,
    outer_lhs_embedding,
    outer_rhs_embedding,
    final_projection_matrix,
    final_offset,
):
    homolog_extent, position_extent, discarded_placeholder = aligned_chain_embedding.shape
    width = outer_lhs_embedding.shape[1]
    standardized_source = standardized_activations(aligned_chain_embedding)
    weight_list = presence_indicator.astype(jnp.float32)
    left = (
        jnp.einsum(
            "sik,kc->sic",
            standardized_source,
            outer_lhs_embedding.astype(jnp.float32),
            precision=lax.Precision.HIGHEST,
        )
        * weight_list[:, :, None]
    ).astype(jnp.bfloat16)
    right = (
        jnp.einsum(
            "sik,kc->sic",
            standardized_source,
            outer_rhs_embedding.astype(jnp.float32),
            precision=lax.Precision.HIGHEST,
        )
        * weight_list[:, :, None]
    ).astype(jnp.bfloat16)
    right_rows = right.transpose(1, 0, 2).reshape(position_extent, homolog_extent * width)
    mask_row_slices = presence_indicator.astype(jnp.bfloat16).T
    left_by_res = left.transpose(1, 0, 2)
    right_piece = lax.all_gather(right_rows, "res", axis=0, tiled=True)
    mask_piece = lax.all_gather(mask_row_slices, "res", axis=0, tiled=True)
    rows = right_piece.shape[0]
    right_cube = right_piece.reshape(rows, homolog_extent, width)

    def one_row(left_row):
        outer = jnp.einsum(
            "sc,jse->jce", left_row, right_cube, preferred_element_type=jnp.float32
        ).astype(jnp.bfloat16)
        return jnp.dot(
            outer.reshape(rows, width * width),
            final_projection_matrix,
            preferred_element_type=jnp.float32,
        ).astype(jnp.bfloat16)

    projected = lax.map(one_row, left_by_res)
    counted = jnp.dot(mask_row_slices, mask_piece.T, preferred_element_type=jnp.float32).astype(
        jnp.bfloat16
    )
    projected, counted = (projected, counted)
    total, count = (
        lax.psum_scatter(projected, "seq", scatter_dimension=1, tiled=True).astype(jnp.float32),
        lax.psum_scatter(counted, "seq", scatter_dimension=1, tiled=True).astype(jnp.float32),
    )
    return total / (count[:, :, None] + 1.0) + final_offset


def solution(mesh):
    placed = (P("seq", "res", None), P("seq", "res"), P(), P(), P(), P())
    return jax.shard_map(
        local, mesh=mesh, in_specs=placed, out_specs=P("res", "seq", None), check_vma=False
    )
```

profile of v0, /device:TPU:20, one launch (start us, length us, event | category | flops | bytes accessed | tf_op | source)
XLA Modules:
  0.0 445.9 jit_solution(9848397786632941160)
XLA Ops:
  7.4 0.0 copy-start
  7.4 0.0 all-gather.4.cloned.1.call-start
  7.4 1.2 convert_reduce_fusion
  8.7 1.3 fusion.14
  10.0 0.8 convert_bitcast_fusion.1
  10.8 1.8 fusion.9
  12.6 0.1 copy.11
  12.7 0.8 reshape.27
  13.6 0.0 all-gather.4.cloned.1.call-update
  13.6 0.0 reduce-scatter.7.cloned.1.call-start
  13.7 132.4 %all-gather.1 = bf16[64,12,64]{2,1,0:T(8,128)(2,1)S(1)} all-gather(bf16[1,12,64]{2,1,0:T(8,128)(2,1)S(1)} %get-tuple-element.53), channel_id=1, replica_groups=mesh['res'=64,'seq'=8] {'res'}, dimensions={0}, use_global_device_ids=true | all-gather | bytes 99840 | tf_op jit(solution)/shard_map/all_gather | solution.py:48
  146.0 0.1 reshape.30
  146.2 0.2 convolution_convert_fusion.2
  146.3 0.9 copy.13
  147.2 0.0 reduce-scatter.7.cloned.1.call-update
  147.2 0.0 reduce-scatter.5.cloned.1.call-start
  147.3 0.0 copy-done.1
  147.3 0.0 copy-done.5
  147.3 0.8 fusion.8
  148.1 158.7 %all-gather.4.cloned.1.call-done = bf16[64,12,2048]{2,1,0:T(8,128)(2,1)} async-done(((bf16[1,12,2048]{2,1,0:T(8,128)(2,1)}), bf16[64,12,2048]{2,1,0:T(8,128)(2,1)}) %all-gather.4.cloned.1.call-update) | async-done | bytes 3145744 | tf_op jit(solution)/shard_map/all_gather | solution.py:47
  306.8 15.5 %reshape.26 = bf16[768,64,32]{2,1,0:T(8,128)(2,1)} reshape(bf16[64,12,2048]{2,1,0:T(8,128)(2,1)} %all-gather.4.cloned.1.call-done) | data formatting | bytes 6291456 | tf_op jit(solution)/shard_map/reshape | solution.py:50
  322.2 16.1 %copy.12 = bf16[768,64,32]{0,1,2:T(8,128)(2,1)S(1)} copy(bf16[768,64,32]{2,1,0:T(8,128)(2,1)} %reshape.26) | data formatting | bytes 6291456 | tf_op jit(solution)/shard_map/while | solution.py:62
  338.3 33.0 %while.10 = (s32[]{:T(128)}, bf16[12,768,128]{2,1,0:T(8,128)(2,1)}, bf16[12,64,32]{1,2,0:T(8,128)(2,1)S(1)}, bf16[768,64,32]{0,1,2:T(8,128)(2,1)S(1)}, bf16[1024,128]{1,0:T(8,128)(2,1)S(1)}, /*index=5*/s32[]{:T(128)}) while((s32[]{:T(128)}, bf16[12,768,128]{2,1,0:T(8,128)(2,1)}, bf16[12,64,32]{1,2,0:T(8,128)(2,1)S(1)}, ...), condition=%wide.region_3.4_spmd, body=%wide.region_2.3_spmd.sunk | while | flops 302874624 | bytes 9904713 | solution.py:62
  338.4 0.6 fusion.36
  338.9 0.9 copy.16
  339.8 1.3 fusion.37
  341.1 0.6 fusion.36
  341.7 0.9 copy.16
  342.6 1.3 fusion.37
  343.9 0.6 fusion.36
  344.4 0.9 copy.16
  345.3 1.3 fusion.37
  346.6 0.6 fusion.36
  347.2 0.9 copy.16
  348.1 1.3 fusion.37
  349.4 0.6 fusion.36
  349.9 0.9 copy.16
  350.8 1.3 fusion.37
  352.1 0.6 fusion.36
  352.7 0.9 copy.16
  353.5 1.3 fusion.37
  354.9 0.6 fusion.36
  355.4 0.9 copy.16
  356.3 1.3 fusion.37
  357.6 0.6 fusion.36
  358.2 0.9 copy.16
  359.1 1.3 fusion.37
  360.3 0.6 fusion.36
  360.9 0.9 copy.16
  361.8 1.3 fusion.37
  363.1 0.6 fusion.36
  363.7 0.9 copy.16
  364.5 1.3 fusion.37
  365.9 0.6 fusion.36
  366.4 0.9 copy.16
  367.3 1.3 fusion.37
  368.6 0.6 fusion.36
  369.2 0.9 copy.16
  370.1 1.3 fusion.37
  371.4 0.0 reduce-scatter.5.cloned.1.call-update
  371.4 0.0 reduce-scatter.7.cloned.1.call-done
  371.4 0.8 copy.14
  372.2 64.3 %reduce-scatter.5.cloned.1.call-done = bf16[12,96,128]{2,1,0:T(8,128)(2,1)} async-done(((bf16[12,768,128]{2,1,0:T(8,128)(2,1)}), bf16[12,96,128]{2,1,0:T(8,128)(2,1)}) %reduce-scatter.5.cloned.1.call-update) | async-done | bytes 294928 | tf_op jit(solution)/shard_map/reduce_scatter | solution.py:68
  436.5 2.0 divide_add_fusion
  (13 shorter events, 0.0 us)
Async XLA Ops:
  7.4 3.4 copy-start
  7.4 139.9 %copy-start.1 = (bf16[64,12,256]{2,0,1:T(8,128)(2,1)S(1)}, bf16[64,12,256]{2,0,1:T(8,128)(2,1)}, u32[]{:S(2)}) copy-start(bf16[64,12,256]{2,0,1:T(8,128)(2,1)} %param.8) | copy-start | bytes 1179652
  7.4 138.8 %copy-start.2 = (s32[64,12]{0,1:T(8,128)S(1)}, s32[64,12]{0,1:T(8,128)}, u32[]{:S(2)}) copy-start(s32[64,12]{0,1:T(8,128)} %param.9) | copy-start | bytes 9220
  7.4 139.9 %copy-start.5 = (bf16[256,32]{0,1:T(8,128)(2,1)S(1)}, bf16[256,32]{0,1:T(8,128)(2,1)}, u32[]{:S(2)}) copy-start(bf16[256,32]{0,1:T(8,128)(2,1)} %param.10) | copy-start | bytes 49156
  7.4 299.4 %all-gather.4.cloned.1.call-start = ((), (), s32[]{:S(2)}) async-start(), calls=%async_computation.3 | async-start | bytes 4259840 | tf_op jit(solution)/shard_map/all_gather | solution.py:47
  13.6 357.8 %reduce-scatter.7.cloned.1.call-start = ((), (), s32[]{:S(2)}) async-start(), calls=%async_computation.4 | async-start | bytes 221184
  147.2 289.3 %reduce-scatter.5.cloned.1.call-start = ((), (), s32[]{:S(2)}) async-start(), calls=%async_computation.2 | async-start | bytes 2654208 | tf_op jit(solution)/shard_map/reduce_scatter | solution.py:68
  322.2 16.1 %copy-start.4 = (bf16[1024,128]{1,0:T(8,128)(2,1)S(1)}, bf16[1024,128]{1,0:T(8,128)(2,1)}, u32[]{:S(2)}) copy-start(bf16[1024,128]{1,0:T(8,128)(2,1)} %param.12) | copy-start | bytes 786436
  371.4 65.1 %copy-start.3 = (f32[128]{0:T(128)S(1)}, f32[128]{0:T(128)}, u32[]{:S(2)}) copy-start(f32[128]{0:T(128)} %param.13) | copy-start | bytes 1540
Sparse Core Ops, SparseCore 0:
  13.7 292.9 all-gather.3
Sparse Core Ops, SparseCore 1:
  147.3 64.8 reduce-scatter.6
  371.5 65.0 reduce-scatter.4
where the time goes:
time: 447 us; the launch traced here: 446 us
  waiting for transfers between devices  223 us (50%)
  blocking collectives  132 us (30%)
  local copies, waits for them, and re-layouts  44.7 us (10%)
  matrix products  25.2 us (6%)
  between operations  15 us (3%)
  other arithmetic  5.34 us (1%)
    all_gather x1, waiting for transfers between devices, local(): right_piece = lax.all_gather(right_rows, 'res', axis=0, tiled=True)  159 us
    all_gather x1, blocking collectives, local(): mask_piece = lax.all_gather(mask_row_slices, 'res', axis=0, tiled=True)  132 us
    reduce_scatter x1, waiting for transfers between devices, local(): lax.psum_scatter(projected, 'seq', scatter_dimension=1, tiled=True)  64.3 us
    while x1, local copies, waits for them, and re-layouts, local(): projected = lax.map(one_row, left_by_res)  16.1 us
    dot_general x12, matrix products, one_row(): jnp.dot(outer.reshape(rows, width * width), final_projection_matrix, pref...  15.6 us
    reshape x1, local copies, waits for them, and re-layouts, local(): right_cube = right_piece.reshape(rows, homolog_extent, width)  15.5 us
    convert_element_type x12, local copies, waits for them, and re-layouts, one_row(): outer = jnp.einsum('sc,jse->jce', left_row, right_cube, preferred_element...  10.4 us
  transfers between devices with their start and end apart: 3, of which 2 were waited for; matrix products, arithmetic and copies ran while one was open for 15% of the time, Pallas kernels for 0%

commit v1 on v0

v1 whole, which is shorter than its diff:
```python
import numpy as np

import jax
import jax.numpy as jnp
from jax import lax
from jax.experimental import pallas as pl
from jax.experimental.pallas import tpu as pltpu
from jax.sharding import Mesh
from jax.sharding import PartitionSpec as P

F32, BF16 = jnp.float32, jnp.bfloat16
SIZES = (8, 2, 4, 4, 2)
AXES = ("y", "zl", "x", "zh", "core")
S, I, C, WIDTH, PAIR = 64, 12, 256, 32, 128
ROWS = 208
NT = (((1,), (1,)), ((), ()))
VMEM = pl.BlockSpec(memory_space=pltpu.VMEM)
SMEM = pl.BlockSpec(memory_space=pltpu.SMEM)


def one_hot(shape, match):
    row = lax.broadcasted_iota(jnp.int32, shape, 0)
    col = lax.broadcasted_iota(jnp.int32, shape, 1)
    return match(row, col).astype(F32).astype(BF16)


def dot(a, b, dims=(((1,), (0,)), ((), ()))):
    return lax.dot_general(a, b, dims, preferred_element_type=F32)


def project_kernel(x_ref, m_ref, wl_ref, wr_ref, l_ref, r_ref, rows, spread):
    x = x_ref[...].astype(F32)
    centred = x - jnp.sum(x, axis=-1, keepdims=True) * (1.0 / C)
    variance = jnp.sum(centred * centred, axis=-1, keepdims=True) * (1.0 / C)
    normed = centred * lax.rsqrt(variance + 1e-05)
    for s in range(S):
        for h in range(2):
            rows[h, s * 16 : s * 16 + I, :] = normed[s, :, h * 128 : h * 128 + 128]

    mask = m_ref[...].astype(F32)
    mask_twice = jnp.concatenate([mask, mask], axis=0).astype(BF16)
    mask_rows = dot(one_hot((16, I), lambda r, t: r == t), mask_twice, NT)
    mask_pairs = dot(one_hot((32, I), lambda r, t: r // 2 == t), mask_twice, NT)
    wl = dot(wl_ref[...], one_hot((WIDTH, 128), lambda r, t: r == t % WIDTH)).astype(BF16)
    wr = dot(
        one_hot((WIDTH, WIDTH), lambda r, t: t == 2 * (r % 16) + r // 16), wr_ref[...], NT
    ).astype(BF16)
    lane = lax.broadcasted_iota(jnp.int32, (8, 128), 1)
    block = lax.broadcasted_iota(jnp.int32, (S, 128), 1) // WIDTH
    low = lane < 64
    for g in range(I // 4):
        tile = None
        for k in range(4):
            i = 4 * g + k
            xi = jnp.concatenate([rows[h, pl.ds(i, S, stride=16), :] for h in range(2)], axis=1)
            high = xi.astype(BF16)
            rest = (xi - high.astype(F32)).astype(BF16)
            left = (dot(high, wl) + dot(rest, wl)) * mask[:, i : i + 1]
            tile = left if k == 0 else jnp.where(block == k, left, tile)
            high2 = jnp.concatenate([high, high], axis=0)
            rest2 = jnp.concatenate([rest, rest], axis=0)
            right = (dot(wr, high2, NT) + dot(wr, rest2, NT)) * mask_rows[i : i + 1, :]
            for e in range(2):
                part = jnp.where(low, right[e * 16 : e * 16 + 8], right[e * 16 + 8 : e * 16 + 16])
                spread[pl.ds(2 * i + e, 8, stride=24), :] = part
        l_ref[g * S : (g + 1) * S, :] = tile.astype(BF16)
    l_ref[192:208, :] = mask_rows.astype(BF16)
    r_ref[0:192, :] = spread[...].astype(BF16)
    low16 = lax.broadcasted_iota(jnp.int32, (16, 128), 1) < 64
    r_ref[192:208, :] = jnp.where(low16, mask_pairs[0:16], mask_pairs[16:32]).astype(BF16)


def pair_kernel(core_ref, lm_ref, lo_ref, rm_ref, ro_ref, w_ref, out_ref, rt, rmask, lmask, z):
    core = core_ref[0]
    low = lax.broadcasted_iota(jnp.int32, (ROWS, 128), 1) < 64
    low16 = lax.broadcasted_iota(jnp.int32, (16, 128), 1) < 64
    for zl, ref in enumerate((rm_ref, ro_ref)):
        for t in range(4):
            a = ref[2 * t + core].astype(F32)
            b = ref[2 * t + 1 - core].astype(F32)
            first = jnp.where(low, a, pltpu.roll(b, 64, 1)).astype(BF16)
            second = jnp.where(low, pltpu.roll(a, 64, 1), b).astype(BF16)
            cols = slice(t * 128, t * 128 + 128)
            rt[zl, 0:192, cols] = first[0:192]
            rt[zl, 192:384, cols] = second[0:192]
            rmask[zl, 0:16, cols] = first[192:208]
            rmask[zl, 16:32, cols] = second[192:208]
    for x0 in range(4):
        for t in range(4):
            a = lm_ref[x0, t, 192:208, :].astype(F32)
            b = lo_ref[x0, t, 192:208, :].astype(F32)
            lmask[x0 * 16 : x0 * 16 + 16, t * 128 : t * 128 + 128] = jnp.where(low16, a, b).astype(BF16)
    scale = [1.0 / (dot(rmask[zl], lmask[...], NT) + 1.0) for zl in range(2)]

    lanes = lax.broadcasted_iota(jnp.int32, (24, 128), 1)
    half = lanes < 64
    even = (lanes // WIDTH) % 2 == 0
    for x0 in range(4):
        rhs = jnp.concatenate(
            [
                jnp.concatenate([ref[x0, t, g * S : g * S + S, :] for g in range(3)], axis=1)
                for t in range(4)
                for ref in (lm_ref, lo_ref)
            ],
            axis=0,
        )
        for zl in range(2):
            outer = dot(rt[zl], rhs)
            left_rows = []
            for g in range(3):
                quads = [[], [], [], []]
                for q in range(4):
                    a = [
                        outer[(4 * q + n) * 24 : (4 * q + n) * 24 + 24, g * 128 : g * 128 + 128]
                        for n in range(4)
                    ]
                    a0 = jnp.where(half, a[0], pltpu.roll(a[2], 64, 1))
                    a1 = jnp.where(half, a[1], pltpu.roll(a[3], 64, 1))
                    a2 = jnp.where(half, pltpu.roll(a[0], 64, 1), a[2])
                    a3 = jnp.where(half, pltpu.roll(a[1], 64, 1), a[3])
                    quads[0].append(jnp.where(even, a0, pltpu.roll(a1, 32, 1)))
                    quads[1].append(jnp.where(even, pltpu.roll(a0, 96, 1), a1))
                    quads[2].append(jnp.where(even, a2, pltpu.roll(a3, 32, 1)))
                    quads[3].append(jnp.where(even, pltpu.roll(a2, 96, 1), a3))
                left_rows += [jnp.concatenate(quad, axis=1) for quad in quads]
            operand = jnp.concatenate(left_rows, axis=0).astype(BF16)
            wide = dot(operand, w_ref[...])
            for i in range(I):
                column = scale[zl][0:24, x0 * 16 + i : x0 * 16 + i + 1]
                for e in range(2):
                    z[e, i * 24 : i * 24 + 24, :] = (
                        wide[i * 24 : i * 24 + 24, e * 128 : e * 128 + 128] * column
                    )
            result = z[0, pl.ds(0, 144, stride=2), :] + z[1, pl.ds(1, 144, stride=2), :]
            out_ref[x0, zl] = result.astype(BF16)


def finish_kernel(zl_ref, pair_ref, offset_ref, out_ref):
    mine = zl_ref[0]
    offset = offset_ref[...]
    for zl in range(2):
        for x1 in range(4):
            block = pair_ref[x1, zl ^ mine].astype(F32) + offset
            for i in range(I):
                at = (zl * 4 + x1) * I
                out_ref[i, at : at + I, :] = block[i * I : i * I + I, :]


def swap(match):
    index = np.arange(int(np.prod(SIZES))).reshape(SIZES)
    return [(int(index[at]), int(index[match(*at)])) for at in np.ndindex(*SIZES)]


TRANSPOSE = swap(lambda y, zl, x, zh, c: (2 * zh + c, zl, x, y // 2, y % 2))
OTHER_ZL = swap(lambda y, zl, x, zh, c: (y, 1 - zl, x, zh, c))
OTHER_CORE = swap(lambda y, zl, x, zh, c: (y, zl, x, zh, 1 - c))


def spread_along(value, axis, count):
    return lax.all_to_all(
        jnp.broadcast_to(value[None], (count,) + value.shape), axis, 0, 0, tiled=True
    )


def after(value, earlier):
    return lax.optimization_barrier((value, earlier))[0]


def local(x, m, wl, wr, w, offset):
    left, right = pl.pallas_call(
        project_kernel,
        out_shape=[jax.ShapeDtypeStruct((ROWS, 128), BF16)] * 2,
        in_specs=[VMEM] * 4,
        out_specs=[VMEM] * 2,
        scratch_shapes=[pltpu.VMEM((2, S * 16, 128), F32), pltpu.VMEM((192, 128), F32)],
        compiler_params=pltpu.CompilerParams(vmem_limit_bytes=48 << 20),
    )(x, m, wl, wr)
    w2 = w.reshape(WIDTH, 16, 2, PAIR).transpose(1, 0, 2, 3).reshape(512, 2 * PAIR)

    right = lax.ppermute(right, AXES, TRANSPOSE)
    left = spread_along(left, "zh", 4)
    right = spread_along(after(right, left), "y", 8)
    right_other = lax.ppermute(right, AXES, OTHER_ZL)
    left = spread_along(after(left, right), "x", 4)
    left_other = lax.ppermute(left, AXES, OTHER_CORE)

    core = lax.axis_index("core").astype(jnp.int32).reshape(1)
    zl = lax.axis_index("zl").astype(jnp.int32).reshape(1)
    pairs = pl.pallas_call(
        pair_kernel,
        out_shape=jax.ShapeDtypeStruct((4, 2, 144, 128), BF16),
        in_specs=[SMEM] + [VMEM] * 5,
        out_specs=VMEM,
        scratch_shapes=[
            pltpu.VMEM((2, 384, 512), BF16),
            pltpu.VMEM((2, 32, 512), BF16),
            pltpu.VMEM((64, 512), BF16),
            pltpu.VMEM((2, 288, 128), F32),
        ],
        compiler_params=pltpu.CompilerParams(vmem_limit_bytes=48 << 20),
    )(core, left, left_other, right, right_other, w2)
    pairs = lax.all_to_all(pairs, "x", 0, 0, tiled=True)
    return pl.pallas_call(
        finish_kernel,
        out_shape=jax.ShapeDtypeStruct((I, 96, PAIR), F32),
        in_specs=[SMEM, VMEM, VMEM],
        out_specs=VMEM,
        compiler_params=pltpu.CompilerParams(vmem_limit_bytes=48 << 20),
    )(zl, pairs, offset.reshape(1, PAIR))


def solution(mesh):
    fine = Mesh(mesh.devices.reshape(SIZES), AXES)
    res, seq = ("y", "zl", "x"), ("zh", "core")
    return jax.shard_map(
        local,
        mesh=fine,
        in_specs=(P(seq, res, None), P(seq, res), P(), P(), P(), P()),
        out_specs=P(res, seq, None),
        check_vma=False,
    )
```

time: 447 us -> 101 us (0.23)
  the two profiles are of different devices: /device:TPU:20 before, /device:TPU:1 now
where the time goes in v1:
time: 101 us
  blocking collectives  41.2 us (41%)
  starting transfers between devices  25.9 us (26%)
  waiting for transfers between devices  20.9 us (21%)
  Pallas kernels  8.02 us (8%)
  local copies, waits for them, and re-layouts  4.67 us (5%)
    all_to_all x2, blocking collectives, spread_along(): lax.all_to_all(jnp.broadcast_to(value[None], (count,) + value.shape), axi...  41.2 us
    ppermute x1, waiting for transfers between devices, local(): right_other = lax.ppermute(right, AXES, OTHER_ZL)  11.1 us
    all_to_all x1, starting transfers between devices, spread_along(): lax.all_to_all(jnp.broadcast_to(value[None], (count,) + value.shape), axi...  10.8 us
    pallas_call x1, Pallas kernels, local(): pl.pallas_call(pair_kernel, out_shape=jax.ShapeDtypeStruct((4, 2, 144, 12...  5.97 us
    all_to_all x1, waiting for transfers between devices, local(): pairs = lax.all_to_all(pairs, 'x', 0, 0, tiled=True)  5.96 us
    ppermute x1, starting transfers between devices, local(): left_other = lax.ppermute(left, AXES, OTHER_CORE)  5.68 us
    ppermute x1, starting transfers between devices, local(): right = lax.ppermute(right, AXES, TRANSPOSE)  4.03 us
    unnamed x13, local copies, waits for them, and re-layouts  3.55 us
  transfers between devices with their start and end apart: 5, of which 4 were waited for; matrix products, arithmetic and copies ran while one was open for 0% of the time, Pallas kernels for 0%

profile of v1, /device:TPU:1, one launch (start us, length us, event | category | flops | bytes accessed | tf_op | source)
XLA Modules:
  0.0 100.8 jit_solution(7341386582804629439)
XLA Ops:
  0.0 0.0 copy-start.2
  0.0 0.8 copy.8.m_ref
  0.8 0.0 copy-done.2
  0.8 0.0 copy-start.3
  0.8 0.1 copy.9.wl_ref
  0.9 0.6 copy-done.3
  1.5 0.1 copy.10.wr_ref
  1.6 1.2 %copy.7.x_ref = bf16[64,12,256]{2,1,0:T(8,128)(2,1)S(1)} copy(bf16[64,12,256]{2,0,1:T(8,128)(2,1)} %param.6) | data formatting | bytes 786432 | tf_op args[0]
  2.9 1.2 %shard_map.64 = (bf16[208,128]{1,0:T(8,128)(2,1)S(1)}, bf16[208,128]{1,0:T(8,128)(2,1)S(1)}) custom-call(bf16[64,12,256]{2,1,0:T(8,128)(2,1)S(1)} %copy.7.x_ref, s32[64,12]{1,0:T(8,128)S(1)} %copy.8.m_ref, bf16[256,32]{1,0:T(8,128)(2,1)S(1)} %copy.9.wl_ref, bf16[256,32]{1,0:T(8,128)(2,1)S(1)} %copy.10.wr_ref), custom_call_target="tpu_custom_call" | custom-call | tf_op jit(solution)/shard_map/pallas_call | solution.py:170
  4.1 0.7 broadcast_in_dim.6
  4.8 10.8 %all-to-all-start = ((bf16[4,208,128]{2,1,0:T(8,128)(2,1)}), bf16[4,208,128]{2,1,0:T(8,128)(2,1)S(1)}, u32[]{:S(2)}, u32[]{:S(2)}) async-start(bf16[4,208,128]{2,1,0:T(8,128)(2,1)} %broadcast_in_dim.6), calls=%async_computation | async-start | bytes 425984 | tf_op jit(solution)/shard_map/all_to_all | solution.py:160
  15.6 4.0 %collective-permute-start = (bf16[208,128]{1,0:T(8,128)(2,1)S(1)}, bf16[208,128]{1,0:T(8,128)(2,1)S(1)}, u32[]{:S(2)}, u32[]{:S(2)}) collective-permute-start(bf16[208,128]{1,0:T(8,128)(2,1)S(1)} %get-tuple-element.10), channel_id=1, source_target_pairs={{0,0},{1,64},{2,128},{3,192},{4,256},{5,320},{6,384},{7,448},{8,8}... | collective-permute-start | bytes 159752 | tf_op jit(solution)/shard_map/ppermute | solution.py:180
  19.7 2.1 %collective-permute-done = bf16[208,128]{1,0:T(8,128)(2,1)S(1)} collective-permute-done((bf16[208,128]{1,0:T(8,128)(2,1)S(1)}, bf16[208,128]{1,0:T(8,128)(2,1)S(1)}, u32[]{:S(2)}, u32[]{:S(2)}) %collective-permute-start) | collective-permute-done | bytes 53280 | tf_op jit(solution)/shard_map/ppermute | solution.py:180
  21.8 1.7 %all-to-all-done = bf16[4,208,128]{2,1,0:T(8,128)(2,1)S(1)} async-done(((bf16[4,208,128]{2,1,0:T(8,128)(2,1)}), bf16[4,208,128]{2,1,0:T(8,128)(2,1)S(1)}, u32[]{:S(2)}, u32[]{:S(2)}) %all-to-all-start) | async-done | bytes 213024 | tf_op jit(solution)/shard_map/all_to_all | solution.py:160
  23.5 0.1 broadcast_in_dim.7
  23.6 27.1 %all_to_all.20.rm_ref = bf16[8,208,128]{2,1,0:T(8,128)(2,1)S(1)} all-to-all(bf16[8,208,128]{2,1,0:T(8,128)(2,1)S(1)} %broadcast_in_dim.7), channel_id=1, replica_groups=mesh['y'=8,'zl'=2,'x'=4,'zh'=4,'core'=2] {'y'}, dimensions={0} | all-to-all | bytes 851968 | tf_op jit(solution)/shard_map/all_to_all | solution.py:160
  50.7 0.1 broadcast_in_dim.8
  50.8 0.0 copy-start.1
  50.8 14.1 %all_to_all.21.lm_ref = bf16[4,4,208,128]{3,2,1,0:T(8,128)(2,1)S(1)} all-to-all(bf16[4,4,208,128]{3,2,1,0:T(8,128)(2,1)S(1)} %broadcast_in_dim.8), channel_id=1, replica_groups=mesh['y'=8,'zl'=2,'x'=4,'zh'=4,'core'=2] {'x'}, dimensions={0} | all-to-all | bytes 1703936 | tf_op jit(solution)/shard_map/all_to_all | solution.py:160
  64.9 5.7 %collective-permute-start.1 = (bf16[4,4,208,128]{3,2,1,0:T(8,128)(2,1)S(1)}, bf16[4,4,208,128]{3,2,1,0:T(8,128)(2,1)S(1)}, u32[]{:S(2)}, u32[]{:S(2)}) collective-permute-start(bf16[4,4,208,128]{3,2,1,0:T(8,128)(2,1)S(1)} %all_to_all.21.lm_ref), channel_id=1, source_target_pairs={{0,1},{1,0},{2,3},{3,2},{4,5},{5,4},{6,7},{7,6},{8,9},{9,8},{10,11... | collective-permute-start | bytes 2555912 | tf_op jit(solution)/shard_map/ppermute | solution.py:185
  70.6 1.9 %collective-permute-start.2 = (bf16[8,208,128]{2,1,0:T(8,128)(2,1)S(1)}, bf16[8,208,128]{2,1,0:T(8,128)(2,1)S(1)}, u32[]{:S(2)}, u32[]{:S(2)}) collective-permute-start(bf16[8,208,128]{2,1,0:T(8,128)(2,1)S(1)} %all_to_all.20.rm_ref), channel_id=1, source_target_pairs={{0,32},{1,33},{2,34},{3,35},{4,36},{5,37},{6,38},{7,39},{8,40},{9,... | collective-permute-start | bytes 1277960 | tf_op jit(solution)/shard_map/ppermute | solution.py:183
  72.5 0.0 copy-done.1
  72.5 0.2 copy.11
  72.8 11.1 %collective-permute-done.2.ro_ref = bf16[8,208,128]{2,1,0:T(8,128)(2,1)S(1)} collective-permute-done((bf16[8,208,128]{2,1,0:T(8,128)(2,1)S(1)}, bf16[8,208,128]{2,1,0:T(8,128)(2,1)S(1)}, u32[]{:S(2)}, u32[]{:S(2)}) %collective-permute-start.2) | collective-permute-done | bytes 426016 | tf_op jit(solution)/shard_map/ppermute | solution.py:183
  83.9 0.0 collective-permute-done.1.lo_ref
  83.9 6.0 %shard_map.65 = bf16[4,2,144,128]{3,2,1,0:T(8,128)(2,1)} custom-call(s32[1]{0:T(128)} %bitcast.1.core_ref, bf16[4,4,208,128]{3,2,1,0:T(8,128)(2,1)S(1)} %all_to_all.21.lm_ref, bf16[4,4,208,128]{3,2,1,0:T(8,128)(2,1)S(1)} %collective-permute-done.1.lo_ref, bf16[8,208,128]{2,1,0:T(8,128)(2,1)S(1)} %all_to_all.20.rm_ref, ...), custom_call_target="tpu_custom_call" | custom-call | tf_op jit(solution)/shard_map/pallas_call | solution.py:189
  89.9 3.5 %all-to-all-start.3 = ((bf16[4,2,144,128]{3,2,1,0:T(8,128)(2,1)}), bf16[4,2,144,128]{3,2,1,0:T(8,128)(2,1)S(1)}, u32[]{:S(2)}, u32[]{:S(2)}) async-start(bf16[4,2,144,128]{3,2,1,0:T(8,128)(2,1)} %shard_map.65), calls=%async_computation.3 | async-start | bytes 589824 | tf_op jit(solution)/shard_map/all_to_all | solution.py:202
  93.4 6.0 %all-to-all-done.3.pair_ref = bf16[4,2,144,128]{3,2,1,0:T(8,128)(2,1)S(1)} async-done(((bf16[4,2,144,128]{3,2,1,0:T(8,128)(2,1)}), bf16[4,2,144,128]{3,2,1,0:T(8,128)(2,1)S(1)}, u32[]{:S(2)}, u32[]{:S(2)}) %all-to-all-start.3) | async-done | bytes 294944 | tf_op jit(solution)/shard_map/all_to_all | solution.py:202
  99.3 0.0 copy-start
  99.3 0.7 copy-done
  100.0 0.9 shard_map.66
  (1 shorter events, 0.0 us)
Async XLA Ops:
  0.0 0.8 copy-start.2
  0.8 0.7 copy-start.3
  4.8 18.7 %all-to-all-start = ((bf16[4,208,128]{2,1,0:T(8,128)(2,1)}), bf16[4,208,128]{2,1,0:T(8,128)(2,1)S(1)}, u32[]{:S(2)}, u32[]{:S(2)}) async-start(bf16[4,208,128]{2,1,0:T(8,128)(2,1)} %broadcast_in_dim.6), calls=%async_computation | async-start | bytes 425984 | tf_op jit(solution)/shard_map/all_to_all | solution.py:160
  15.6 6.1 %collective-permute-start = (bf16[208,128]{1,0:T(8,128)(2,1)S(1)}, bf16[208,128]{1,0:T(8,128)(2,1)S(1)}, u32[]{:S(2)}, u32[]{:S(2)}) collective-permute-start(bf16[208,128]{1,0:T(8,128)(2,1)S(1)} %get-tuple-element.10), channel_id=1, source_target_pairs={{0,0},{1,64},{2,128},{3,192},{4,256},{5,320},{6,384},{7,448},{8,8}... | collective-permute-start | bytes 159752 | tf_op jit(solution)/shard_map/ppermute | solution.py:180
  50.8 21.7 %copy-start.1 = (bf16[1024,128]{1,0:T(8,128)(2,1)S(1)}, bf16[1024,128]{1,0:T(8,128)(2,1)}, u32[]{:S(2)}) copy-start(bf16[1024,128]{1,0:T(8,128)(2,1)} %param.10) | copy-start | bytes 786436
  64.9 19.0 %collective-permute-start.1 = (bf16[4,4,208,128]{3,2,1,0:T(8,128)(2,1)S(1)}, bf16[4,4,208,128]{3,2,1,0:T(8,128)(2,1)S(1)}, u32[]{:S(2)}, u32[]{:S(2)}) collective-permute-start(bf16[4,4,208,128]{3,2,1,0:T(8,128)(2,1)S(1)} %all_to_all.21.lm_ref), channel_id=1, source_target_pairs={{0,1},{1,0},{2,3},{3,2},{4,5},{5,4},{6,7},{7,6},{8,9},{9,8},{10,11... | collective-permute-start | bytes 2555912 | tf_op jit(solution)/shard_map/ppermute | solution.py:185
  70.6 13.3 %collective-permute-start.2 = (bf16[8,208,128]{2,1,0:T(8,128)(2,1)S(1)}, bf16[8,208,128]{2,1,0:T(8,128)(2,1)S(1)}, u32[]{:S(2)}, u32[]{:S(2)}) collective-permute-start(bf16[8,208,128]{2,1,0:T(8,128)(2,1)S(1)} %all_to_all.20.rm_ref), channel_id=1, source_target_pairs={{0,32},{1,33},{2,34},{3,35},{4,36},{5,37},{6,38},{7,39},{8,40},{9,... | collective-permute-start | bytes 1277960 | tf_op jit(solution)/shard_map/ppermute | solution.py:183
  89.9 9.4 %all-to-all-start.3 = ((bf16[4,2,144,128]{3,2,1,0:T(8,128)(2,1)}), bf16[4,2,144,128]{3,2,1,0:T(8,128)(2,1)S(1)}, u32[]{:S(2)}, u32[]{:S(2)}) async-start(bf16[4,2,144,128]{3,2,1,0:T(8,128)(2,1)} %shard_map.65), calls=%async_computation.3 | async-start | bytes 589824 | tf_op jit(solution)/shard_map/all_to_all | solution.py:202
  99.3 0.7 copy-start

commit v2 on v1

v2 whole, which is shorter than its diff:
```python
import numpy as np

import jax
import jax.numpy as jnp
from jax import lax
from jax.experimental import pallas as pl
from jax.experimental.pallas import tpu as pltpu
from jax.sharding import Mesh
from jax.sharding import PartitionSpec as P

F32, BF16 = jnp.float32, jnp.bfloat16
SIZES = (8, 2, 4, 4, 2)
AXES = ("y", "zl", "x", "zh", "core")
S, I, C, WIDTH, PAIR = 64, 12, 256, 32, 128
ROWS = 208
NT = (((1,), (1,)), ((), ()))
VMEM = pl.BlockSpec(memory_space=pltpu.VMEM)
HBM = pl.BlockSpec(memory_space=pltpu.HBM)
SMEM = pl.BlockSpec(memory_space=pltpu.SMEM)


def one_hot(shape, match):
    row = lax.broadcasted_iota(jnp.int32, shape, 0)
    col = lax.broadcasted_iota(jnp.int32, shape, 1)
    return match(row, col).astype(F32).astype(BF16)


def dot(a, b, dims=(((1,), (0,)), ((), ()))):
    return lax.dot_general(a, b, dims, preferred_element_type=F32)


def project_kernel(
    x_in, m_in, wl_in, wr_in, offset_in, l_ref, r_ref, offset_ref, x_ref, m_ref, wl_ref, wr_ref, spread, sems
):
    copies = [
        pltpu.make_async_copy(source, target, sems.at[n])
        for n, (source, target) in enumerate(
            ((m_in, m_ref), (wl_in, wl_ref), (wr_in, wr_ref), (x_in, x_ref), (offset_in, offset_ref))
        )
    ]
    for copy in copies:
        copy.start()
    for copy in copies[:3]:
        copy.wait()
    mask = m_ref[...].astype(F32).astype(BF16)
    mask_twice = jnp.concatenate([mask, mask], axis=1)
    mask_rows = dot(one_hot((16, I), lambda r, t: r == t), mask_twice)
    mask_pairs = dot(one_hot((32, I), lambda r, t: r // 2 == t), mask_twice)
    mask_cols = dot(one_hot((S, S), lambda r, t: r == t), mask, NT)
    wl = dot(one_hot((128, WIDTH), lambda r, t: r % WIDTH == t), wl_ref[...]).astype(BF16)
    wr = dot(
        one_hot((WIDTH, WIDTH), lambda r, t: t == 2 * (r % 16) + r // 16), wr_ref[...]
    ).astype(BF16)
    copies[3].wait()
    low = lax.broadcasted_iota(jnp.int32, (8, 128), 1) < 64
    block = lax.broadcasted_iota(jnp.int32, (S, 128), 1) // WIDTH
    for g in range(I // 4):
        tile = None
        for k in range(4):
            i = 4 * g + k
            x = x_ref[i].astype(F32)
            centred = x - jnp.sum(x, axis=-1, keepdims=True) * (1.0 / C)
            variance = jnp.sum(centred * centred, axis=-1, keepdims=True) * (1.0 / C)
            xi = centred * lax.rsqrt(variance + 1e-05)
            high = xi.astype(BF16)
            rest = (xi - high.astype(F32)).astype(BF16)
            left = (dot(high, wl, NT) + dot(rest, wl, NT)) * mask_cols[:, i : i + 1]
            tile = left if k == 0 else jnp.where(block == k, left, tile)
            high2 = jnp.concatenate([high, high], axis=0)
            rest2 = jnp.concatenate([rest, rest], axis=0)
            right = (dot(wr, high2, NT) + dot(wr, rest2, NT)) * mask_rows[i : i + 1, :]
            for e in range(2):
                part = jnp.where(low, right[e * 16 : e * 16 + 8], right[e * 16 + 8 : e * 16 + 16])
                spread[pl.ds(2 * i + e, 8, stride=24), :] = part
        tile = tile.astype(BF16)
        for copy in range(4):
            l_ref[copy, g * S : (g + 1) * S, :] = tile
    for copy in range(4):
        l_ref[copy, 192:208, :] = mask_rows.astype(BF16)
    r_ref[0:192, :] = spread[...].astype(BF16)
    low16 = lax.broadcasted_iota(jnp.int32, (16, 128), 1) < 64
    r_ref[192:208, :] = jnp.where(low16, mask_pairs[0:16], mask_pairs[16:32]).astype(BF16)
    copies[4].wait()


SHIFT = ((4, 3), (1, 2), (0, 7), (6, 5))


def pair_kernel(at_ref, r_ref, w_ref, *refs):
    lm_refs, lo_refs, (out_ref, rt, rmask, lmask, z) = refs[:4], refs[4:8], refs[8:]
    zh, core, x = at_ref[0], at_ref[1], at_ref[2]
    low = lax.broadcasted_iota(jnp.int32, (ROWS, 128), 1) < 64
    low16 = lax.broadcasted_iota(jnp.int32, (16, 128), 1) < 64

    def piece(zl, t, c):
        step = (t - zh) & 3
        shift = jnp.int32(0)
        for n in range(4):
            for k in range(2):
                shift = jnp.where((step == n) & (c == k), SHIFT[n][k], shift)
        return r_ref[((2 * zh + core + shift) & 7) * 2 + zl].astype(F32)

    for zl in range(2):
        for t in range(4):
            a, b = piece(zl, t, core), piece(zl, t, 1 - core)
            first = jnp.where(low, a, pltpu.roll(b, 64, 1)).astype(BF16)
            second = jnp.where(low, pltpu.roll(a, 64, 1), b).astype(BF16)
            cols = slice(t * 128, t * 128 + 128)
            rt[zl, 0:192, cols] = first[0:192]
            rt[zl, 192:384, cols] = second[0:192]
            rmask[zl, 0:16, cols] = first[192:208]
            rmask[zl, 16:32, cols] = second[192:208]
    for k in range(4):
        for t in range(4):
            a = lm_refs[k][t, 192:208, :].astype(F32)
            b = lo_refs[k][t, 192:208, :].astype(F32)
            lmask[k * 16 : k * 16 + 16, t * 128 : t * 128 + 128] = jnp.where(low16, a, b).astype(BF16)
    scale = [1.0 / (dot(rmask[zl], lmask[...], NT) + 1.0) for zl in range(2)]

    lanes = lax.broadcasted_iota(jnp.int32, (24, 128), 1)
    half = lanes < 64
    even = (lanes // WIDTH) % 2 == 0
    for k in range(4):
        rhs = jnp.concatenate(
            [
                jnp.concatenate([ref[t, g * S : g * S + S, :] for g in range(3)], axis=1)
                for t in range(4)
                for ref in (lm_refs[k], lo_refs[k])
            ],
            axis=0,
        )
        for zl in range(2):
            outer = dot(rt[zl], rhs)
            left_rows = []
            for g in range(3):
                quads = [[], [], [], []]
                for q in range(4):
                    a = [
                        outer[(4 * q + n) * 24 : (4 * q + n) * 24 + 24, g * 128 : g * 128 + 128]
                        for n in range(4)
                    ]
                    a0 = jnp.where(half, a[0], pltpu.roll(a[2], 64, 1))
                    a1 = jnp.where(half, a[1], pltpu.roll(a[3], 64, 1))
                    a2 = jnp.where(half, pltpu.roll(a[0], 64, 1), a[2])
                    a3 = jnp.where(half, pltpu.roll(a[1], 64, 1), a[3])
                    quads[0].append(jnp.where(even, a0, pltpu.roll(a1, 32, 1)))
                    quads[1].append(jnp.where(even, pltpu.roll(a0, 96, 1), a1))
                    quads[2].append(jnp.where(even, a2, pltpu.roll(a3, 32, 1)))
                    quads[3].append(jnp.where(even, pltpu.roll(a2, 96, 1), a3))
                left_rows += [jnp.concatenate(quad, axis=1) for quad in quads]
            operand = jnp.concatenate(left_rows, axis=0).astype(BF16)
            wide = dot(operand, w_ref[...])
            for i in range(I):
                column = scale[zl][0:24, k * 16 + i : k * 16 + i + 1]
                for e in range(2):
                    z[e, i * 24 : i * 24 + 24, :] = (
                        wide[i * 24 : i * 24 + 24, e * 128 : e * 128 + 128] * column
                    )
            result = z[0, pl.ds(0, 144, stride=2), :] + z[1, pl.ds(1, 144, stride=2), :]
            out_ref[(x - k) & 3, zl] = result.astype(BF16)


def finish_kernel(pair_ref, offset_ref, out_ref):
    offset = offset_ref[...]
    for zl in range(2):
        for x1 in range(4):
            block = pair_ref[x1, zl].astype(F32) + offset
            at = (zl * 4 + x1) * I
            for i in range(I):
                out_ref[i, at : at + I, :] = block[i * I : i * I + I, :]


def swap(match):
    index = np.arange(int(np.prod(SIZES))).reshape(SIZES)
    return [(int(index[at]), int(index[match(*at)])) for at in np.ndindex(*SIZES)]


def shifted(y, zl, x, zh, c):
    return (y + SHIFT[(zh - y // 2) % 4][c]) % 8, zl, x, y // 2, y % 2


TRANSPOSE = swap(shifted)
ALONG_X = [swap(lambda y, zl, x, zh, c, k=k: (y, zl, (x + k) % 4, zh, c)) for k in range(4)]
OTHER_CORE = swap(lambda y, zl, x, zh, c: (y, zl, x, zh, 1 - c))


def spread_along(value, axis, count):
    return lax.all_to_all(
        jnp.broadcast_to(value[None], (count,) + value.shape), axis, 0, 0, tiled=True
    )


def call(kernel, out_shape, in_specs, scratch_shapes=(), vmem=48, flops=0, bytes_accessed=0):
    return pl.pallas_call(
        kernel,
        out_shape=out_shape,
        in_specs=in_specs,
        out_specs=jax.tree.map(lambda _: VMEM, out_shape),
        scratch_shapes=scratch_shapes,
        compiler_params=pltpu.CompilerParams(vmem_limit_bytes=vmem << 20),
        cost_estimate=pl.CostEstimate(
            flops=flops, bytes_accessed=bytes_accessed, transcendentals=0
        ),
    )


def local(x, m, wl, wr, w, offset):
    left, right, offset = call(
        project_kernel,
        [
            jax.ShapeDtypeStruct((4, ROWS, 128), BF16),
            jax.ShapeDtypeStruct((ROWS, 128), BF16),
            jax.ShapeDtypeStruct((1, PAIR), F32),
        ],
        [HBM] * 5,
        [
            pltpu.VMEM((I, S, C), BF16),
            pltpu.VMEM((I, S), jnp.int32),
            pltpu.VMEM((WIDTH, C), BF16),
            pltpu.VMEM((WIDTH, C), BF16),
            pltpu.VMEM((192, 128), F32),
            pltpu.SemaphoreType.DMA((5,)),
        ],
        vmem=60,
    )(x.transpose(1, 0, 2), m.T, wl.T, wr.T, offset.reshape(1, PAIR))
    w2 = w.reshape(WIDTH, 16, 2, PAIR).transpose(1, 0, 2, 3).reshape(512, 2 * PAIR)
    at = jnp.stack([lax.axis_index(name) for name in ("zh", "core", "x")]).astype(jnp.int32)

    right = lax.ppermute(right, AXES, TRANSPOSE)
    left = lax.all_to_all(left, "zh", 0, 0, tiled=True)
    right = spread_along(right, ("y", "zl"), 16)
    lefts = [left] + [lax.ppermute(left, AXES, ALONG_X[k]) for k in (1, 2, 3)]
    lefts += [lax.ppermute(left, AXES, OTHER_CORE) for left in lefts]

    pairs = call(
        pair_kernel,
        jax.ShapeDtypeStruct((4, 2, 144, 128), BF16),
        [SMEM] + [VMEM] * 10,
        [
            pltpu.VMEM((2, 384, 512), BF16),
            pltpu.VMEM((2, 32, 512), BF16),
            pltpu.VMEM((64, 512), BF16),
            pltpu.VMEM((2, 288, 128), F32),
        ],
        flops=3 << 30,
        bytes_accessed=4 << 20,
    )(at, right, w2, *lefts)
    pairs = lax.all_to_all(pairs, "x", 0, 0, tiled=True)
    return call(
        finish_kernel, jax.ShapeDtypeStruct((I, 96, PAIR), F32), [VMEM, VMEM]
    )(pairs, offset)


def solution(mesh):
    fine = Mesh(mesh.devices.reshape(SIZES), AXES)
    res, seq = ("y", "zl", "x"), ("zh", "core")
    return jax.shard_map(
        local,
        mesh=fine,
        in_specs=(P(seq, res, None), P(seq, res), P(), P(), P(), P()),
        out_specs=P(res, seq, None),
        check_vma=False,
    )
```

time: 101 us -> 74.4 us (0.74)
  the two profiles are of different devices: /device:TPU:1 before, /device:TPU:2 now
where the time goes in v2:
time: 74.4 us; the launch traced here: 73.8 us
  starting transfers between devices  45 us (60%)
  blocking collectives  10 us (13%)
  Pallas kernels  9.89 us (13%)
  waiting for transfers between devices  6.78 us (9%)
  local copies, waits for them, and re-layouts  1.88 us (3%)
    ppermute x3, starting transfers between devices, local(): lefts = [left] + [lax.ppermute(left, AXES, ALONG_X[k]) for k in (1, 2, 3)]  10.5 us
    all_to_all x1, starting transfers between devices, local(): left = lax.all_to_all(left, 'zh', 0, 0, tiled=True)  10.4 us
    all_to_all x1, blocking collectives, local(): pairs = lax.all_to_all(pairs, 'x', 0, 0, tiled=True)  10 us
    ppermute x4, starting transfers between devices, local(): lefts += [lax.ppermute(left, AXES, OTHER_CORE) for left in lefts]  8.65 us
    all_to_all x1, starting transfers between devices, spread_along(): lax.all_to_all(jnp.broadcast_to(value[None], (count,) + value.shape), axi...  7.73 us
    ppermute x1, starting transfers between devices, local(): right = lax.ppermute(right, AXES, TRANSPOSE)  7.72 us
    pallas_call x1, Pallas kernels, local(): call(pair_kernel, jax.ShapeDtypeStruct((4, 2, 144, 128), BF16), [SMEM] +...  5.77 us
    ppermute x1, waiting for transfers between devices, local(): right = lax.ppermute(right, AXES, TRANSPOSE)  4.24 us
  transfers between devices with their start and end apart: 10, of which 3 were waited for; matrix products, arithmetic and copies ran while one was open for 0% of the time, Pallas kernels for 0%

profile of v2, /device:TPU:2, one launch (start us, length us, event | category | flops | bytes accessed | tf_op | source)
XLA Modules:
  0.0 73.8 jit_solution(5060332501078760813)
XLA Ops:
  0.0 3.3 %shard_map.64 = (bf16[4,208,128]{2,1,0:T(8,128)(2,1)}, bf16[208,128]{1,0:T(8,128)(2,1)}, f32[1,128]{1,0:T(1,128)}) custom-call(bf16[12,64,256]{2,1,0:T(8,128)(2,1)} %bitcast.17, s32[12,64]{1,0:T(8,128)} %bitcast.21, bf16[32,256]{1,0:T(8,128)(2,1)} %bitcast.19, bf16[32,256]{1,0:T(8,128)(2,1)} %bitcast.20, f32[1,128]{1,0:T(1,128)} %bitcast.22), custom_call_target="tpu_custom_call" | custom-call | tf_op jit(solution)/shard_map/pallas_call | solution.py:208
  3.3 0.0 copy-start.2
  3.3 10.4 %all-to-all-start.1 = ((bf16[4,208,128]{2,1,0:T(8,128)(2,1)}), bf16[4,208,128]{2,1,0:T(8,128)(2,1)S(1)}, u32[]{:S(2)}, u32[]{:S(2)}) async-start(bf16[4,208,128]{2,1,0:T(8,128)(2,1)} %get-tuple-element.9), calls=%async_computation.1 | async-start | bytes 425984 | tf_op jit(solution)/shard_map/all_to_all | solution.py:230
  13.7 0.0 copy-done.2
  13.7 7.7 %collective-permute-start = (bf16[208,128]{1,0:T(8,128)(2,1)S(1)}, bf16[208,128]{1,0:T(8,128)(2,1)S(1)}, u32[]{:S(2)}, u32[]{:S(2)}) collective-permute-start(bf16[208,128]{1,0:T(8,128)(2,1)S(1)} %copy-done.2), channel_id=1, source_target_pairs={{0,256},{1,192},{2,64},{3,128},{4,0},{5,448},{6,384},{7,320},{8,26... | collective-permute-start | bytes 159752 | tf_op jit(solution)/shard_map/ppermute | solution.py:229
  21.4 4.2 %collective-permute-done = bf16[208,128]{1,0:T(8,128)(2,1)S(1)} collective-permute-done((bf16[208,128]{1,0:T(8,128)(2,1)S(1)}, bf16[208,128]{1,0:T(8,128)(2,1)S(1)}, u32[]{:S(2)}, u32[]{:S(2)}) %collective-permute-start) | collective-permute-done | bytes 53280 | tf_op jit(solution)/shard_map/ppermute | solution.py:229
  25.7 0.0 all-to-all-done.1.refs_0_
  25.7 1.0 %broadcast_in_dim.2 = bf16[16,208,128]{2,1,0:T(8,128)(2,1)} broadcast(bf16[208,128]{1,0:T(8,128)(2,1)S(1)} %collective-permute-done), dimensions={1,2} | broadcast | bytes 905216 | tf_op jit(solution)/shard_map/broadcast_in_dim | solution.py:189
  26.7 0.0 copy-start.1
  26.7 7.7 %all-to-all-start = ((bf16[16,208,128]{2,1,0:T(8,128)(2,1)}), bf16[16,208,128]{2,1,0:T(8,128)(2,1)S(1)}, u32[]{:S(2)}, u32[]{:S(2)}) async-start(bf16[16,208,128]{2,1,0:T(8,128)(2,1)} %broadcast_in_dim.2), calls=%async_computation | async-start | bytes 1703936 | tf_op jit(solution)/shard_map/all_to_all | solution.py:188
  34.5 3.4 %collective-permute-start.1 = (bf16[4,208,128]{2,1,0:T(8,128)(2,1)S(1)}, bf16[4,208,128]{2,1,0:T(8,128)(2,1)S(1)}, u32[]{:S(2)}, u32[]{:S(2)}) collective-permute-start(bf16[4,208,128]{2,1,0:T(8,128)(2,1)S(1)} %all-to-all-done.1.refs_0_), channel_id=1, source_target_pairs={{0,8},{1,9},{2,10},{3,11},{4,12},{5,13},{6,14},{7,15},{8,16},{9,17... | collective-permute-start | bytes 638984 | tf_op jit(solution)/shard_map/ppermute | solution.py:232
  37.9 3.0 %collective-permute-start.2 = (bf16[4,208,128]{2,1,0:T(8,128)(2,1)S(1)}, bf16[4,208,128]{2,1,0:T(8,128)(2,1)S(1)}, u32[]{:S(2)}, u32[]{:S(2)}) collective-permute-start(bf16[4,208,128]{2,1,0:T(8,128)(2,1)S(1)} %all-to-all-done.1.refs_0_), channel_id=1, source_target_pairs={{0,16},{1,17},{2,18},{3,19},{4,20},{5,21},{6,22},{7,23},{8,24},{9,... | collective-permute-start | bytes 638984 | tf_op jit(solution)/shard_map/ppermute | solution.py:232
  40.9 4.1 %collective-permute-start.3 = (bf16[4,208,128]{2,1,0:T(8,128)(2,1)S(1)}, bf16[4,208,128]{2,1,0:T(8,128)(2,1)S(1)}, u32[]{:S(2)}, u32[]{:S(2)}) collective-permute-start(bf16[4,208,128]{2,1,0:T(8,128)(2,1)S(1)} %all-to-all-done.1.refs_0_), channel_id=1, source_target_pairs={{0,24},{1,25},{2,26},{3,27},{4,28},{5,29},{6,30},{7,31},{8,0},{9,1... | collective-permute-start | bytes 638984 | tf_op jit(solution)/shard_map/ppermute | solution.py:232
  45.0 1.9 %collective-permute-start.4 = (bf16[4,208,128]{2,1,0:T(8,128)(2,1)S(1)}, bf16[4,208,128]{2,1,0:T(8,128)(2,1)S(1)}, u32[]{:S(2)}, u32[]{:S(2)}) collective-permute-start(bf16[4,208,128]{2,1,0:T(8,128)(2,1)S(1)} %all-to-all-done.1.refs_0_), channel_id=1, source_target_pairs={{0,1},{1,0},{2,3},{3,2},{4,5},{5,4},{6,7},{7,6},{8,9},{9,8},{10,11... | collective-permute-start | bytes 638984 | tf_op jit(solution)/shard_map/ppermute | solution.py:233
  46.9 0.0 collective-permute-done.1.refs_1_
  46.9 2.4 %collective-permute-start.5 = (bf16[4,208,128]{2,1,0:T(8,128)(2,1)S(1)}, bf16[4,208,128]{2,1,0:T(8,128)(2,1)S(1)}, u32[]{:S(2)}, u32[]{:S(2)}) collective-permute-start(bf16[4,208,128]{2,1,0:T(8,128)(2,1)S(1)} %collective-permute-done.1.refs_1_), channel_id=1, source_target_pairs={{0,1},{1,0},{2,3},{3,2},{4,5},{5,4},{6,7},{7,6},{8,9},{9,8},{10,11... | collective-permute-start | bytes 638984 | tf_op jit(solution)/shard_map/ppermute | solution.py:233
  49.3 0.0 collective-permute-done.2.refs_2_
  49.3 1.9 %collective-permute-start.6 = (bf16[4,208,128]{2,1,0:T(8,128)(2,1)S(1)}, bf16[4,208,128]{2,1,0:T(8,128)(2,1)S(1)}, u32[]{:S(2)}, u32[]{:S(2)}) collective-permute-start(bf16[4,208,128]{2,1,0:T(8,128)(2,1)S(1)} %collective-permute-done.2.refs_2_), channel_id=1, source_target_pairs={{0,1},{1,0},{2,3},{3,2},{4,5},{5,4},{6,7},{7,6},{8,9},{9,8},{10,11... | collective-permute-start | bytes 638984 | tf_op jit(solution)/shard_map/ppermute | solution.py:233
  51.3 0.0 collective-permute-done.3.refs_3_
  51.3 2.4 %collective-permute-start.7 = (bf16[4,208,128]{2,1,0:T(8,128)(2,1)S(1)}, bf16[4,208,128]{2,1,0:T(8,128)(2,1)S(1)}, u32[]{:S(2)}, u32[]{:S(2)}) collective-permute-start(bf16[4,208,128]{2,1,0:T(8,128)(2,1)S(1)} %collective-permute-done.3.refs_3_), channel_id=1, source_target_pairs={{0,1},{1,0},{2,3},{3,2},{4,5},{5,4},{6,7},{7,6},{8,9},{9,8},{10,11... | collective-permute-start | bytes 638984 | tf_op jit(solution)/shard_map/ppermute | solution.py:233
  53.7 0.0 copy-done.1
  53.7 0.2 copy.7
  54.0 0.1 pad_add_fusion.at_ref
  54.1 0.0 collective-permute-done.4.refs_4_
  54.1 0.0 collective-permute-done.5.refs_5_
  54.1 0.0 collective-permute-done.6.refs_6_
  54.1 0.7 collective-permute-done.7.refs_7_
  54.7 1.9 %all-to-all-done.r_ref = bf16[16,208,128]{2,1,0:T(8,128)(2,1)S(1)} async-done(((bf16[16,208,128]{2,1,0:T(8,128)(2,1)}), bf16[16,208,128]{2,1,0:T(8,128)(2,1)S(1)}, u32[]{:S(2)}, u32[]{:S(2)}) %all-to-all-start) | async-done | bytes 852000 | tf_op jit(solution)/shard_map/all_to_all | solution.py:188
  56.6 5.8 %shard_map.65 = bf16[4,2,144,128]{3,2,1,0:T(8,128)(2,1)S(1)} custom-call(s32[3]{0:T(128)S(1)} %pad_add_fusion.at_ref, bf16[16,208,128]{2,1,0:T(8,128)(2,1)S(1)} %all-to-all-done.r_ref, bf16[512,256]{1,0:T(8,128)(2,1)S(1)} %bitcast.15, bf16[4,208,128]{2,1,0:T(8,128)(2,1)S(1)} %all-to-all-done.1.refs_0_, ...), custom_call_target="tpu_custom_call" | custom-call | flops 3221225472 | bytes 4194304 | tf_op jit(solution)/shard_map/pallas_call | solution.py:235
  62.4 10.0 %all_to_all.15.pair_ref = bf16[4,2,144,128]{3,2,1,0:T(8,128)(2,1)S(1)} all-to-all(bf16[4,2,144,128]{3,2,1,0:T(8,128)(2,1)S(1)} %shard_map.65), channel_id=1, replica_groups=mesh['y'=8,'zl'=2,'x'=4,'zh'=4,'core'=2] {'x'}, dimensions={0} | all-to-all | bytes 589824 | tf_op jit(solution)/shard_map/all_to_all | solution.py:248
  72.4 0.0 copy-start
  72.4 0.6 copy-done
  73.0 0.9 %shard_map.66 = f32[12,96,128]{2,1,0:T(8,128)} custom-call(bf16[4,2,144,128]{3,2,1,0:T(8,128)(2,1)S(1)} %all_to_all.15.pair_ref, f32[1,128]{1,0:T(1,128)S(1)} %copy-done), custom_call_target="tpu_custom_call" | custom-call | tf_op jit(solution)/shard_map/pallas_call | solution.py:249
  (1 shorter events, 0.0 us)
Async XLA Ops:
  3.3 10.5 %copy-start.2 = (bf16[208,128]{1,0:T(8,128)(2,1)S(1)}, bf16[208,128]{1,0:T(8,128)(2,1)}, u32[]{:S(2)}) copy-start(bf16[208,128]{1,0:T(8,128)(2,1)} %get-tuple-element.8) | copy-start | bytes 159748
  3.3 22.4 %all-to-all-start.1 = ((bf16[4,208,128]{2,1,0:T(8,128)(2,1)}), bf16[4,208,128]{2,1,0:T(8,128)(2,1)S(1)}, u32[]{:S(2)}, u32[]{:S(2)}) async-start(bf16[4,208,128]{2,1,0:T(8,128)(2,1)} %get-tuple-element.9), calls=%async_computation.1 | async-start | bytes 425984 | tf_op jit(solution)/shard_map/all_to_all | solution.py:230
  13.7 12.0 %collective-permute-start = (bf16[208,128]{1,0:T(8,128)(2,1)S(1)}, bf16[208,128]{1,0:T(8,128)(2,1)S(1)}, u32[]{:S(2)}, u32[]{:S(2)}) collective-permute-start(bf16[208,128]{1,0:T(8,128)(2,1)S(1)} %copy-done.2), channel_id=1, source_target_pairs={{0,256},{1,192},{2,64},{3,128},{4,0},{5,448},{6,384},{7,320},{8,26... | collective-permute-start | bytes 159752 | tf_op jit(solution)/shard_map/ppermute | solution.py:229
  26.7 27.0 %copy-start.1 = (bf16[1024,128]{1,0:T(8,128)(2,1)S(1)}, bf16[1024,128]{1,0:T(8,128)(2,1)}, u32[]{:S(2)}) copy-start(bf16[1024,128]{1,0:T(8,128)(2,1)} %param.10) | copy-start | bytes 786436
  26.7 29.9 %all-to-all-start = ((bf16[16,208,128]{2,1,0:T(8,128)(2,1)}), bf16[16,208,128]{2,1,0:T(8,128)(2,1)S(1)}, u32[]{:S(2)}, u32[]{:S(2)}) async-start(bf16[16,208,128]{2,1,0:T(8,128)(2,1)} %broadcast_in_dim.2), calls=%async_computation | async-start | bytes 1703936 | tf_op jit(solution)/shard_map/all_to_all | solution.py:188
  34.5 12.4 %collective-permute-start.1 = (bf16[4,208,128]{2,1,0:T(8,128)(2,1)S(1)}, bf16[4,208,128]{2,1,0:T(8,128)(2,1)S(1)}, u32[]{:S(2)}, u32[]{:S(2)}) collective-permute-start(bf16[4,208,128]{2,1,0:T(8,128)(2,1)S(1)} %all-to-all-done.1.refs_0_), channel_id=1, source_target_pairs={{0,8},{1,9},{2,10},{3,11},{4,12},{5,13},{6,14},{7,15},{8,16},{9,17... | collective-permute-start | bytes 638984 | tf_op jit(solution)/shard_map/ppermute | solution.py:232
  37.9 11.4 %collective-permute-start.2 = (bf16[4,208,128]{2,1,0:T(8,128)(2,1)S(1)}, bf16[4,208,128]{2,1,0:T(8,128)(2,1)S(1)}, u32[]{:S(2)}, u32[]{:S(2)}) collective-permute-start(bf16[4,208,128]{2,1,0:T(8,128)(2,1)S(1)} %all-to-all-done.1.refs_0_), channel_id=1, source_target_pairs={{0,16},{1,17},{2,18},{3,19},{4,20},{5,21},{6,22},{7,23},{8,24},{9,... | collective-permute-start | bytes 638984 | tf_op jit(solution)/shard_map/ppermute | solution.py:232
  40.9 10.4 %collective-permute-start.3 = (bf16[4,208,128]{2,1,0:T(8,128)(2,1)S(1)}, bf16[4,208,128]{2,1,0:T(8,128)(2,1)S(1)}, u32[]{:S(2)}, u32[]{:S(2)}) collective-permute-start(bf16[4,208,128]{2,1,0:T(8,128)(2,1)S(1)} %all-to-all-done.1.refs_0_), channel_id=1, source_target_pairs={{0,24},{1,25},{2,26},{3,27},{4,28},{5,29},{6,30},{7,31},{8,0},{9,1... | collective-permute-start | bytes 638984 | tf_op jit(solution)/shard_map/ppermute | solution.py:232
  45.0 9.1 %collective-permute-start.4 = (bf16[4,208,128]{2,1,0:T(8,128)(2,1)S(1)}, bf16[4,208,128]{2,1,0:T(8,128)(2,1)S(1)}, u32[]{:S(2)}, u32[]{:S(2)}) collective-permute-start(bf16[4,208,128]{2,1,0:T(8,128)(2,1)S(1)} %all-to-all-done.1.refs_0_), channel_id=1, source_target_pairs={{0,1},{1,0},{2,3},{3,2},{4,5},{5,4},{6,7},{7,6},{8,9},{9,8},{10,11... | collective-permute-start | bytes 638984 | tf_op jit(solution)/shard_map/ppermute | solution.py:233
  46.9 7.2 %collective-permute-start.5 = (bf16[4,208,128]{2,1,0:T(8,128)(2,1)S(1)}, bf16[4,208,128]{2,1,0:T(8,128)(2,1)S(1)}, u32[]{:S(2)}, u32[]{:S(2)}) collective-permute-start(bf16[4,208,128]{2,1,0:T(8,128)(2,1)S(1)} %collective-permute-done.1.refs_1_), channel_id=1, source_target_pairs={{0,1},{1,0},{2,3},{3,2},{4,5},{5,4},{6,7},{7,6},{8,9},{9,8},{10,11... | collective-permute-start | bytes 638984 | tf_op jit(solution)/shard_map/ppermute | solution.py:233
  49.3 4.7 %collective-permute-start.6 = (bf16[4,208,128]{2,1,0:T(8,128)(2,1)S(1)}, bf16[4,208,128]{2,1,0:T(8,128)(2,1)S(1)}, u32[]{:S(2)}, u32[]{:S(2)}) collective-permute-start(bf16[4,208,128]{2,1,0:T(8,128)(2,1)S(1)} %collective-permute-done.2.refs_2_), channel_id=1, source_target_pairs={{0,1},{1,0},{2,3},{3,2},{4,5},{5,4},{6,7},{7,6},{8,9},{9,8},{10,11... | collective-permute-start | bytes 638984 | tf_op jit(solution)/shard_map/ppermute | solution.py:233
  51.3 3.5 %collective-permute-start.7 = (bf16[4,208,128]{2,1,0:T(8,128)(2,1)S(1)}, bf16[4,208,128]{2,1,0:T(8,128)(2,1)S(1)}, u32[]{:S(2)}, u32[]{:S(2)}) collective-permute-start(bf16[4,208,128]{2,1,0:T(8,128)(2,1)S(1)} %collective-permute-done.3.refs_3_), channel_id=1, source_target_pairs={{0,1},{1,0},{2,3},{3,2},{4,5},{5,4},{6,7},{7,6},{8,9},{9,8},{10,11... | collective-permute-start | bytes 638984 | tf_op jit(solution)/shard_map/ppermute | solution.py:233
  72.4 0.6 copy-start

commit v3 on v2

v3 whole, which is shorter than its diff:
```python
import numpy as np

import jax
import jax.numpy as jnp
from jax import lax
from jax.experimental import pallas as pl
from jax.experimental.pallas import tpu as pltpu
from jax.sharding import Mesh
from jax.sharding import PartitionSpec as P

F32, BF16 = jnp.float32, jnp.bfloat16
SIZES = (8, 2, 4, 4, 2)
AXES = ("y", "zl", "x", "zh", "core")
S, I, C, WIDTH, PAIR = 64, 12, 256, 32, 128
ROWS = 208
NT = (((1,), (1,)), ((), ()))
VMEM = pl.BlockSpec(memory_space=pltpu.VMEM)
HBM = pl.BlockSpec(memory_space=pltpu.HBM)
SMEM = pl.BlockSpec(memory_space=pltpu.SMEM)


def one_hot(shape, match):
    row = lax.broadcasted_iota(jnp.int32, shape, 0)
    col = lax.broadcasted_iota(jnp.int32, shape, 1)
    return match(row, col).astype(F32).astype(BF16)


def dot(a, b, dims=(((1,), (0,)), ((), ()))):
    return lax.dot_general(a, b, dims, preferred_element_type=F32)


def project_kernel(
    x_in, m_in, wl_in, wr_in, offset_in, l_ref, r_ref, x_ref, m_ref, wl_ref, wr_ref, offset_ref, spread, sems
):
    pairs = [
        (x_in, x_ref), (m_in, m_ref), (wl_in, wl_ref), (wr_in, wr_ref), (offset_in, offset_ref)
    ]
    copies = [
        pltpu.make_async_copy(source, target, sems.at[n])
        for n, (source, target) in enumerate(pairs)
    ]
    for copy in copies:
        copy.start()
    for copy in copies:
        copy.wait()
    mask = m_ref[...].astype(F32).astype(BF16)
    mask_twice = jnp.concatenate([mask, mask], axis=1)
    mask_rows = dot(one_hot((16, I), lambda r, t: r == t), mask_twice)
    mask_pairs = dot(one_hot((32, I), lambda r, t: r // 2 == t), mask_twice)
    mask_cols = dot(one_hot((S, S), lambda r, t: r == t), mask, NT)
    wl = dot(one_hot((128, WIDTH), lambda r, t: r % WIDTH == t), wl_ref[...])
    wr = dot(
        one_hot((128, WIDTH), lambda r, t: t == 2 * (r % 16) + r % WIDTH // 16), wr_ref[...]
    )
    weights = jnp.concatenate([wl, wr], axis=0).astype(BF16)
    block = lax.broadcasted_iota(jnp.int32, (S, 256), 1) % 128 // WIDTH
    low = lax.broadcasted_iota(jnp.int32, (8, 128), 1) < 64
    for g in range(I // 4):
        x = x_ref[4 * g : 4 * g + 4].reshape(4 * S, C).astype(F32)
        centred = x - jnp.sum(x, axis=-1, keepdims=True) * (1.0 / C)
        variance = jnp.sum(centred * centred, axis=-1, keepdims=True) * (1.0 / C)
        normed = centred * lax.rsqrt(variance + 1e-05)
        high = normed.astype(BF16)
        rest = (normed - high.astype(F32)).astype(BF16)
        both = dot(high, weights, NT) + dot(rest, weights, NT)
        tile = None
        for k in range(4):
            i = 4 * g + k
            part = both[k * S : k * S + S] * mask_cols[:, i : i + 1]
            tile = part if k == 0 else jnp.where(block == k, part, tile)
        l_ref[0, g * S : (g + 1) * S, :] = tile[:, 0:128].astype(BF16)
        right = tile[:, 128:256]
        right = jnp.concatenate([right, right], axis=0).T
        for k in range(4):
            for e in range(2):
                row = k * WIDTH + e * 16
                part = jnp.where(low, right[row : row + 8], right[row + 8 : row + 16])
                spread[pl.ds(2 * (4 * g + k) + e, 8, stride=24), :] = part
    row = lax.broadcasted_iota(jnp.int32, (16, 128), 0)
    last, rest = mask_rows, offset_ref[...]
    for n in range(3):
        part = rest.astype(BF16).astype(F32)
        last = jnp.where(row == I + n, jnp.broadcast_to(part, (16, 128)), last)
        rest = rest - part
    l_ref[0, 192:208, :] = last.astype(BF16)
    r_ref[0:192, :] = spread[...].astype(BF16)
    low16 = lax.broadcasted_iota(jnp.int32, (16, 128), 1) < 64
    r_ref[192:208, :] = jnp.where(low16, mask_pairs[0:16], mask_pairs[16:32]).astype(BF16)


def placed(step, core):
    zl = (step >= 1) & (step <= 4)
    far = zl * (step - 1) + (1 - zl) * ((8 - step) & 7)
    return core * (3 - far) + (1 - core) * (4 + far), zl


def pair_kernel(at_ref, r_ref, w_ref, lm_ref, lo_ref, out_ref, offset_ref, rt, rmask, lmask, z):
    zh, core, x = at_ref[0], at_ref[1], at_ref[2]
    low = lax.broadcasted_iota(jnp.int32, (ROWS, 128), 1) < 64
    low16 = lax.broadcasted_iota(jnp.int32, (16, 128), 1) < 64

    def piece(zl, t, c):
        step = (2 * ((zh ^ (0, 2, 1, 3)[t]) - zh) + zl) & 7
        target = jnp.where((step >= 1) & (step <= 4), 1, 0)
        far = jnp.where(target == 1, step - 1, (8 - step) & 7)
        shift = jnp.where(c == 1, 3 - far, 4 + far)
        return r_ref[((2 * zh + core + shift) & 7) * 2 + target]

    for zl in range(2):
        for t in range(4):
            a, b = piece(zl, t, core), piece(zl, t, 1 - core)
            first = jnp.where(low, a, pltpu.roll(b, 64, 1))
            second = jnp.where(low, pltpu.roll(a, 64, 1), b)
            cols = slice(t * 128, t * 128 + 128)
            rt[zl, 0:192, cols] = first[0:192]
            rt[zl, 192:384, cols] = second[0:192]
            rmask[zl, 0:16, cols] = first[192:208]
            rmask[zl, 16:32, cols] = second[192:208]
    for k in range(4):
        for t in range(4):
            a, b = lm_ref[4 * k + t, 192:208, :], lo_ref[4 * k + t, 192:208, :]
            lmask[k * 16 : k * 16 + 16, t * 128 : t * 128 + 128] = jnp.where(low16, a, b)
    parts = lm_ref[0, 192:208, :].astype(F32)
    offset_ref[...] = parts[12:13] + parts[13:14] + parts[14:15]
    scale = jnp.concatenate(
        [1.0 / (dot(rmask[zl], lmask[...], NT)[0:24] + 1.0) for zl in range(2)], axis=0
    )

    lanes = lax.broadcasted_iota(jnp.int32, (48, 128), 1)
    half = lanes < 64
    even = (lanes // WIDTH) % 2 == 0
    for pair in range(2):
        rhs = jnp.concatenate(
            [
                jnp.concatenate(
                    [
                        ref[4 * k + t, g * S : g * S + S, :]
                        for k in (2 * pair, 2 * pair + 1)
                        for g in range(3)
                    ],
                    axis=1,
                )
                for t in range(4)
                for ref in (lm_ref, lo_ref)
            ],
            axis=0,
        )
        outer = [dot(rt[zl], rhs) for zl in range(2)]
        for n in range(2):
            left_rows = []
            for g in range(3 * n, 3 * n + 3):
                cols = slice(g * 128, g * 128 + 128)
                quads = [[], [], [], []]
                for q in range(4):
                    a = [
                        jnp.concatenate([o[e * 24 : e * 24 + 24, cols] for o in outer], axis=0)
                        .astype(BF16)
                        for e in range(4 * q, 4 * q + 4)
                    ]
                    a0 = jnp.where(half, a[0], pltpu.roll(a[2], 64, 1))
                    a1 = jnp.where(half, a[1], pltpu.roll(a[3], 64, 1))
                    a2 = jnp.where(half, pltpu.roll(a[0], 64, 1), a[2])
                    a3 = jnp.where(half, pltpu.roll(a[1], 64, 1), a[3])
                    quads[0].append(jnp.where(even, a0, pltpu.roll(a1, 32, 1)))
                    quads[1].append(jnp.where(even, pltpu.roll(a0, 96, 1), a1))
                    quads[2].append(jnp.where(even, a2, pltpu.roll(a3, 32, 1)))
                    quads[3].append(jnp.where(even, pltpu.roll(a2, 96, 1), a3))
                left_rows += [jnp.concatenate(quad, axis=1) for quad in quads]
            wide = dot(jnp.concatenate(left_rows, axis=0), w_ref[...])
            k = 2 * pair + n
            for i in range(I):
                column = scale[:, k * 16 + i : k * 16 + i + 1]
                for e in range(2):
                    z[e, i * 48 : i * 48 + 48, :] = (
                        wide[i * 48 : i * 48 + 48, e * 128 : e * 128 + 128] * column
                    )
            result = z[0, pl.ds(0, 288, stride=2), :] + z[1, pl.ds(1, 288, stride=2), :]
            out_ref[(x - k) & 3] = result.astype(BF16)


def finish_kernel(pair_ref, offset_ref, out_ref):
    offset = offset_ref[...]
    for x1 in range(4):
        block = pair_ref[x1].astype(F32) + offset
        for i in range(I):
            for zl in range(2):
                at, row = (zl * 4 + x1) * I, (2 * i + zl) * I
                out_ref[i, at : at + I, :] = block[row : row + I, :]


def swap(match):
    index = np.arange(int(np.prod(SIZES))).reshape(SIZES)
    return [(int(index[at]), int(index[match(*at)])) for at in np.ndindex(*SIZES)]


def shifted(y, zl, x, zh, c):
    shift, target = placed((2 * zh + zl - y // 2 * 2) % 8, c)
    return (y + shift) % 8, int(target), x, y // 2, y % 2


TRANSPOSE = swap(shifted)
ALONG_X = [swap(lambda y, zl, x, zh, c, k=k: (y, zl, (x + k) % 4, zh, c)) for k in range(4)]
ACROSS_ZH = [swap(lambda y, zl, x, zh, c, k=k: (y, zl, x, zh ^ k, c)) for k in range(4)]
OTHER_CORE = swap(lambda y, zl, x, zh, c: (y, zl, x, zh, 1 - c))


def spread_along(value, axis, count):
    return lax.all_to_all(
        jnp.broadcast_to(value[None], (count,) + value.shape), axis, 0, 0, tiled=True
    )


def call(kernel, out_shape, in_specs, scratch_shapes=(), vmem=48, flops=0, bytes_accessed=0):
    return pl.pallas_call(
        kernel,
        out_shape=out_shape,
        in_specs=in_specs,
        out_specs=jax.tree.map(lambda _: VMEM, out_shape),
        scratch_shapes=scratch_shapes,
        compiler_params=pltpu.CompilerParams(vmem_limit_bytes=vmem << 20),
        cost_estimate=pl.CostEstimate(
            flops=flops, bytes_accessed=bytes_accessed, transcendentals=0
        ),
    )


def local(x, m, wl, wr, w, offset):
    left, right = call(
        project_kernel,
        [
            jax.ShapeDtypeStruct((1, ROWS, 128), BF16),
            jax.ShapeDtypeStruct((ROWS, 128), BF16),
        ],
        [HBM] * 5,
        [
            pltpu.VMEM((I, S, C), BF16),
            pltpu.VMEM((I, S), jnp.int32),
            pltpu.VMEM((WIDTH, C), BF16),
            pltpu.VMEM((WIDTH, C), BF16),
            pltpu.VMEM((1, PAIR), F32),
            pltpu.VMEM((192, 128), F32),
            pltpu.SemaphoreType.DMA((5,)),
        ],
        vmem=60,
    )(x.transpose(1, 0, 2), m.T, wl.T, wr.T, offset.reshape(1, PAIR))
    w2 = w.reshape(WIDTH, 16, 2, PAIR).transpose(1, 0, 2, 3).reshape(512, 2 * PAIR)
    at = jnp.stack([lax.axis_index(name) for name in ("zh", "core", "x")]).astype(jnp.int32)

    right = lax.ppermute(right, AXES, TRANSPOSE)
    right = jnp.broadcast_to(right[None], (16, ROWS, 128))
    left = jnp.concatenate([left, lax.ppermute(left, AXES, ACROSS_ZH[2])])
    left = jnp.concatenate([left, lax.ppermute(left, AXES, ACROSS_ZH[1])])
    left = lax.optimization_barrier((left, right))[0]
    right = lax.all_to_all(right, ("y", "zl"), 0, 0, tiled=True)
    left = jnp.concatenate(
        [left] + [lax.ppermute(left, AXES, ALONG_X[k]) for k in (1, 2, 3)], axis=0
    )
    left_other = lax.ppermute(left, AXES, OTHER_CORE)

    pairs, offset = call(
        pair_kernel,
        [jax.ShapeDtypeStruct((4, 288, 128), BF16), jax.ShapeDtypeStruct((1, PAIR), F32)],
        [SMEM] + [VMEM] * 4,
        [
            pltpu.VMEM((2, 384, 512), BF16),
            pltpu.VMEM((2, 32, 512), BF16),
            pltpu.VMEM((64, 512), BF16),
            pltpu.VMEM((2, 576, 128), F32),
        ],
        flops=3 << 30,
        bytes_accessed=4 << 20,
    )(at, right, w2, left, left_other)
    pairs = lax.all_to_all(pairs, "x", 0, 0, tiled=True)
    return call(
        finish_kernel, jax.ShapeDtypeStruct((I, 96, PAIR), F32), [VMEM, VMEM]
    )(pairs, offset)


def solution(mesh):
    fine = Mesh(mesh.devices.reshape(SIZES), AXES)
    res, seq = ("y", "zl", "x"), ("zh", "core")
    return jax.shard_map(
        local,
        mesh=fine,
        in_specs=(P(seq, res, None), P(seq, res), P(), P(), P(), P()),
        out_specs=P(res, seq, None),
        check_vma=False,
    )
```

time: 74.4 us -> 70.3 us (0.945)
  starting transfers between devices: 45 us -> 41.2 us
  Pallas kernels: 9.89 us -> 7.06 us
  waiting for transfers between devices: 6.78 us -> 8.99 us
  other arithmetic: 0.08 us -> 0.93 us
    all_to_all x2 -> x1, starting transfers between devices: 18.2 us -> 6.64 us  [local(): right = lax.all_to_all(right, ('y', 'zl'), 0, 0, tiled=True)]
    ppermute x7 -> x6, starting transfers between devices: 19.1 us -> 26.8 us  [the longest x1 10.9 us: local(): left = jnp.concatenate([left, lax.ppermute(left, AXES, ACROSS_ZH[2])])]
    ppermute x7 -> x6, waiting for transfers between devices: 0.69 us -> 7.17 us  [the longest x3 5.2 us: local(): lax.ppermute(left, AXES, ALONG_X[k])]
    ppermute x1, waiting for transfers between devices: 4.24 us -> 0.01 us  [local(): right = lax.ppermute(right, AXES, TRANSPOSE)]
    pallas_call x2, Pallas kernels: 9.02 us -> 6.21 us  [the longest x1 3.65 us: local(): call(pair_kernel, [jax.ShapeDtypeStruct((4, 288, 128), BF16), jax.ShapeDt...]
    concatenate x0 -> x2, other arithmetic: none -> 0.85 us  [the longest x1 0.82 us: local(): left = jnp.concatenate([left, lax.ppermute(left, AXES, ACROSS_ZH[2])])]
    all_to_all x2 -> x1, waiting for transfers between devices: 1.85 us -> 1.82 us  [local(): right = lax.all_to_all(right, ('y', 'zl'), 0, 0, tiled=True)]
  transfers between devices with their start and end apart: 10 -> 8, of which waited for: 3 -> 4; matrix products, arithmetic and copies ran while one was open for 0% -> 3% of each run, Pallas kernels for 0% -> 0%
where the time goes in v3:
time: 70.3 us; the launch traced here: 69.8 us
  starting transfers between devices  41.2 us (59%)
  blocking collectives  10 us (14%)
  waiting for transfers between devices  8.99 us (13%)
  Pallas kernels  7.06 us (10%)
  local copies, waits for them, and re-layouts  1.42 us (2%)
  other arithmetic  0.93 us (1%)
    ppermute x1, starting transfers between devices, local(): left = jnp.concatenate([left, lax.ppermute(left, AXES, ACROSS_ZH[2])])  10.9 us
    ppermute x3, starting transfers between devices, local(): lax.ppermute(left, AXES, ALONG_X[k])  10.5 us
    all_to_all x1, blocking collectives, local(): pairs = lax.all_to_all(pairs, 'x', 0, 0, tiled=True)  10 us
    ppermute x1, starting transfers between devices, local(): right = lax.ppermute(right, AXES, TRANSPOSE)  7.73 us
    all_to_all x1, starting transfers between devices, local(): right = lax.all_to_all(right, ('y', 'zl'), 0, 0, tiled=True)  6.64 us
    ppermute x3, waiting for transfers between devices, local(): lax.ppermute(left, AXES, ALONG_X[k])  5.2 us
    pallas_call x1, Pallas kernels, local(): call(pair_kernel, [jax.ShapeDtypeStruct((4, 288, 128), BF16), jax.ShapeDt...  3.65 us
    ppermute x1, starting transfers between devices, local(): left = jnp.concatenate([left, lax.ppermute(left, AXES, ACROSS_ZH[1])])  3.49 us
  transfers between devices with their start and end apart: 8, of which 4 were waited for; matrix products, arithmetic and copies ran while one was open for 3% of the time, Pallas kernels for 0%

profile of v3, /device:TPU:2, one launch (start us, length us, event | category | flops | bytes accessed | tf_op | source)
XLA Modules:
  0.0 69.8 jit_solution(10971507999667056089)
XLA Ops:
  0.0 2.6 %shard_map.64 = (bf16[1,208,128]{2,1,0:T(8,128)(2,1)}, bf16[208,128]{1,0:T(8,128)(2,1)}) custom-call(bf16[12,64,256]{2,1,0:T(8,128)(2,1)} %bitcast.17, s32[12,64]{1,0:T(8,128)} %bitcast.21, bf16[32,256]{1,0:T(8,128)(2,1)} %bitcast.19, bf16[32,256]{1,0:T(8,128)(2,1)} %bitcast.20, f32[1,128]{1,0:T(1,128)} %bitcast.22), custom_call_target="tpu_custom_call" | custom-call | tf_op jit(solution)/shard_map/pallas_call | solution.py:228
  2.6 10.9 %collective-permute-start.1 = (bf16[1,208,128]{2,1,0:T(8,128)(2,1)}, bf16[1,208,128]{2,1,0:T(8,128)(2,1)S(1)}, u32[]{:S(2)}, u32[]{:S(2)}) collective-permute-start(bf16[1,208,128]{2,1,0:T(8,128)(2,1)} %get-tuple-element.11), channel_id=1, source_target_pairs={{0,4},{1,5},{2,6},{3,7},{4,0},{5,1},{6,2},{7,3},{8,12},{9,13},{10,... | collective-permute-start | bytes 159752 | tf_op jit(solution)/shard_map/ppermute | solution.py:251
  13.5 7.7 %collective-permute-start = (bf16[208,128]{1,0:T(8,128)(2,1)}, bf16[208,128]{1,0:T(8,128)(2,1)S(1)}, u32[]{:S(2)}, u32[]{:S(2)}) collective-permute-start(bf16[208,128]{1,0:T(8,128)(2,1)} %get-tuple-element.10), channel_id=1, source_target_pairs={{0,256},{1,192},{2,352},{3,160},{4,480},{5,32},{6,384},{7,64},{8,2... | collective-permute-start | bytes 159752 | tf_op jit(solution)/shard_map/ppermute | solution.py:249
  21.2 0.0 collective-permute-done.1
  21.2 0.8 %pad_maximum_fusion.1 = bf16[2,208,128]{2,1,0:T(8,128)(2,1)S(1)} fusion(bf16[1,208,128]{2,1,0:T(8,128)(2,1)S(1)} %collective-permute-done.1, bf16[1,208,128]{2,1,0:T(8,128)(2,1)} %get-tuple-element.11), kind=kLoop, calls=%fused_computation.2 | loop fusion | flops 53248 | bytes 212992 | tf_op jit(solution)/shard_map/concatenate | solution.py:251
  22.1 3.5 %collective-permute-start.2 = (bf16[2,208,128]{2,1,0:T(8,128)(2,1)S(1)}, bf16[2,208,128]{2,1,0:T(8,128)(2,1)S(1)}, u32[]{:S(2)}, u32[]{:S(2)}) collective-permute-start(bf16[2,208,128]{2,1,0:T(8,128)(2,1)S(1)} %pad_maximum_fusion.1), channel_id=1, source_target_pairs={{0,2},{1,3},{2,0},{3,1},{4,6},{5,7},{6,4},{7,5},{8,10},{9,11},{10,... | collective-permute-start | bytes 319496 | tf_op jit(solution)/shard_map/ppermute | solution.py:252
  25.6 0.0 collective-permute-done
  25.6 1.0 %broadcast_in_dim.2 = bf16[16,208,128]{2,1,0:T(8,128)(2,1)} broadcast(bf16[208,128]{1,0:T(8,128)(2,1)S(1)} %collective-permute-done), dimensions={1,2} | broadcast | bytes 905216 | tf_op jit(solution)/shard_map/broadcast_in_dim | solution.py:250
  26.6 0.0 copy-start.1
  26.6 6.6 %all-to-all-start = ((bf16[16,208,128]{2,1,0:T(8,128)(2,1)}), bf16[16,208,128]{2,1,0:T(8,128)(2,1)S(1)}, u32[]{:S(2)}, u32[]{:S(2)}) async-start(bf16[16,208,128]{2,1,0:T(8,128)(2,1)} %broadcast_in_dim.2), calls=%async_computation | async-start | bytes 1703936 | tf_op jit(solution)/shard_map/all_to_all | solution.py:254
  33.3 0.0 collective-permute-done.2
  33.3 0.0 copy-done.1
  33.3 3.4 %collective-permute-start.3 = (bf16[4,208,128]{2,1,0:T(8,128)(2,1)S(1)}, bf16[4,208,128]{2,1,0:T(8,128)(2,1)S(1)}, u32[]{:S(2)}, u32[]{:S(2)}) collective-permute-start(bf16[4,208,128]{2,1,0:T(8,128)(2,1)S(1)} %pad_maximum_fusion), channel_id=1, source_target_pairs={{0,8},{1,9},{2,10},{3,11},{4,12},{5,13},{6,14},{7,15},{8,16},{9,17... | collective-permute-start | bytes 638984 | tf_op jit(solution)/shard_map/ppermute | solution.py:256
  36.7 3.0 %collective-permute-start.4 = (bf16[4,208,128]{2,1,0:T(8,128)(2,1)S(1)}, bf16[4,208,128]{2,1,0:T(8,128)(2,1)S(1)}, u32[]{:S(2)}, u32[]{:S(2)}) collective-permute-start(bf16[4,208,128]{2,1,0:T(8,128)(2,1)S(1)} %pad_maximum_fusion), channel_id=1, source_target_pairs={{0,16},{1,17},{2,18},{3,19},{4,20},{5,21},{6,22},{7,23},{8,24},{9,... | collective-permute-start | bytes 638984 | tf_op jit(solution)/shard_map/ppermute | solution.py:256
  39.7 4.1 %collective-permute-start.5 = (bf16[4,208,128]{2,1,0:T(8,128)(2,1)S(1)}, bf16[4,208,128]{2,1,0:T(8,128)(2,1)S(1)}, u32[]{:S(2)}, u32[]{:S(2)}) collective-permute-start(bf16[4,208,128]{2,1,0:T(8,128)(2,1)S(1)} %pad_maximum_fusion), channel_id=1, source_target_pairs={{0,24},{1,25},{2,26},{3,27},{4,28},{5,29},{6,30},{7,31},{8,0},{9,1... | collective-permute-start | bytes 638984 | tf_op jit(solution)/shard_map/ppermute | solution.py:256
  43.8 0.0 collective-permute-done.3
  43.9 3.1 %collective-permute-done.4 = bf16[4,208,128]{2,1,0:T(8,128)(2,1)S(1)} collective-permute-done((bf16[4,208,128]{2,1,0:T(8,128)(2,1)S(1)}, bf16[4,208,128]{2,1,0:T(8,128)(2,1)S(1)}, u32[]{:S(2)}, u32[]{:S(2)}) %collective-permute-start.4) | collective-permute-done | bytes 213024 | tf_op jit(solution)/shard_map/ppermute | solution.py:256
  47.0 0.0 copy-start
  47.0 2.1 %collective-permute-done.5 = bf16[4,208,128]{2,1,0:T(8,128)(2,1)S(1)} collective-permute-done((bf16[4,208,128]{2,1,0:T(8,128)(2,1)S(1)}, bf16[4,208,128]{2,1,0:T(8,128)(2,1)S(1)}, u32[]{:S(2)}, u32[]{:S(2)}) %collective-permute-start.5) | collective-permute-done | bytes 213024 | tf_op jit(solution)/shard_map/ppermute | solution.py:256
  49.2 1.9 %collective-permute-start.6 = (bf16[16,208,128]{2,1,0:T(8,128)(2,1)S(1)}, bf16[16,208,128]{2,1,0:T(8,128)(2,1)S(1)}, u32[]{:S(2)}, u32[]{:S(2)}) collective-permute-start(bf16[16,208,128]{2,1,0:T(8,128)(2,1)S(1)} %constant_dynamic-update-slice_fusion.lm_ref), channel_id=1, source_target_pairs={{0,1},{1,0},{2,3},{3,2},{4,5},{5,4},{6,7},{7,6},{8,9},{9,8},{10,11... | collective-permute-start | bytes 2555912 | tf_op jit(solution)/shard_map/ppermute | solution.py:258
  51.1 0.0 copy-done
  51.1 0.2 copy.7
  51.4 0.1 pad_add_fusion.at_ref
  51.5 2.0 %collective-permute-done.6.lo_ref = bf16[16,208,128]{2,1,0:T(8,128)(2,1)S(1)} collective-permute-done((bf16[16,208,128]{2,1,0:T(8,128)(2,1)S(1)}, bf16[16,208,128]{2,1,0:T(8,128)(2,1)S(1)}, u32[]{:S(2)}, u32[]{:S(2)}) %collective-permute-start.6) | collective-permute-done | bytes 852000 | tf_op jit(solution)/shard_map/ppermute | solution.py:258
  53.4 1.8 %all-to-all-done.r_ref = bf16[16,208,128]{2,1,0:T(8,128)(2,1)S(1)} async-done(((bf16[16,208,128]{2,1,0:T(8,128)(2,1)}), bf16[16,208,128]{2,1,0:T(8,128)(2,1)S(1)}, u32[]{:S(2)}, u32[]{:S(2)}) %all-to-all-start) | async-done | bytes 852000 | tf_op jit(solution)/shard_map/all_to_all | solution.py:254
  55.3 3.7 %shard_map.65 = (bf16[4,288,128]{2,1,0:T(8,128)(2,1)S(1)}, f32[1,128]{1,0:T(1,128)S(1)}) custom-call(s32[3]{0:T(128)S(1)} %pad_add_fusion.at_ref, bf16[16,208,128]{2,1,0:T(8,128)(2,1)S(1)} %all-to-all-done.r_ref, bf16[512,256]{1,0:T(8,128)(2,1)S(1)} %bitcast.15, bf16[16,208,128]{2,1,0:T(8,128)(2,1)S(1)} %constant_dynamic-update-slice_fusion.lm_ref, ...), custom_call_target="tpu_custom_call" | custom-call | flops 3221225472 | bytes 4194304 | tf_op jit(solution)/shard_map/pallas_call | solution.py:260
  58.9 10.0 %all_to_all.10.pair_ref = bf16[4,288,128]{2,1,0:T(8,128)(2,1)S(1)} all-to-all(bf16[4,288,128]{2,1,0:T(8,128)(2,1)S(1)} %get-tuple-element.13), channel_id=1, replica_groups=mesh['y'=8,'zl'=2,'x'=4,'zh'=4,'core'=2] {'x'}, dimensions={0} | all-to-all | bytes 589824 | tf_op jit(solution)/shard_map/all_to_all | solution.py:273
  68.9 0.9 %shard_map.66 = f32[12,96,128]{2,1,0:T(8,128)} custom-call(bf16[4,288,128]{2,1,0:T(8,128)(2,1)S(1)} %all_to_all.10.pair_ref, f32[1,128]{1,0:T(1,128)S(1)} %get-tuple-element.14.offset_ref), custom_call_target="tpu_custom_call" | custom-call | tf_op jit(solution)/shard_map/pallas_call | solution.py:274
  (6 shorter events, 0.2 us)
Async XLA Ops:
  2.6 18.7 %collective-permute-start.1 = (bf16[1,208,128]{2,1,0:T(8,128)(2,1)}, bf16[1,208,128]{2,1,0:T(8,128)(2,1)S(1)}, u32[]{:S(2)}, u32[]{:S(2)}) collective-permute-start(bf16[1,208,128]{2,1,0:T(8,128)(2,1)} %get-tuple-element.11), channel_id=1, source_target_pairs={{0,4},{1,5},{2,6},{3,7},{4,0},{5,1},{6,2},{7,3},{8,12},{9,13},{10,... | collective-permute-start | bytes 159752 | tf_op jit(solution)/shard_map/ppermute | solution.py:251
  13.5 12.1 %collective-permute-start = (bf16[208,128]{1,0:T(8,128)(2,1)}, bf16[208,128]{1,0:T(8,128)(2,1)S(1)}, u32[]{:S(2)}, u32[]{:S(2)}) collective-permute-start(bf16[208,128]{1,0:T(8,128)(2,1)} %get-tuple-element.10), channel_id=1, source_target_pairs={{0,256},{1,192},{2,352},{3,160},{4,480},{5,32},{6,384},{7,64},{8,2... | collective-permute-start | bytes 159752 | tf_op jit(solution)/shard_map/ppermute | solution.py:249
  22.1 11.2 %collective-permute-start.2 = (bf16[2,208,128]{2,1,0:T(8,128)(2,1)S(1)}, bf16[2,208,128]{2,1,0:T(8,128)(2,1)S(1)}, u32[]{:S(2)}, u32[]{:S(2)}) collective-permute-start(bf16[2,208,128]{2,1,0:T(8,128)(2,1)S(1)} %pad_maximum_fusion.1), channel_id=1, source_target_pairs={{0,2},{1,3},{2,0},{3,1},{4,6},{5,7},{6,4},{7,5},{8,10},{9,11},{10,... | collective-permute-start | bytes 319496 | tf_op jit(solution)/shard_map/ppermute | solution.py:252
  26.6 6.7 %copy-start.1 = (bf16[1,208,128]{2,1,0:T(8,128)(2,1)S(1)}, bf16[1,208,128]{2,1,0:T(8,128)(2,1)}, u32[]{:S(2)}) copy-start(bf16[1,208,128]{2,1,0:T(8,128)(2,1)} %get-tuple-element.11) | copy-start | bytes 159748
  26.6 28.6 %all-to-all-start = ((bf16[16,208,128]{2,1,0:T(8,128)(2,1)}), bf16[16,208,128]{2,1,0:T(8,128)(2,1)S(1)}, u32[]{:S(2)}, u32[]{:S(2)}) async-start(bf16[16,208,128]{2,1,0:T(8,128)(2,1)} %broadcast_in_dim.2), calls=%async_computation | async-start | bytes 1703936 | tf_op jit(solution)/shard_map/all_to_all | solution.py:254
  33.3 10.5 %collective-permute-start.3 = (bf16[4,208,128]{2,1,0:T(8,128)(2,1)S(1)}, bf16[4,208,128]{2,1,0:T(8,128)(2,1)S(1)}, u32[]{:S(2)}, u32[]{:S(2)}) collective-permute-start(bf16[4,208,128]{2,1,0:T(8,128)(2,1)S(1)} %pad_maximum_fusion), channel_id=1, source_target_pairs={{0,8},{1,9},{2,10},{3,11},{4,12},{5,13},{6,14},{7,15},{8,16},{9,17... | collective-permute-start | bytes 638984 | tf_op jit(solution)/shard_map/ppermute | solution.py:256
  36.7 10.2 %collective-permute-start.4 = (bf16[4,208,128]{2,1,0:T(8,128)(2,1)S(1)}, bf16[4,208,128]{2,1,0:T(8,128)(2,1)S(1)}, u32[]{:S(2)}, u32[]{:S(2)}) collective-permute-start(bf16[4,208,128]{2,1,0:T(8,128)(2,1)S(1)} %pad_maximum_fusion), channel_id=1, source_target_pairs={{0,16},{1,17},{2,18},{3,19},{4,20},{5,21},{6,22},{7,23},{8,24},{9,... | collective-permute-start | bytes 638984 | tf_op jit(solution)/shard_map/ppermute | solution.py:256
  39.7 9.4 %collective-permute-start.5 = (bf16[4,208,128]{2,1,0:T(8,128)(2,1)S(1)}, bf16[4,208,128]{2,1,0:T(8,128)(2,1)S(1)}, u32[]{:S(2)}, u32[]{:S(2)}) collective-permute-start(bf16[4,208,128]{2,1,0:T(8,128)(2,1)S(1)} %pad_maximum_fusion), channel_id=1, source_target_pairs={{0,24},{1,25},{2,26},{3,27},{4,28},{5,29},{6,30},{7,31},{8,0},{9,1... | collective-permute-start | bytes 638984 | tf_op jit(solution)/shard_map/ppermute | solution.py:256
  47.0 4.1 %copy-start = (bf16[1024,128]{1,0:T(8,128)(2,1)S(1)}, bf16[1024,128]{1,0:T(8,128)(2,1)}, u32[]{:S(2)}) copy-start(bf16[1024,128]{1,0:T(8,128)(2,1)} %param.10) | copy-start | bytes 786436
  49.2 4.3 %collective-permute-start.6 = (bf16[16,208,128]{2,1,0:T(8,128)(2,1)S(1)}, bf16[16,208,128]{2,1,0:T(8,128)(2,1)S(1)}, u32[]{:S(2)}, u32[]{:S(2)}) collective-permute-start(bf16[16,208,128]{2,1,0:T(8,128)(2,1)S(1)} %constant_dynamic-update-slice_fusion.lm_ref), channel_id=1, source_target_pairs={{0,1},{1,0},{2,3},{3,2},{4,5},{5,4},{6,7},{7,6},{8,9},{9,8},{10,11... | collective-permute-start | bytes 2555912 | tf_op jit(solution)/shard_map/ppermute | solution.py:258

commit v4 on v3

--- a/solution.py
+++ b/solution.py
@@ -248,7 +248,9 @@
 
     right = lax.ppermute(right, AXES, TRANSPOSE)
     right = jnp.broadcast_to(right[None], (16, ROWS, 128))
-    left = jnp.concatenate([left, lax.ppermute(left, AXES, ACROSS_ZH[2])])
+    left = lax.optimization_barrier(
+        jnp.concatenate([left, lax.ppermute(left, AXES, ACROSS_ZH[2])])
+    )
     left = jnp.concatenate([left, lax.ppermute(left, AXES, ACROSS_ZH[1])])
     left = lax.optimization_barrier((left, right))[0]
     right = lax.all_to_all(right, ("y", "zl"), 0, 0, tiled=True)

time: 70.3 us -> 70.1 us (level)
  no operation moved by 1% of the time
where the time goes in v4:
time: 70.1 us; the launch traced here: 69.7 us
  starting transfers between devices  41.1 us (59%)
  blocking collectives  10 us (14%)
  waiting for transfers between devices  9 us (13%)
  Pallas kernels  7.06 us (10%)
  local copies, waits for them, and re-layouts  1.42 us (2%)
  other arithmetic  0.92 us (1%)
    ppermute x1, starting transfers between devices, local(): lax.ppermute(left, AXES, ACROSS_ZH[2])  10.9 us
    ppermute x3, starting transfers between devices, local(): lax.ppermute(left, AXES, ALONG_X[k])  10.5 us
    all_to_all x1, blocking collectives, local(): pairs = lax.all_to_all(pairs, 'x', 0, 0, tiled=True)  10 us
    ppermute x1, starting transfers between devices, local(): right = lax.ppermute(right, AXES, TRANSPOSE)  7.73 us
    all_to_all x1, starting transfers between devices, local(): right = lax.all_to_all(right, ('y', 'zl'), 0, 0, tiled=True)  6.51 us
    ppermute x3, waiting for transfers between devices, local(): lax.ppermute(left, AXES, ALONG_X[k])  5.2 us
    pallas_call x1, Pallas kernels, local(): call(pair_kernel, [jax.ShapeDtypeStruct((4, 288, 128), BF16), jax.ShapeDt...  3.65 us
    ppermute x1, starting transfers between devices, local(): left = jnp.concatenate([left, lax.ppermute(left, AXES, ACROSS_ZH[1])])  3.49 us
  transfers between devices with their start and end apart: 8, of which 4 were waited for; matrix products, arithmetic and copies ran while one was open for 3% of the time, Pallas kernels for 0%

profile of v4, /device:TPU:2, one launch (start us, length us, event | category | flops | bytes accessed | tf_op | source)
XLA Modules:
  0.0 69.7 jit_solution(14717567521496973148)
XLA Ops:
  0.0 2.6 %shard_map.64 = (bf16[1,208,128]{2,1,0:T(8,128)(2,1)}, bf16[208,128]{1,0:T(8,128)(2,1)}) custom-call(bf16[12,64,256]{2,1,0:T(8,128)(2,1)} %bitcast.17, s32[12,64]{1,0:T(8,128)} %bitcast.21, bf16[32,256]{1,0:T(8,128)(2,1)} %bitcast.19, bf16[32,256]{1,0:T(8,128)(2,1)} %bitcast.20, f32[1,128]{1,0:T(1,128)} %bitcast.22), custom_call_target="tpu_custom_call" | custom-call | tf_op jit(solution)/shard_map/pallas_call | solution.py:228
  2.6 10.9 %collective-permute-start.1 = (bf16[1,208,128]{2,1,0:T(8,128)(2,1)}, bf16[1,208,128]{2,1,0:T(8,128)(2,1)S(1)}, u32[]{:S(2)}, u32[]{:S(2)}) collective-permute-start(bf16[1,208,128]{2,1,0:T(8,128)(2,1)} %get-tuple-element.11), channel_id=1, source_target_pairs={{0,4},{1,5},{2,6},{3,7},{4,0},{5,1},{6,2},{7,3},{8,12},{9,13},{10,... | collective-permute-start | bytes 159752 | tf_op jit(solution)/shard_map/ppermute | solution.py:252
  13.5 7.7 %collective-permute-start = (bf16[208,128]{1,0:T(8,128)(2,1)}, bf16[208,128]{1,0:T(8,128)(2,1)S(1)}, u32[]{:S(2)}, u32[]{:S(2)}) collective-permute-start(bf16[208,128]{1,0:T(8,128)(2,1)} %get-tuple-element.10), channel_id=1, source_target_pairs={{0,256},{1,192},{2,352},{3,160},{4,480},{5,32},{6,384},{7,64},{8,2... | collective-permute-start | bytes 159752 | tf_op jit(solution)/shard_map/ppermute | solution.py:249
  21.2 0.0 collective-permute-done.1
  21.2 0.8 %pad_maximum_fusion.1 = bf16[2,208,128]{2,1,0:T(8,128)(2,1)S(1)} fusion(bf16[1,208,128]{2,1,0:T(8,128)(2,1)S(1)} %collective-permute-done.1, bf16[1,208,128]{2,1,0:T(8,128)(2,1)} %get-tuple-element.11), kind=kLoop, calls=%fused_computation.2 | loop fusion | flops 53248 | bytes 212992 | tf_op jit(solution)/shard_map/concatenate | solution.py:252
  22.1 3.5 %collective-permute-start.2 = (bf16[2,208,128]{2,1,0:T(8,128)(2,1)S(1)}, bf16[2,208,128]{2,1,0:T(8,128)(2,1)S(1)}, u32[]{:S(2)}, u32[]{:S(2)}) collective-permute-start(bf16[2,208,128]{2,1,0:T(8,128)(2,1)S(1)} %pad_maximum_fusion.1), channel_id=1, source_target_pairs={{0,2},{1,3},{2,0},{3,1},{4,6},{5,7},{6,4},{7,5},{8,10},{9,11},{10,... | collective-permute-start | bytes 319496 | tf_op jit(solution)/shard_map/ppermute | solution.py:254
  25.6 0.0 collective-permute-done
  25.6 1.0 %broadcast_in_dim.2 = bf16[16,208,128]{2,1,0:T(8,128)(2,1)} broadcast(bf16[208,128]{1,0:T(8,128)(2,1)S(1)} %collective-permute-done), dimensions={1,2} | broadcast | bytes 905216 | tf_op jit(solution)/shard_map/broadcast_in_dim | solution.py:250
  26.6 6.5 %all-to-all-start = ((bf16[16,208,128]{2,1,0:T(8,128)(2,1)}), bf16[16,208,128]{2,1,0:T(8,128)(2,1)S(1)}, u32[]{:S(2)}, u32[]{:S(2)}) async-start(bf16[16,208,128]{2,1,0:T(8,128)(2,1)} %broadcast_in_dim.2), calls=%async_computation | async-start | bytes 1703936 | tf_op jit(solution)/shard_map/all_to_all | solution.py:256
  33.1 0.0 collective-permute-done.2
  33.2 3.4 %collective-permute-start.3 = (bf16[4,208,128]{2,1,0:T(8,128)(2,1)S(1)}, bf16[4,208,128]{2,1,0:T(8,128)(2,1)S(1)}, u32[]{:S(2)}, u32[]{:S(2)}) collective-permute-start(bf16[4,208,128]{2,1,0:T(8,128)(2,1)S(1)} %pad_maximum_fusion), channel_id=1, source_target_pairs={{0,8},{1,9},{2,10},{3,11},{4,12},{5,13},{6,14},{7,15},{8,16},{9,17... | collective-permute-start | bytes 638984 | tf_op jit(solution)/shard_map/ppermute | solution.py:258
  36.6 3.0 %collective-permute-start.4 = (bf16[4,208,128]{2,1,0:T(8,128)(2,1)S(1)}, bf16[4,208,128]{2,1,0:T(8,128)(2,1)S(1)}, u32[]{:S(2)}, u32[]{:S(2)}) collective-permute-start(bf16[4,208,128]{2,1,0:T(8,128)(2,1)S(1)} %pad_maximum_fusion), channel_id=1, source_target_pairs={{0,16},{1,17},{2,18},{3,19},{4,20},{5,21},{6,22},{7,23},{8,24},{9,... | collective-permute-start | bytes 638984 | tf_op jit(solution)/shard_map/ppermute | solution.py:258
  39.6 4.1 %collective-permute-start.5 = (bf16[4,208,128]{2,1,0:T(8,128)(2,1)S(1)}, bf16[4,208,128]{2,1,0:T(8,128)(2,1)S(1)}, u32[]{:S(2)}, u32[]{:S(2)}) collective-permute-start(bf16[4,208,128]{2,1,0:T(8,128)(2,1)S(1)} %pad_maximum_fusion), channel_id=1, source_target_pairs={{0,24},{1,25},{2,26},{3,27},{4,28},{5,29},{6,30},{7,31},{8,0},{9,1... | collective-permute-start | bytes 638984 | tf_op jit(solution)/shard_map/ppermute | solution.py:258
  43.7 0.0 collective-permute-done.3
  43.7 3.1 %collective-permute-done.4 = bf16[4,208,128]{2,1,0:T(8,128)(2,1)S(1)} collective-permute-done((bf16[4,208,128]{2,1,0:T(8,128)(2,1)S(1)}, bf16[4,208,128]{2,1,0:T(8,128)(2,1)S(1)}, u32[]{:S(2)}, u32[]{:S(2)}) %collective-permute-start.4) | collective-permute-done | bytes 213024 | tf_op jit(solution)/shard_map/ppermute | solution.py:258
  46.8 0.0 copy-start
  46.9 2.1 %collective-permute-done.5 = bf16[4,208,128]{2,1,0:T(8,128)(2,1)S(1)} collective-permute-done((bf16[4,208,128]{2,1,0:T(8,128)(2,1)S(1)}, bf16[4,208,128]{2,1,0:T(8,128)(2,1)S(1)}, u32[]{:S(2)}, u32[]{:S(2)}) %collective-permute-start.5) | collective-permute-done | bytes 213024 | tf_op jit(solution)/shard_map/ppermute | solution.py:258
  49.0 1.9 %collective-permute-start.6 = (bf16[16,208,128]{2,1,0:T(8,128)(2,1)S(1)}, bf16[16,208,128]{2,1,0:T(8,128)(2,1)S(1)}, u32[]{:S(2)}, u32[]{:S(2)}) collective-permute-start(bf16[16,208,128]{2,1,0:T(8,128)(2,1)S(1)} %constant_dynamic-update-slice_fusion.lm_ref), channel_id=1, source_target_pairs={{0,1},{1,0},{2,3},{3,2},{4,5},{5,4},{6,7},{7,6},{8,9},{9,8},{10,11... | collective-permute-start | bytes 2555912 | tf_op jit(solution)/shard_map/ppermute | solution.py:260
  51.0 0.0 copy-done
  51.0 0.2 copy.7
  51.3 0.1 pad_add_fusion.at_ref
  51.3 2.0 %collective-permute-done.6.lo_ref = bf16[16,208,128]{2,1,0:T(8,128)(2,1)S(1)} collective-permute-done((bf16[16,208,128]{2,1,0:T(8,128)(2,1)S(1)}, bf16[16,208,128]{2,1,0:T(8,128)(2,1)S(1)}, u32[]{:S(2)}, u32[]{:S(2)}) %collective-permute-start.6) | collective-permute-done | bytes 852000 | tf_op jit(solution)/shard_map/ppermute | solution.py:260
  53.3 1.8 %all-to-all-done.r_ref = bf16[16,208,128]{2,1,0:T(8,128)(2,1)S(1)} async-done(((bf16[16,208,128]{2,1,0:T(8,128)(2,1)}), bf16[16,208,128]{2,1,0:T(8,128)(2,1)S(1)}, u32[]{:S(2)}, u32[]{:S(2)}) %all-to-all-start) | async-done | bytes 852000 | tf_op jit(solution)/shard_map/all_to_all | solution.py:256
  55.1 3.6 %shard_map.65 = (bf16[4,288,128]{2,1,0:T(8,128)(2,1)S(1)}, f32[1,128]{1,0:T(1,128)S(1)}) custom-call(s32[3]{0:T(128)S(1)} %pad_add_fusion.at_ref, bf16[16,208,128]{2,1,0:T(8,128)(2,1)S(1)} %all-to-all-done.r_ref, bf16[512,256]{1,0:T(8,128)(2,1)S(1)} %bitcast.15, bf16[16,208,128]{2,1,0:T(8,128)(2,1)S(1)} %constant_dynamic-update-slice_fusion.lm_ref, ...), custom_call_target="tpu_custom_call" | custom-call | flops 3221225472 | bytes 4194304 | tf_op jit(solution)/shard_map/pallas_call | solution.py:262
  58.8 10.0 %all_to_all.10.pair_ref = bf16[4,288,128]{2,1,0:T(8,128)(2,1)S(1)} all-to-all(bf16[4,288,128]{2,1,0:T(8,128)(2,1)S(1)} %get-tuple-element.13), channel_id=1, replica_groups=mesh['y'=8,'zl'=2,'x'=4,'zh'=4,'core'=2] {'x'}, dimensions={0} | all-to-all | bytes 589824 | tf_op jit(solution)/shard_map/all_to_all | solution.py:275
  68.8 0.9 %shard_map.66 = f32[12,96,128]{2,1,0:T(8,128)} custom-call(bf16[4,288,128]{2,1,0:T(8,128)(2,1)S(1)} %all_to_all.10.pair_ref, f32[1,128]{1,0:T(1,128)S(1)} %get-tuple-element.14.offset_ref), custom_call_target="tpu_custom_call" | custom-call | tf_op jit(solution)/shard_map/pallas_call | solution.py:276
  (6 shorter events, 0.2 us)
Async XLA Ops:
  2.6 18.7 %collective-permute-start.1 = (bf16[1,208,128]{2,1,0:T(8,128)(2,1)}, bf16[1,208,128]{2,1,0:T(8,128)(2,1)S(1)}, u32[]{:S(2)}, u32[]{:S(2)}) collective-permute-start(bf16[1,208,128]{2,1,0:T(8,128)(2,1)} %get-tuple-element.11), channel_id=1, source_target_pairs={{0,4},{1,5},{2,6},{3,7},{4,0},{5,1},{6,2},{7,3},{8,12},{9,13},{10,... | collective-permute-start | bytes 159752 | tf_op jit(solution)/shard_map/ppermute | solution.py:252
  13.5 12.1 %collective-permute-start = (bf16[208,128]{1,0:T(8,128)(2,1)}, bf16[208,128]{1,0:T(8,128)(2,1)S(1)}, u32[]{:S(2)}, u32[]{:S(2)}) collective-permute-start(bf16[208,128]{1,0:T(8,128)(2,1)} %get-tuple-element.10), channel_id=1, source_target_pairs={{0,256},{1,192},{2,352},{3,160},{4,480},{5,32},{6,384},{7,64},{8,2... | collective-permute-start | bytes 159752 | tf_op jit(solution)/shard_map/ppermute | solution.py:249
  22.1 11.1 %collective-permute-start.2 = (bf16[2,208,128]{2,1,0:T(8,128)(2,1)S(1)}, bf16[2,208,128]{2,1,0:T(8,128)(2,1)S(1)}, u32[]{:S(2)}, u32[]{:S(2)}) collective-permute-start(bf16[2,208,128]{2,1,0:T(8,128)(2,1)S(1)} %pad_maximum_fusion.1), channel_id=1, source_target_pairs={{0,2},{1,3},{2,0},{3,1},{4,6},{5,7},{6,4},{7,5},{8,10},{9,11},{10,... | collective-permute-start | bytes 319496 | tf_op jit(solution)/shard_map/ppermute | solution.py:254
  26.6 28.5 %all-to-all-start = ((bf16[16,208,128]{2,1,0:T(8,128)(2,1)}), bf16[16,208,128]{2,1,0:T(8,128)(2,1)S(1)}, u32[]{:S(2)}, u32[]{:S(2)}) async-start(bf16[16,208,128]{2,1,0:T(8,128)(2,1)} %broadcast_in_dim.2), calls=%async_computation | async-start | bytes 1703936 | tf_op jit(solution)/shard_map/all_to_all | solution.py:256
  33.2 10.5 %collective-permute-start.3 = (bf16[4,208,128]{2,1,0:T(8,128)(2,1)S(1)}, bf16[4,208,128]{2,1,0:T(8,128)(2,1)S(1)}, u32[]{:S(2)}, u32[]{:S(2)}) collective-permute-start(bf16[4,208,128]{2,1,0:T(8,128)(2,1)S(1)} %pad_maximum_fusion), channel_id=1, source_target_pairs={{0,8},{1,9},{2,10},{3,11},{4,12},{5,13},{6,14},{7,15},{8,16},{9,17... | collective-permute-start | bytes 638984 | tf_op jit(solution)/shard_map/ppermute | solution.py:258
  36.6 10.2 %collective-permute-start.4 = (bf16[4,208,128]{2,1,0:T(8,128)(2,1)S(1)}, bf16[4,208,128]{2,1,0:T(8,128)(2,1)S(1)}, u32[]{:S(2)}, u32[]{:S(2)}) collective-permute-start(bf16[4,208,128]{2,1,0:T(8,128)(2,1)S(1)} %pad_maximum_fusion), channel_id=1, source_target_pairs={{0,16},{1,17},{2,18},{3,19},{4,20},{5,21},{6,22},{7,23},{8,24},{9,... | collective-permute-start | bytes 638984 | tf_op jit(solution)/shard_map/ppermute | solution.py:258
  39.6 9.4 %collective-permute-start.5 = (bf16[4,208,128]{2,1,0:T(8,128)(2,1)S(1)}, bf16[4,208,128]{2,1,0:T(8,128)(2,1)S(1)}, u32[]{:S(2)}, u32[]{:S(2)}) collective-permute-start(bf16[4,208,128]{2,1,0:T(8,128)(2,1)S(1)} %pad_maximum_fusion), channel_id=1, source_target_pairs={{0,24},{1,25},{2,26},{3,27},{4,28},{5,29},{6,30},{7,31},{8,0},{9,1... | collective-permute-start | bytes 638984 | tf_op jit(solution)/shard_map/ppermute | solution.py:258
  46.8 4.1 %copy-start = (bf16[1024,128]{1,0:T(8,128)(2,1)S(1)}, bf16[1024,128]{1,0:T(8,128)(2,1)}, u32[]{:S(2)}) copy-start(bf16[1024,128]{1,0:T(8,128)(2,1)} %param.10) | copy-start | bytes 786436
  49.0 4.3 %collective-permute-start.6 = (bf16[16,208,128]{2,1,0:T(8,128)(2,1)S(1)}, bf16[16,208,128]{2,1,0:T(8,128)(2,1)S(1)}, u32[]{:S(2)}, u32[]{:S(2)}) collective-permute-start(bf16[16,208,128]{2,1,0:T(8,128)(2,1)S(1)} %constant_dynamic-update-slice_fusion.lm_ref), channel_id=1, source_target_pairs={{0,1},{1,0},{2,3},{3,2},{4,5},{5,4},{6,7},{7,6},{8,9},{9,8},{10,11... | collective-permute-start | bytes 2555912 | tf_op jit(solution)/shard_map/ppermute | solution.py:260

commit v5 on v4

--- a/solution.py
+++ b/solution.py
@@ -210,6 +210,10 @@
     )
 
 
+def stay(value):
+    return pltpu.with_memory_space_constraint(value, pltpu.HBM)
+
+
 def call(kernel, out_shape, in_specs, scratch_shapes=(), vmem=48, flops=0, bytes_accessed=0):
     return pl.pallas_call(
         kernel,
@@ -241,8 +245,7 @@
             pltpu.VMEM((192, 128), F32),
             pltpu.SemaphoreType.DMA((5,)),
         ],
-        vmem=60,
-    )(x.transpose(1, 0, 2), m.T, wl.T, wr.T, offset.reshape(1, PAIR))
+    )(*map(stay, (x.transpose(1, 0, 2), m.T, wl.T, wr.T, offset.reshape(1, PAIR))))
     w2 = w.reshape(WIDTH, 16, 2, PAIR).transpose(1, 0, 2, 3).reshape(512, 2 * PAIR)
     at = jnp.stack([lax.axis_index(name) for name in ("zh", "core", "x")]).astype(jnp.int32)
 
@@ -254,9 +257,8 @@
     left = jnp.concatenate([left, lax.ppermute(left, AXES, ACROSS_ZH[1])])
     left = lax.optimization_barrier((left, right))[0]
     right = lax.all_to_all(right, ("y", "zl"), 0, 0, tiled=True)
-    left = jnp.concatenate(
-        [left] + [lax.ppermute(left, AXES, ALONG_X[k]) for k in (1, 2, 3)], axis=0
-    )
+    along = {k: lax.ppermute(left, AXES, ALONG_X[k]) for k in (2, 3, 1)}
+    left = jnp.concatenate([left, along[1], along[2], along[3]], axis=0)
     left_other = lax.ppermute(left, AXES, OTHER_CORE)
 
     pairs, offset = call(

time: 70.1 us -> 69.1 us (0.986)
  other arithmetic: 0.92 us -> 0.12 us
    concatenate x1, other arithmetic: 0.82 us -> 0.01 us  [local(): jnp.concatenate([left, lax.ppermute(left, AXES, ACROSS_ZH[2])])]
  transfers between devices with their start and end apart: 8 -> 8, of which waited for: 4 -> 4; matrix products, arithmetic and copies ran while one was open for 3% -> 2% of each run, Pallas kernels for 0% -> 0%
where the time goes in v5:
time: 69.1 us; the launch traced here: 68.6 us
  starting transfers between devices  41.3 us (60%)
  blocking collectives  10 us (14%)
  waiting for transfers between devices  9.14 us (13%)
  Pallas kernels  6.45 us (9%)
  local copies, waits for them, and re-layouts  1.42 us (2%)
    ppermute x1, starting transfers between devices, local(): lax.ppermute(left, AXES, ACROSS_ZH[2])  10.9 us
    ppermute x3, starting transfers between devices, local(): along = {k: lax.ppermute(left, AXES, ALONG_X[k]) for k in (2, 3, 1)}  10.5 us
    all_to_all x1, blocking collectives, local(): pairs = lax.all_to_all(pairs, 'x', 0, 0, tiled=True)  10 us
    ppermute x1, starting transfers between devices, local(): right = lax.ppermute(right, AXES, TRANSPOSE)  7.74 us
    all_to_all x1, starting transfers between devices, local(): right = lax.all_to_all(right, ('y', 'zl'), 0, 0, tiled=True)  6.77 us
    ppermute x3, waiting for transfers between devices, local(): along = {k: lax.ppermute(left, AXES, ALONG_X[k]) for k in (2, 3, 1)}  5.54 us
    pallas_call x1, Pallas kernels, local(): call(pair_kernel, [jax.ShapeDtypeStruct((4, 288, 128), BF16), jax.ShapeDt...  3.65 us
    ppermute x1, starting transfers between devices, local(): left = jnp.concatenate([left, lax.ppermute(left, AXES, ACROSS_ZH[1])])  3.49 us
  transfers between devices with their start and end apart: 8, of which 4 were waited for; matrix products, arithmetic and copies ran while one was open for 2% of the time, Pallas kernels for 0%

profile of v5, /device:TPU:2, one launch (start us, length us, event | category | flops | bytes accessed | tf_op | source)
XLA Modules:
  0.0 68.6 jit_solution(16780741117674217658)
XLA Ops:
  0.0 1.9 %shard_map.64 = (bf16[1,208,128]{2,1,0:T(8,128)(2,1)S(1)}, bf16[208,128]{1,0:T(8,128)(2,1)S(1)}) custom-call(bf16[12,64,256]{2,1,0:T(8,128)(2,1)} %bitcast.17, s32[12,64]{1,0:T(8,128)} %bitcast.21, bf16[32,256]{1,0:T(8,128)(2,1)} %bitcast.19, bf16[32,256]{1,0:T(8,128)(2,1)} %bitcast.20, f32[1,128]{1,0:T(1,128)} %bitcast.22), custom_call_target="tpu_custom_call" | custom-call | tf_op jit(solution)/shard_map/pallas_call | solution.py:232
  2.0 10.9 %collective-permute-start.1 = (bf16[1,208,128]{2,1,0:T(8,128)(2,1)S(1)}, bf16[1,208,128]{2,1,0:T(8,128)(2,1)S(1)}, u32[]{:S(2)}, u32[]{:S(2)}) collective-permute-start(bf16[1,208,128]{2,1,0:T(8,128)(2,1)S(1)} %get-tuple-element.11), channel_id=1, source_target_pairs={{0,4},{1,5},{2,6},{3,7},{4,0},{5,1},{6,2},{7,3},{8,12},{9,13},{10,... | collective-permute-start | bytes 159752 | tf_op jit(solution)/shard_map/ppermute | solution.py:255
  12.9 7.7 %collective-permute-start = (bf16[208,128]{1,0:T(8,128)(2,1)S(1)}, bf16[208,128]{1,0:T(8,128)(2,1)S(1)}, u32[]{:S(2)}, u32[]{:S(2)}) collective-permute-start(bf16[208,128]{1,0:T(8,128)(2,1)S(1)} %get-tuple-element.10), channel_id=1, source_target_pairs={{0,256},{1,192},{2,352},{3,160},{4,480},{5,32},{6,384},{7,64},{8,2... | collective-permute-start | bytes 159752 | tf_op jit(solution)/shard_map/ppermute | solution.py:252
  20.6 0.0 collective-permute-done.1
  20.7 3.5 %collective-permute-start.2 = (bf16[2,208,128]{2,1,0:T(8,128)(2,1)S(1)}, bf16[2,208,128]{2,1,0:T(8,128)(2,1)S(1)}, u32[]{:S(2)}, u32[]{:S(2)}) collective-permute-start(bf16[2,208,128]{2,1,0:T(8,128)(2,1)S(1)} %pad_maximum_fusion.1), channel_id=1, source_target_pairs={{0,2},{1,3},{2,0},{3,1},{4,6},{5,7},{6,4},{7,5},{8,10},{9,11},{10,... | collective-permute-start | bytes 319496 | tf_op jit(solution)/shard_map/ppermute | solution.py:257
  24.2 0.0 collective-permute-done
  24.2 1.0 %broadcast_in_dim.2 = bf16[16,208,128]{2,1,0:T(8,128)(2,1)} broadcast(bf16[208,128]{1,0:T(8,128)(2,1)S(1)} %collective-permute-done), dimensions={1,2} | broadcast | bytes 905216 | tf_op jit(solution)/shard_map/broadcast_in_dim | solution.py:253
  25.2 6.8 %all-to-all-start = ((bf16[16,208,128]{2,1,0:T(8,128)(2,1)}), bf16[16,208,128]{2,1,0:T(8,128)(2,1)S(1)}, u32[]{:S(2)}, u32[]{:S(2)}) async-start(bf16[16,208,128]{2,1,0:T(8,128)(2,1)} %broadcast_in_dim.2), calls=%async_computation | async-start | bytes 1703936 | tf_op jit(solution)/shard_map/all_to_all | solution.py:259
  32.0 0.0 collective-permute-done.2
  32.0 3.4 %collective-permute-start.3 = (bf16[4,208,128]{2,1,0:T(8,128)(2,1)S(1)}, bf16[4,208,128]{2,1,0:T(8,128)(2,1)S(1)}, u32[]{:S(2)}, u32[]{:S(2)}) collective-permute-start(bf16[4,208,128]{2,1,0:T(8,128)(2,1)S(1)} %pad_maximum_fusion), channel_id=1, source_target_pairs={{0,8},{1,9},{2,10},{3,11},{4,12},{5,13},{6,14},{7,15},{8,16},{9,17... | collective-permute-start | bytes 638984 | tf_op jit(solution)/shard_map/ppermute | solution.py:260
  35.4 3.0 %collective-permute-start.4 = (bf16[4,208,128]{2,1,0:T(8,128)(2,1)S(1)}, bf16[4,208,128]{2,1,0:T(8,128)(2,1)S(1)}, u32[]{:S(2)}, u32[]{:S(2)}) collective-permute-start(bf16[4,208,128]{2,1,0:T(8,128)(2,1)S(1)} %pad_maximum_fusion), channel_id=1, source_target_pairs={{0,16},{1,17},{2,18},{3,19},{4,20},{5,21},{6,22},{7,23},{8,24},{9,... | collective-permute-start | bytes 638984 | tf_op jit(solution)/shard_map/ppermute | solution.py:260
  38.5 4.1 %collective-permute-start.5 = (bf16[4,208,128]{2,1,0:T(8,128)(2,1)S(1)}, bf16[4,208,128]{2,1,0:T(8,128)(2,1)S(1)}, u32[]{:S(2)}, u32[]{:S(2)}) collective-permute-start(bf16[4,208,128]{2,1,0:T(8,128)(2,1)S(1)} %pad_maximum_fusion), channel_id=1, source_target_pairs={{0,24},{1,25},{2,26},{3,27},{4,28},{5,29},{6,30},{7,31},{8,0},{9,1... | collective-permute-start | bytes 638984 | tf_op jit(solution)/shard_map/ppermute | solution.py:260
  42.5 0.0 collective-permute-done.3
  42.6 3.4 %collective-permute-done.4 = bf16[4,208,128]{2,1,0:T(8,128)(2,1)S(1)} collective-permute-done((bf16[4,208,128]{2,1,0:T(8,128)(2,1)S(1)}, bf16[4,208,128]{2,1,0:T(8,128)(2,1)S(1)}, u32[]{:S(2)}, u32[]{:S(2)}) %collective-permute-start.4) | collective-permute-done | bytes 213024 | tf_op jit(solution)/shard_map/ppermute | solution.py:260
  46.0 0.0 copy-start
  46.0 2.1 %collective-permute-done.5 = bf16[4,208,128]{2,1,0:T(8,128)(2,1)S(1)} collective-permute-done((bf16[4,208,128]{2,1,0:T(8,128)(2,1)S(1)}, bf16[4,208,128]{2,1,0:T(8,128)(2,1)S(1)}, u32[]{:S(2)}, u32[]{:S(2)}) %collective-permute-start.5) | collective-permute-done | bytes 213024 | tf_op jit(solution)/shard_map/ppermute | solution.py:260
  48.2 1.9 %collective-permute-start.6 = (bf16[16,208,128]{2,1,0:T(8,128)(2,1)S(1)}, bf16[16,208,128]{2,1,0:T(8,128)(2,1)S(1)}, u32[]{:S(2)}, u32[]{:S(2)}) collective-permute-start(bf16[16,208,128]{2,1,0:T(8,128)(2,1)S(1)} %constant_dynamic-update-slice_fusion.lm_ref), channel_id=1, source_target_pairs={{0,1},{1,0},{2,3},{3,2},{4,5},{5,4},{6,7},{7,6},{8,9},{9,8},{10,11... | collective-permute-start | bytes 2555912 | tf_op jit(solution)/shard_map/ppermute | solution.py:262
  50.1 0.0 copy-done
  50.2 0.2 copy.7
  50.4 0.1 pad_add_fusion.at_ref
  50.5 2.0 %collective-permute-done.6.lo_ref = bf16[16,208,128]{2,1,0:T(8,128)(2,1)S(1)} collective-permute-done((bf16[16,208,128]{2,1,0:T(8,128)(2,1)S(1)}, bf16[16,208,128]{2,1,0:T(8,128)(2,1)S(1)}, u32[]{:S(2)}, u32[]{:S(2)}) %collective-permute-start.6) | collective-permute-done | bytes 852000 | tf_op jit(solution)/shard_map/ppermute | solution.py:262
  52.5 1.6 %all-to-all-done.r_ref = bf16[16,208,128]{2,1,0:T(8,128)(2,1)S(1)} async-done(((bf16[16,208,128]{2,1,0:T(8,128)(2,1)}), bf16[16,208,128]{2,1,0:T(8,128)(2,1)S(1)}, u32[]{:S(2)}, u32[]{:S(2)}) %all-to-all-start) | async-done | bytes 852000 | tf_op jit(solution)/shard_map/all_to_all | solution.py:259
  54.1 3.6 %shard_map.65 = (bf16[4,288,128]{2,1,0:T(8,128)(2,1)S(1)}, f32[1,128]{1,0:T(1,128)S(1)}) custom-call(s32[3]{0:T(128)S(1)} %pad_add_fusion.at_ref, bf16[16,208,128]{2,1,0:T(8,128)(2,1)S(1)} %all-to-all-done.r_ref, bf16[512,256]{1,0:T(8,128)(2,1)S(1)} %bitcast.15, bf16[16,208,128]{2,1,0:T(8,128)(2,1)S(1)} %constant_dynamic-update-slice_fusion.lm_ref, ...), custom_call_target="tpu_custom_call" | custom-call | flops 3221225472 | bytes 4194304 | tf_op jit(solution)/shard_map/pallas_call | solution.py:264
  57.8 10.0 %all_to_all.10.pair_ref = bf16[4,288,128]{2,1,0:T(8,128)(2,1)S(1)} all-to-all(bf16[4,288,128]{2,1,0:T(8,128)(2,1)S(1)} %get-tuple-element.13), channel_id=1, replica_groups=mesh['y'=8,'zl'=2,'x'=4,'zh'=4,'core'=2] {'x'}, dimensions={0} | all-to-all | bytes 589824 | tf_op jit(solution)/shard_map/all_to_all | solution.py:277
  67.8 0.9 %shard_map.66 = f32[12,96,128]{2,1,0:T(8,128)} custom-call(bf16[4,288,128]{2,1,0:T(8,128)(2,1)S(1)} %all_to_all.10.pair_ref, f32[1,128]{1,0:T(1,128)S(1)} %get-tuple-element.14.offset_ref), custom_call_target="tpu_custom_call" | custom-call | tf_op jit(solution)/shard_map/pallas_call | solution.py:278
  (7 shorter events, 0.2 us)
Async XLA Ops:
  2.0 18.7 %collective-permute-start.1 = (bf16[1,208,128]{2,1,0:T(8,128)(2,1)S(1)}, bf16[1,208,128]{2,1,0:T(8,128)(2,1)S(1)}, u32[]{:S(2)}, u32[]{:S(2)}) collective-permute-start(bf16[1,208,128]{2,1,0:T(8,128)(2,1)S(1)} %get-tuple-element.11), channel_id=1, source_target_pairs={{0,4},{1,5},{2,6},{3,7},{4,0},{5,1},{6,2},{7,3},{8,12},{9,13},{10,... | collective-permute-start | bytes 159752 | tf_op jit(solution)/shard_map/ppermute | solution.py:255
  12.9 11.3 %collective-permute-start = (bf16[208,128]{1,0:T(8,128)(2,1)S(1)}, bf16[208,128]{1,0:T(8,128)(2,1)S(1)}, u32[]{:S(2)}, u32[]{:S(2)}) collective-permute-start(bf16[208,128]{1,0:T(8,128)(2,1)S(1)} %get-tuple-element.10), channel_id=1, source_target_pairs={{0,256},{1,192},{2,352},{3,160},{4,480},{5,32},{6,384},{7,64},{8,2... | collective-permute-start | bytes 159752 | tf_op jit(solution)/shard_map/ppermute | solution.py:252
  20.7 11.3 %collective-permute-start.2 = (bf16[2,208,128]{2,1,0:T(8,128)(2,1)S(1)}, bf16[2,208,128]{2,1,0:T(8,128)(2,1)S(1)}, u32[]{:S(2)}, u32[]{:S(2)}) collective-permute-start(bf16[2,208,128]{2,1,0:T(8,128)(2,1)S(1)} %pad_maximum_fusion.1), channel_id=1, source_target_pairs={{0,2},{1,3},{2,0},{3,1},{4,6},{5,7},{6,4},{7,5},{8,10},{9,11},{10,... | collective-permute-start | bytes 319496 | tf_op jit(solution)/shard_map/ppermute | solution.py:257
  25.2 28.9 %all-to-all-start = ((bf16[16,208,128]{2,1,0:T(8,128)(2,1)}), bf16[16,208,128]{2,1,0:T(8,128)(2,1)S(1)}, u32[]{:S(2)}, u32[]{:S(2)}) async-start(bf16[16,208,128]{2,1,0:T(8,128)(2,1)} %broadcast_in_dim.2), calls=%async_computation | async-start | bytes 1703936 | tf_op jit(solution)/shard_map/all_to_all | solution.py:259
  32.0 10.5 %collective-permute-start.3 = (bf16[4,208,128]{2,1,0:T(8,128)(2,1)S(1)}, bf16[4,208,128]{2,1,0:T(8,128)(2,1)S(1)}, u32[]{:S(2)}, u32[]{:S(2)}) collective-permute-start(bf16[4,208,128]{2,1,0:T(8,128)(2,1)S(1)} %pad_maximum_fusion), channel_id=1, source_target_pairs={{0,8},{1,9},{2,10},{3,11},{4,12},{5,13},{6,14},{7,15},{8,16},{9,17... | collective-permute-start | bytes 638984 | tf_op jit(solution)/shard_map/ppermute | solution.py:260
  35.4 10.6 %collective-permute-start.4 = (bf16[4,208,128]{2,1,0:T(8,128)(2,1)S(1)}, bf16[4,208,128]{2,1,0:T(8,128)(2,1)S(1)}, u32[]{:S(2)}, u32[]{:S(2)}) collective-permute-start(bf16[4,208,128]{2,1,0:T(8,128)(2,1)S(1)} %pad_maximum_fusion), channel_id=1, source_target_pairs={{0,16},{1,17},{2,18},{3,19},{4,20},{5,21},{6,22},{7,23},{8,24},{9,... | collective-permute-start | bytes 638984 | tf_op jit(solution)/shard_map/ppermute | solution.py:260
  38.5 9.7 %collective-permute-start.5 = (bf16[4,208,128]{2,1,0:T(8,128)(2,1)S(1)}, bf16[4,208,128]{2,1,0:T(8,128)(2,1)S(1)}, u32[]{:S(2)}, u32[]{:S(2)}) collective-permute-start(bf16[4,208,128]{2,1,0:T(8,128)(2,1)S(1)} %pad_maximum_fusion), channel_id=1, source_target_pairs={{0,24},{1,25},{2,26},{3,27},{4,28},{5,29},{6,30},{7,31},{8,0},{9,1... | collective-permute-start | bytes 638984 | tf_op jit(solution)/shard_map/ppermute | solution.py:260
  46.0 4.1 %copy-start = (bf16[1024,128]{1,0:T(8,128)(2,1)S(1)}, bf16[1024,128]{1,0:T(8,128)(2,1)}, u32[]{:S(2)}) copy-start(bf16[1024,128]{1,0:T(8,128)(2,1)} %param.10) | copy-start | bytes 786436
  48.2 4.3 %collective-permute-start.6 = (bf16[16,208,128]{2,1,0:T(8,128)(2,1)S(1)}, bf16[16,208,128]{2,1,0:T(8,128)(2,1)S(1)}, u32[]{:S(2)}, u32[]{:S(2)}) collective-permute-start(bf16[16,208,128]{2,1,0:T(8,128)(2,1)S(1)} %constant_dynamic-update-slice_fusion.lm_ref), channel_id=1, source_target_pairs={{0,1},{1,0},{2,3},{3,2},{4,5},{5,4},{6,7},{7,6},{8,9},{9,8},{10,11... | collective-permute-start | bytes 2555912 | tf_op jit(solution)/shard_map/ppermute | solution.py:262

commit v6 on v5

--- a/solution.py
+++ b/solution.py
@@ -157,10 +157,10 @@
                         .astype(BF16)
                         for e in range(4 * q, 4 * q + 4)
                     ]
-                    a0 = jnp.where(half, a[0], pltpu.roll(a[2], 64, 1))
-                    a1 = jnp.where(half, a[1], pltpu.roll(a[3], 64, 1))
-                    a2 = jnp.where(half, pltpu.roll(a[0], 64, 1), a[2])
-                    a3 = jnp.where(half, pltpu.roll(a[1], 64, 1), a[3])
+                    r02 = pltpu.roll(jnp.where(half, a[2], a[0]), 64, 1)
+                    r13 = pltpu.roll(jnp.where(half, a[3], a[1]), 64, 1)
+                    a0, a2 = jnp.where(half, a[0], r02), jnp.where(half, r02, a[2])
+                    a1, a3 = jnp.where(half, a[1], r13), jnp.where(half, r13, a[3])
                     quads[0].append(jnp.where(even, a0, pltpu.roll(a1, 32, 1)))
                     quads[1].append(jnp.where(even, pltpu.roll(a0, 96, 1), a1))
                     quads[2].append(jnp.where(even, a2, pltpu.roll(a3, 32, 1)))

time: 69.1 us -> 68.9 us (level)
  no operation moved by 1% of the time
where the time goes in v6:
time: 68.9 us; the launch traced here: 68.5 us
  starting transfers between devices  41.3 us (60%)
  blocking collectives  10 us (15%)
  waiting for transfers between devices  9.14 us (13%)
  Pallas kernels  6.28 us (9%)
  local copies, waits for them, and re-layouts  1.42 us (2%)
    ppermute x1, starting transfers between devices, local(): lax.ppermute(left, AXES, ACROSS_ZH[2])  10.9 us
    ppermute x3, starting transfers between devices, local(): along = {k: lax.ppermute(left, AXES, ALONG_X[k]) for k in (2, 3, 1)}  10.5 us
    all_to_all x1, blocking collectives, local(): pairs = lax.all_to_all(pairs, 'x', 0, 0, tiled=True)  10 us
    ppermute x1, starting transfers between devices, local(): right = lax.ppermute(right, AXES, TRANSPOSE)  7.74 us
    all_to_all x1, starting transfers between devices, local(): right = lax.all_to_all(right, ('y', 'zl'), 0, 0, tiled=True)  6.77 us
    ppermute x3, waiting for transfers between devices, local(): along = {k: lax.ppermute(left, AXES, ALONG_X[k]) for k in (2, 3, 1)}  5.54 us
    ppermute x1, starting transfers between devices, local(): left = jnp.concatenate([left, lax.ppermute(left, AXES, ACROSS_ZH[1])])  3.49 us
    pallas_call x1, Pallas kernels, local(): call(pair_kernel, [jax.ShapeDtypeStruct((4, 288, 128), BF16), jax.ShapeDt...  3.48 us
  transfers between devices with their start and end apart: 8, of which 4 were waited for; matrix products, arithmetic and copies ran while one was open for 2% of the time, Pallas kernels for 0%

profile of v6, /device:TPU:2, one launch (start us, length us, event | category | flops | bytes accessed | tf_op | source)
XLA Modules:
  0.0 68.5 jit_solution(1414951104775805164)
XLA Ops:
  0.0 1.9 %shard_map.64 = (bf16[1,208,128]{2,1,0:T(8,128)(2,1)S(1)}, bf16[208,128]{1,0:T(8,128)(2,1)S(1)}) custom-call(bf16[12,64,256]{2,1,0:T(8,128)(2,1)} %bitcast.17, s32[12,64]{1,0:T(8,128)} %bitcast.21, bf16[32,256]{1,0:T(8,128)(2,1)} %bitcast.19, bf16[32,256]{1,0:T(8,128)(2,1)} %bitcast.20, f32[1,128]{1,0:T(1,128)} %bitcast.22), custom_call_target="tpu_custom_call" | custom-call | tf_op jit(solution)/shard_map/pallas_call | solution.py:232
  2.0 10.9 %collective-permute-start.1 = (bf16[1,208,128]{2,1,0:T(8,128)(2,1)S(1)}, bf16[1,208,128]{2,1,0:T(8,128)(2,1)S(1)}, u32[]{:S(2)}, u32[]{:S(2)}) collective-permute-start(bf16[1,208,128]{2,1,0:T(8,128)(2,1)S(1)} %get-tuple-element.11), channel_id=1, source_target_pairs={{0,4},{1,5},{2,6},{3,7},{4,0},{5,1},{6,2},{7,3},{8,12},{9,13},{10,... | collective-permute-start | bytes 159752 | tf_op jit(solution)/shard_map/ppermute | solution.py:255
  12.9 7.7 %collective-permute-start = (bf16[208,128]{1,0:T(8,128)(2,1)S(1)}, bf16[208,128]{1,0:T(8,128)(2,1)S(1)}, u32[]{:S(2)}, u32[]{:S(2)}) collective-permute-start(bf16[208,128]{1,0:T(8,128)(2,1)S(1)} %get-tuple-element.10), channel_id=1, source_target_pairs={{0,256},{1,192},{2,352},{3,160},{4,480},{5,32},{6,384},{7,64},{8,2... | collective-permute-start | bytes 159752 | tf_op jit(solution)/shard_map/ppermute | solution.py:252
  20.6 0.0 collective-permute-done.1
  20.7 3.5 %collective-permute-start.2 = (bf16[2,208,128]{2,1,0:T(8,128)(2,1)S(1)}, bf16[2,208,128]{2,1,0:T(8,128)(2,1)S(1)}, u32[]{:S(2)}, u32[]{:S(2)}) collective-permute-start(bf16[2,208,128]{2,1,0:T(8,128)(2,1)S(1)} %pad_maximum_fusion.1), channel_id=1, source_target_pairs={{0,2},{1,3},{2,0},{3,1},{4,6},{5,7},{6,4},{7,5},{8,10},{9,11},{10,... | collective-permute-start | bytes 319496 | tf_op jit(solution)/shard_map/ppermute | solution.py:257
  24.2 0.0 collective-permute-done
  24.2 1.0 %broadcast_in_dim.2 = bf16[16,208,128]{2,1,0:T(8,128)(2,1)} broadcast(bf16[208,128]{1,0:T(8,128)(2,1)S(1)} %collective-permute-done), dimensions={1,2} | broadcast | bytes 905216 | tf_op jit(solution)/shard_map/broadcast_in_dim | solution.py:253
  25.2 6.8 %all-to-all-start = ((bf16[16,208,128]{2,1,0:T(8,128)(2,1)}), bf16[16,208,128]{2,1,0:T(8,128)(2,1)S(1)}, u32[]{:S(2)}, u32[]{:S(2)}) async-start(bf16[16,208,128]{2,1,0:T(8,128)(2,1)} %broadcast_in_dim.2), calls=%async_computation | async-start | bytes 1703936 | tf_op jit(solution)/shard_map/all_to_all | solution.py:259
  32.0 0.0 collective-permute-done.2
  32.0 3.4 %collective-permute-start.3 = (bf16[4,208,128]{2,1,0:T(8,128)(2,1)S(1)}, bf16[4,208,128]{2,1,0:T(8,128)(2,1)S(1)}, u32[]{:S(2)}, u32[]{:S(2)}) collective-permute-start(bf16[4,208,128]{2,1,0:T(8,128)(2,1)S(1)} %pad_maximum_fusion), channel_id=1, source_target_pairs={{0,8},{1,9},{2,10},{3,11},{4,12},{5,13},{6,14},{7,15},{8,16},{9,17... | collective-permute-start | bytes 638984 | tf_op jit(solution)/shard_map/ppermute | solution.py:260
  35.4 3.0 %collective-permute-start.4 = (bf16[4,208,128]{2,1,0:T(8,128)(2,1)S(1)}, bf16[4,208,128]{2,1,0:T(8,128)(2,1)S(1)}, u32[]{:S(2)}, u32[]{:S(2)}) collective-permute-start(bf16[4,208,128]{2,1,0:T(8,128)(2,1)S(1)} %pad_maximum_fusion), channel_id=1, source_target_pairs={{0,16},{1,17},{2,18},{3,19},{4,20},{5,21},{6,22},{7,23},{8,24},{9,... | collective-permute-start | bytes 638984 | tf_op jit(solution)/shard_map/ppermute | solution.py:260
  38.5 4.1 %collective-permute-start.5 = (bf16[4,208,128]{2,1,0:T(8,128)(2,1)S(1)}, bf16[4,208,128]{2,1,0:T(8,128)(2,1)S(1)}, u32[]{:S(2)}, u32[]{:S(2)}) collective-permute-start(bf16[4,208,128]{2,1,0:T(8,128)(2,1)S(1)} %pad_maximum_fusion), channel_id=1, source_target_pairs={{0,24},{1,25},{2,26},{3,27},{4,28},{5,29},{6,30},{7,31},{8,0},{9,1... | collective-permute-start | bytes 638984 | tf_op jit(solution)/shard_map/ppermute | solution.py:260
  42.5 0.0 collective-permute-done.3
  42.6 3.4 %collective-permute-done.4 = bf16[4,208,128]{2,1,0:T(8,128)(2,1)S(1)} collective-permute-done((bf16[4,208,128]{2,1,0:T(8,128)(2,1)S(1)}, bf16[4,208,128]{2,1,0:T(8,128)(2,1)S(1)}, u32[]{:S(2)}, u32[]{:S(2)}) %collective-permute-start.4) | collective-permute-done | bytes 213024 | tf_op jit(solution)/shard_map/ppermute | solution.py:260
  46.0 0.0 copy-start
  46.0 2.1 %collective-permute-done.5 = bf16[4,208,128]{2,1,0:T(8,128)(2,1)S(1)} collective-permute-done((bf16[4,208,128]{2,1,0:T(8,128)(2,1)S(1)}, bf16[4,208,128]{2,1,0:T(8,128)(2,1)S(1)}, u32[]{:S(2)}, u32[]{:S(2)}) %collective-permute-start.5) | collective-permute-done | bytes 213024 | tf_op jit(solution)/shard_map/ppermute | solution.py:260
  48.2 1.9 %collective-permute-start.6 = (bf16[16,208,128]{2,1,0:T(8,128)(2,1)S(1)}, bf16[16,208,128]{2,1,0:T(8,128)(2,1)S(1)}, u32[]{:S(2)}, u32[]{:S(2)}) collective-permute-start(bf16[16,208,128]{2,1,0:T(8,128)(2,1)S(1)} %constant_dynamic-update-slice_fusion.lm_ref), channel_id=1, source_target_pairs={{0,1},{1,0},{2,3},{3,2},{4,5},{5,4},{6,7},{7,6},{8,9},{9,8},{10,11... | collective-permute-start | bytes 2555912 | tf_op jit(solution)/shard_map/ppermute | solution.py:262
  50.1 0.0 copy-done
  50.2 0.2 copy.7
  50.4 0.1 pad_add_fusion.at_ref
  50.5 2.0 %collective-permute-done.6.lo_ref = bf16[16,208,128]{2,1,0:T(8,128)(2,1)S(1)} collective-permute-done((bf16[16,208,128]{2,1,0:T(8,128)(2,1)S(1)}, bf16[16,208,128]{2,1,0:T(8,128)(2,1)S(1)}, u32[]{:S(2)}, u32[]{:S(2)}) %collective-permute-start.6) | collective-permute-done | bytes 852000 | tf_op jit(solution)/shard_map/ppermute | solution.py:262
  52.5 1.6 %all-to-all-done.r_ref = bf16[16,208,128]{2,1,0:T(8,128)(2,1)S(1)} async-done(((bf16[16,208,128]{2,1,0:T(8,128)(2,1)}), bf16[16,208,128]{2,1,0:T(8,128)(2,1)S(1)}, u32[]{:S(2)}, u32[]{:S(2)}) %all-to-all-start) | async-done | bytes 852000 | tf_op jit(solution)/shard_map/all_to_all | solution.py:259
  54.1 3.5 %shard_map.65 = (bf16[4,288,128]{2,1,0:T(8,128)(2,1)S(1)}, f32[1,128]{1,0:T(1,128)S(1)}) custom-call(s32[3]{0:T(128)S(1)} %pad_add_fusion.at_ref, bf16[16,208,128]{2,1,0:T(8,128)(2,1)S(1)} %all-to-all-done.r_ref, bf16[512,256]{1,0:T(8,128)(2,1)S(1)} %bitcast.15, bf16[16,208,128]{2,1,0:T(8,128)(2,1)S(1)} %constant_dynamic-update-slice_fusion.lm_ref, ...), custom_call_target="tpu_custom_call" | custom-call | flops 3221225472 | bytes 4194304 | tf_op jit(solution)/shard_map/pallas_call | solution.py:264
  57.6 10.0 %all_to_all.10.pair_ref = bf16[4,288,128]{2,1,0:T(8,128)(2,1)S(1)} all-to-all(bf16[4,288,128]{2,1,0:T(8,128)(2,1)S(1)} %get-tuple-element.13), channel_id=1, replica_groups=mesh['y'=8,'zl'=2,'x'=4,'zh'=4,'core'=2] {'x'}, dimensions={0} | all-to-all | bytes 589824 | tf_op jit(solution)/shard_map/all_to_all | solution.py:277
  67.6 0.9 %shard_map.66 = f32[12,96,128]{2,1,0:T(8,128)} custom-call(bf16[4,288,128]{2,1,0:T(8,128)(2,1)S(1)} %all_to_all.10.pair_ref, f32[1,128]{1,0:T(1,128)S(1)} %get-tuple-element.14.offset_ref), custom_call_target="tpu_custom_call" | custom-call | tf_op jit(solution)/shard_map/pallas_call | solution.py:278
  (7 shorter events, 0.2 us)
Async XLA Ops:
  2.0 18.7 %collective-permute-start.1 = (bf16[1,208,128]{2,1,0:T(8,128)(2,1)S(1)}, bf16[1,208,128]{2,1,0:T(8,128)(2,1)S(1)}, u32[]{:S(2)}, u32[]{:S(2)}) collective-permute-start(bf16[1,208,128]{2,1,0:T(8,128)(2,1)S(1)} %get-tuple-element.11), channel_id=1, source_target_pairs={{0,4},{1,5},{2,6},{3,7},{4,0},{5,1},{6,2},{7,3},{8,12},{9,13},{10,... | collective-permute-start | bytes 159752 | tf_op jit(solution)/shard_map/ppermute | solution.py:255
  12.9 11.3 %collective-permute-start = (bf16[208,128]{1,0:T(8,128)(2,1)S(1)}, bf16[208,128]{1,0:T(8,128)(2,1)S(1)}, u32[]{:S(2)}, u32[]{:S(2)}) collective-permute-start(bf16[208,128]{1,0:T(8,128)(2,1)S(1)} %get-tuple-element.10), channel_id=1, source_target_pairs={{0,256},{1,192},{2,352},{3,160},{4,480},{5,32},{6,384},{7,64},{8,2... | collective-permute-start | bytes 159752 | tf_op jit(solution)/shard_map/ppermute | solution.py:252
  20.7 11.3 %collective-permute-start.2 = (bf16[2,208,128]{2,1,0:T(8,128)(2,1)S(1)}, bf16[2,208,128]{2,1,0:T(8,128)(2,1)S(1)}, u32[]{:S(2)}, u32[]{:S(2)}) collective-permute-start(bf16[2,208,128]{2,1,0:T(8,128)(2,1)S(1)} %pad_maximum_fusion.1), channel_id=1, source_target_pairs={{0,2},{1,3},{2,0},{3,1},{4,6},{5,7},{6,4},{7,5},{8,10},{9,11},{10,... | collective-permute-start | bytes 319496 | tf_op jit(solution)/shard_map/ppermute | solution.py:257
  25.2 28.9 %all-to-all-start = ((bf16[16,208,128]{2,1,0:T(8,128)(2,1)}), bf16[16,208,128]{2,1,0:T(8,128)(2,1)S(1)}, u32[]{:S(2)}, u32[]{:S(2)}) async-start(bf16[16,208,128]{2,1,0:T(8,128)(2,1)} %broadcast_in_dim.2), calls=%async_computation | async-start | bytes 1703936 | tf_op jit(solution)/shard_map/all_to_all | solution.py:259
  32.0 10.5 %collective-permute-start.3 = (bf16[4,208,128]{2,1,0:T(8,128)(2,1)S(1)}, bf16[4,208,128]{2,1,0:T(8,128)(2,1)S(1)}, u32[]{:S(2)}, u32[]{:S(2)}) collective-permute-start(bf16[4,208,128]{2,1,0:T(8,128)(2,1)S(1)} %pad_maximum_fusion), channel_id=1, source_target_pairs={{0,8},{1,9},{2,10},{3,11},{4,12},{5,13},{6,14},{7,15},{8,16},{9,17... | collective-permute-start | bytes 638984 | tf_op jit(solution)/shard_map/ppermute | solution.py:260
  35.4 10.6 %collective-permute-start.4 = (bf16[4,208,128]{2,1,0:T(8,128)(2,1)S(1)}, bf16[4,208,128]{2,1,0:T(8,128)(2,1)S(1)}, u32[]{:S(2)}, u32[]{:S(2)}) collective-permute-start(bf16[4,208,128]{2,1,0:T(8,128)(2,1)S(1)} %pad_maximum_fusion), channel_id=1, source_target_pairs={{0,16},{1,17},{2,18},{3,19},{4,20},{5,21},{6,22},{7,23},{8,24},{9,... | collective-permute-start | bytes 638984 | tf_op jit(solution)/shard_map/ppermute | solution.py:260
  38.5 9.7 %collective-permute-start.5 = (bf16[4,208,128]{2,1,0:T(8,128)(2,1)S(1)}, bf16[4,208,128]{2,1,0:T(8,128)(2,1)S(1)}, u32[]{:S(2)}, u32[]{:S(2)}) collective-permute-start(bf16[4,208,128]{2,1,0:T(8,128)(2,1)S(1)} %pad_maximum_fusion), channel_id=1, source_target_pairs={{0,24},{1,25},{2,26},{3,27},{4,28},{5,29},{6,30},{7,31},{8,0},{9,1... | collective-permute-start | bytes 638984 | tf_op jit(solution)/shard_map/ppermute | solution.py:260
  46.0 4.1 %copy-start = (bf16[1024,128]{1,0:T(8,128)(2,1)S(1)}, bf16[1024,128]{1,0:T(8,128)(2,1)}, u32[]{:S(2)}) copy-start(bf16[1024,128]{1,0:T(8,128)(2,1)} %param.10) | copy-start | bytes 786436
  48.2 4.3 %collective-permute-start.6 = (bf16[16,208,128]{2,1,0:T(8,128)(2,1)S(1)}, bf16[16,208,128]{2,1,0:T(8,128)(2,1)S(1)}, u32[]{:S(2)}, u32[]{:S(2)}) collective-permute-start(bf16[16,208,128]{2,1,0:T(8,128)(2,1)S(1)} %constant_dynamic-update-slice_fusion.lm_ref), channel_id=1, source_target_pairs={{0,1},{1,0},{2,3},{3,2},{4,5},{5,4},{6,7},{7,6},{8,9},{9,8},{10,11... | collective-permute-start | bytes 2555912 | tf_op jit(solution)/shard_map/ppermute | solution.py:262

commit v7 on v6

--- a/solution.py
+++ b/solution.py
@@ -12,7 +12,8 @@
 SIZES = (8, 2, 4, 4, 2)
 AXES = ("y", "zl", "x", "zh", "core")
 S, I, C, WIDTH, PAIR = 64, 12, 256, 32, 128
-ROWS = 208
+SENT_ROWS = 320
+ROWS = 200
 NT = (((1,), (1,)), ((), ()))
 VMEM = pl.BlockSpec(memory_space=pltpu.VMEM)
 HBM = pl.BlockSpec(memory_space=pltpu.HBM)
@@ -30,7 +31,7 @@
 
 
 def project_kernel(
-    x_in, m_in, wl_in, wr_in, offset_in, l_ref, r_ref, x_ref, m_ref, wl_ref, wr_ref, offset_ref, spread, sems
+    x_in, m_in, wl_in, wr_in, offset_in, l_ref, l2_ref, r_ref, x_ref, m_ref, wl_ref, wr_ref, offset_ref, spread, sems
 ):
     pairs = [
         (x_in, x_ref), (m_in, m_ref), (wl_in, wl_ref), (wr_in, wr_ref), (offset_in, offset_ref)
@@ -45,8 +46,7 @@
         copy.wait()
     mask = m_ref[...].astype(F32).astype(BF16)
     mask_twice = jnp.concatenate([mask, mask], axis=1)
-    mask_rows = dot(one_hot((16, I), lambda r, t: r == t), mask_twice)
-    mask_pairs = dot(one_hot((32, I), lambda r, t: r // 2 == t), mask_twice)
+    mask_halves = [dot(one_hot((8, I), lambda r, t: (t == r + h) & (r < 6)), mask_twice) for h in (0, 6)]
     mask_cols = dot(one_hot((S, S), lambda r, t: r == t), mask, NT)
     wl = dot(one_hot((128, WIDTH), lambda r, t: r % WIDTH == t), wl_ref[...])
     wr = dot(
@@ -55,6 +55,7 @@
     weights = jnp.concatenate([wl, wr], axis=0).astype(BF16)
     block = lax.broadcasted_iota(jnp.int32, (S, 256), 1) % 128 // WIDTH
     low = lax.broadcasted_iota(jnp.int32, (8, 128), 1) < 64
+    tiles = []
     for g in range(I // 4):
         x = x_ref[4 * g : 4 * g + 4].reshape(4 * S, C).astype(F32)
         centred = x - jnp.sum(x, axis=-1, keepdims=True) * (1.0 / C)
@@ -68,7 +69,7 @@
             i = 4 * g + k
             part = both[k * S : k * S + S] * mask_cols[:, i : i + 1]
             tile = part if k == 0 else jnp.where(block == k, part, tile)
-        l_ref[0, g * S : (g + 1) * S, :] = tile[:, 0:128].astype(BF16)
+        tiles.append(tile[:, 0:128])
         right = tile[:, 128:256]
         right = jnp.concatenate([right, right], axis=0).T
         for k in range(4):
@@ -76,16 +77,21 @@
                 row = k * WIDTH + e * 16
                 part = jnp.where(low, right[row : row + 8], right[row + 8 : row + 16])
                 spread[pl.ds(2 * (4 * g + k) + e, 8, stride=24), :] = part
-    row = lax.broadcasted_iota(jnp.int32, (16, 128), 0)
-    last, rest = mask_rows, offset_ref[...]
+    mask_block = jnp.where(low, mask_halves[0], mask_halves[1])
+    row = lax.broadcasted_iota(jnp.int32, (8, 128), 0)
+    rest, parts = offset_ref[...], []
     for n in range(3):
         part = rest.astype(BF16).astype(F32)
-        last = jnp.where(row == I + n, jnp.broadcast_to(part, (16, 128)), last)
+        parts.append(jnp.broadcast_to(part, (8, 128)))
         rest = rest - part
-    l_ref[0, 192:208, :] = last.astype(BF16)
-    r_ref[0:192, :] = spread[...].astype(BF16)
-    low16 = lax.broadcasted_iota(jnp.int32, (16, 128), 1) < 64
-    r_ref[192:208, :] = jnp.where(low16, mask_pairs[0:16], mask_pairs[16:32]).astype(BF16)
+    last = jnp.where(row == 6, parts[0], jnp.where(row == 7, parts[1], mask_block))
+    left = jnp.concatenate([jnp.concatenate(tiles, axis=0), last], axis=0).astype(BF16)
+    l_ref[0] = left
+    r_ref[192:SENT_ROWS, :] = jnp.zeros((SENT_ROWS - 192, 128), BF16)
+    l2_ref[0] = left
+    l2_ref[1] = jnp.zeros((ROWS, 128), BF16)
+    last = jnp.where(row == 6, parts[2], mask_block)
+    r_ref[0:ROWS, :] = jnp.concatenate([spread[...], last], axis=0).astype(BF16)
 
 
 def placed(step, core):
@@ -97,7 +103,7 @@
 def pair_kernel(at_ref, r_ref, w_ref, lm_ref, lo_ref, out_ref, offset_ref, rt, rmask, lmask, z):
     zh, core, x = at_ref[0], at_ref[1], at_ref[2]
     low = lax.broadcasted_iota(jnp.int32, (ROWS, 128), 1) < 64
-    low16 = lax.broadcasted_iota(jnp.int32, (16, 128), 1) < 64
+    low8 = lax.broadcasted_iota(jnp.int32, (8, 128), 1) < 64
 
     def piece(zl, t, c):
         step = (2 * ((zh ^ (0, 2, 1, 3)[t]) - zh) + zl) & 7
@@ -114,16 +120,26 @@
             cols = slice(t * 128, t * 128 + 128)
             rt[zl, 0:192, cols] = first[0:192]
             rt[zl, 192:384, cols] = second[0:192]
-            rmask[zl, 0:16, cols] = first[192:208]
-            rmask[zl, 16:32, cols] = second[192:208]
+            rmask[zl, :, cols] = jnp.concatenate([first[192:200], second[192:200]], axis=0)
     for k in range(4):
         for t in range(4):
-            a, b = lm_ref[4 * k + t, 192:208, :], lo_ref[4 * k + t, 192:208, :]
-            lmask[k * 16 : k * 16 + 16, t * 128 : t * 128 + 128] = jnp.where(low16, a, b)
-    parts = lm_ref[0, 192:208, :].astype(F32)
-    offset_ref[...] = parts[12:13] + parts[13:14] + parts[14:15]
+            a, b = lm_ref[4 * k + t][192:200], lo_ref[4 * k + t][192:200]
+            lmask[k * 16 : k * 16 + 16, t * 128 : t * 128 + 128] = jnp.concatenate(
+                [
+                    jnp.where(low8, a, pltpu.roll(b, 64, 1)),
+                    jnp.where(low8, pltpu.roll(a, 64, 1), b),
+                ],
+                axis=0,
+            )
+    parts = lm_ref[0][192:200].astype(F32)
+    offset_ref[...] = parts[6:7] + parts[7:8] + r_ref[0][192:200].astype(F32)[6:7]
+    twice = one_hot((24, 16), lambda r, t: t == r // 2 + jnp.where(r < 12, 0, 2))
     scale = jnp.concatenate(
-        [1.0 / (dot(rmask[zl], lmask[...], NT)[0:24] + 1.0) for zl in range(2)], axis=0
+        [
+            1.0 / (dot(dot(twice, rmask[zl]).astype(BF16), lmask[...], NT) + 1.0)
+            for zl in range(2)
+        ],
+        axis=0,
     )
 
     lanes = lax.broadcasted_iota(jnp.int32, (48, 128), 1)
@@ -169,7 +185,8 @@
             wide = dot(jnp.concatenate(left_rows, axis=0), w_ref[...])
             k = 2 * pair + n
             for i in range(I):
-                column = scale[:, k * 16 + i : k * 16 + i + 1]
+                at = k * 16 + i + (0 if i < 6 else 2)
+                column = scale[:, at : at + 1]
                 for e in range(2):
                     z[e, i * 48 : i * 48 + 48, :] = (
                         wide[i * 48 : i * 48 + 48, e * 128 : e * 128 + 128] * column
@@ -229,11 +246,12 @@
 
 
 def local(x, m, wl, wr, w, offset):
-    left, right = call(
+    left, lefts, right = call(
         project_kernel,
         [
             jax.ShapeDtypeStruct((1, ROWS, 128), BF16),
-            jax.ShapeDtypeStruct((ROWS, 128), BF16),
+            jax.ShapeDtypeStruct((2, ROWS, 128), BF16),
+            jax.ShapeDtypeStruct((SENT_ROWS, 128), BF16),
         ],
         [HBM] * 5,
         [
@@ -250,15 +268,15 @@
     at = jnp.stack([lax.axis_index(name) for name in ("zh", "core", "x")]).astype(jnp.int32)
 
     right = lax.ppermute(right, AXES, TRANSPOSE)
-    right = jnp.broadcast_to(right[None], (16, ROWS, 128))
-    left = lax.optimization_barrier(
-        jnp.concatenate([left, lax.ppermute(left, AXES, ACROSS_ZH[2])])
-    )
+    right = jnp.broadcast_to(right[None, :ROWS], (16, ROWS, 128))
+    far = lax.ppermute(left, AXES, ACROSS_ZH[2])
+    left = lax.dynamic_update_slice(lefts, far, (1, 0, 0))
     left = jnp.concatenate([left, lax.ppermute(left, AXES, ACROSS_ZH[1])])
     left = lax.optimization_barrier((left, right))[0]
     right = lax.all_to_all(right, ("y", "zl"), 0, 0, tiled=True)
-    along = {k: lax.ppermute(left, AXES, ALONG_X[k]) for k in (2, 3, 1)}
-    left = jnp.concatenate([left, along[1], along[2], along[3]], axis=0)
+    left = jnp.concatenate(
+        [left] + [lax.ppermute(left, AXES, ALONG_X[k]) for k in (1, 2, 3)], axis=0
+    )
     left_other = lax.ppermute(left, AXES, OTHER_CORE)
 
     pairs, offset = call(
@@ -267,7 +285,7 @@
         [SMEM] + [VMEM] * 4,
         [
             pltpu.VMEM((2, 384, 512), BF16),
-            pltpu.VMEM((2, 32, 512), BF16),
+            pltpu.VMEM((2, 16, 512), BF16),
             pltpu.VMEM((64, 512), BF16),
             pltpu.VMEM((2, 576, 128), F32),
         ],

time: 68.9 us -> 69.2 us (level)
  waiting for transfers between devices: 9.14 us -> 8.38 us
  starting transfers between devices: 41.3 us -> 42 us
    ppermute x4, waiting for transfers between devices: 5.54 us -> 4.84 us  [the longest x3 4.84 us: local(): lax.ppermute(left, AXES, ALONG_X[k])]
where the time goes in v7:
time: 69.2 us; the launch traced here: 68.6 us
  starting transfers between devices  42 us (61%)
  blocking collectives  10 us (14%)
  waiting for transfers between devices  8.38 us (12%)
  Pallas kernels  6.53 us (9%)
  local copies, waits for them, and re-layouts  1.41 us (2%)
    ppermute x1, starting transfers between devices, local(): far = lax.ppermute(left, AXES, ACROSS_ZH[2])  10.9 us
    ppermute x3, starting transfers between devices, local(): lax.ppermute(left, AXES, ALONG_X[k])  10.5 us
    all_to_all x1, blocking collectives, local(): pairs = lax.all_to_all(pairs, 'x', 0, 0, tiled=True)  10 us
    ppermute x1, starting transfers between devices, local(): right = lax.ppermute(right, AXES, TRANSPOSE)  7.74 us
    all_to_all x1, starting transfers between devices, local(): right = lax.all_to_all(right, ('y', 'zl'), 0, 0, tiled=True)  7.41 us
    ppermute x3, waiting for transfers between devices, local(): lax.ppermute(left, AXES, ALONG_X[k])  4.84 us
    pallas_call x1, Pallas kernels, local(): call(pair_kernel, [jax.ShapeDtypeStruct((4, 288, 128), BF16), jax.ShapeDt...  3.72 us
    ppermute x1, starting transfers between devices, local(): left = jnp.concatenate([left, lax.ppermute(left, AXES, ACROSS_ZH[1])])  3.49 us
  transfers between devices with their start and end apart: 8, of which 4 were waited for; matrix products, arithmetic and copies ran while one was open for 2% of the time, Pallas kernels for 0%

profile of v7, /device:TPU:2, one launch (start us, length us, event | category | flops | bytes accessed | tf_op | source)
XLA Modules:
  0.0 68.6 jit_solution(18382495881729865991)
XLA Ops:
  0.0 2.0 %shard_map.64 = (bf16[1,200,128]{2,1,0:T(8,128)(2,1)S(1)}, bf16[2,200,128]{2,1,0:T(8,128)(2,1)S(1)}, bf16[320,128]{1,0:T(8,128)(2,1)S(1)}) custom-call(bf16[12,64,256]{2,1,0:T(8,128)(2,1)} %bitcast.17, s32[12,64]{1,0:T(8,128)} %bitcast.21, bf16[32,256]{1,0:T(8,128)(2,1)} %bitcast.19, bf16[32,256]{1,0:T(8,128)(2,1)} %bitcast.20, f32[1,128]{1,0:T(1,128)} %bitcast.22), custom_call_target="tpu_custom_call" | custom-call | tf_op jit(solution)/shard_map/pallas_call | solution.py:249
  2.0 10.9 %collective-permute-start.1 = (bf16[1,200,128]{2,1,0:T(8,128)(2,1)S(1)}, bf16[1,200,128]{2,1,0:T(8,128)(2,1)S(1)}, u32[]{:S(2)}, u32[]{:S(2)}) collective-permute-start(bf16[1,200,128]{2,1,0:T(8,128)(2,1)S(1)} %get-tuple-element.13), channel_id=1, source_target_pairs={{0,4},{1,5},{2,6},{3,7},{4,0},{5,1},{6,2},{7,3},{8,12},{9,13},{10,... | collective-permute-start | bytes 153608 | tf_op jit(solution)/shard_map/ppermute | solution.py:272
  12.9 7.7 %collective-permute-start = (bf16[320,128]{1,0:T(8,128)(2,1)S(1)}, bf16[320,128]{1,0:T(8,128)(2,1)S(1)}, u32[]{:S(2)}, u32[]{:S(2)}) collective-permute-start(bf16[320,128]{1,0:T(8,128)(2,1)S(1)} %get-tuple-element.11), channel_id=1, source_target_pairs={{0,256},{1,192},{2,352},{3,160},{4,480},{5,32},{6,384},{7,64},{8,2... | collective-permute-start | bytes 245768 | tf_op jit(solution)/shard_map/ppermute | solution.py:270
  20.6 0.0 collective-permute-done.1
  20.7 3.5 %collective-permute-start.2 = (bf16[2,200,128]{2,1,0:T(8,128)(2,1)S(1)}, bf16[2,200,128]{2,1,0:T(8,128)(2,1)S(1)}, u32[]{:S(2)}, u32[]{:S(2)}) collective-permute-start(bf16[2,200,128]{2,1,0:T(8,128)(2,1)S(1)} %constant_dynamic-update-slice_fusion.4), channel_id=1, source_target_pairs={{0,2},{1,3},{2,0},{3,1},{4,6},{5,7},{6,4},{7,5},{8,10},{9,11},{10,... | collective-permute-start | bytes 307208 | tf_op jit(solution)/shard_map/ppermute | solution.py:274
  24.2 0.0 collective-permute-done
  24.2 1.0 %broadcast_in_dim.2 = bf16[16,200,128]{2,1,0:T(8,128)(2,1)} broadcast(bf16[200,128]{1,0:T(8,128)(2,1)S(1)} %slice.4), dimensions={1,2} | broadcast | bytes 870400 | tf_op jit(solution)/shard_map/broadcast_in_dim | solution.py:271
  25.2 7.4 %all-to-all-start = ((bf16[16,200,128]{2,1,0:T(8,128)(2,1)}), bf16[16,200,128]{2,1,0:T(8,128)(2,1)S(1)}, u32[]{:S(2)}, u32[]{:S(2)}) async-start(bf16[16,200,128]{2,1,0:T(8,128)(2,1)} %broadcast_in_dim.2), calls=%async_computation | async-start | bytes 1638400 | tf_op jit(solution)/shard_map/all_to_all | solution.py:276
  32.6 0.0 collective-permute-done.2
  32.7 3.4 %collective-permute-start.3 = (bf16[4,200,128]{2,1,0:T(8,128)(2,1)S(1)}, bf16[4,200,128]{2,1,0:T(8,128)(2,1)S(1)}, u32[]{:S(2)}, u32[]{:S(2)}) collective-permute-start(bf16[4,200,128]{2,1,0:T(8,128)(2,1)S(1)} %pad_maximum_fusion), channel_id=1, source_target_pairs={{0,8},{1,9},{2,10},{3,11},{4,12},{5,13},{6,14},{7,15},{8,16},{9,17... | collective-permute-start | bytes 614408 | tf_op jit(solution)/shard_map/ppermute | solution.py:278
  36.1 3.0 %collective-permute-start.4 = (bf16[4,200,128]{2,1,0:T(8,128)(2,1)S(1)}, bf16[4,200,128]{2,1,0:T(8,128)(2,1)S(1)}, u32[]{:S(2)}, u32[]{:S(2)}) collective-permute-start(bf16[4,200,128]{2,1,0:T(8,128)(2,1)S(1)} %pad_maximum_fusion), channel_id=1, source_target_pairs={{0,16},{1,17},{2,18},{3,19},{4,20},{5,21},{6,22},{7,23},{8,24},{9,... | collective-permute-start | bytes 614408 | tf_op jit(solution)/shard_map/ppermute | solution.py:278
  39.1 4.1 %collective-permute-start.5 = (bf16[4,200,128]{2,1,0:T(8,128)(2,1)S(1)}, bf16[4,200,128]{2,1,0:T(8,128)(2,1)S(1)}, u32[]{:S(2)}, u32[]{:S(2)}) collective-permute-start(bf16[4,200,128]{2,1,0:T(8,128)(2,1)S(1)} %pad_maximum_fusion), channel_id=1, source_target_pairs={{0,24},{1,25},{2,26},{3,27},{4,28},{5,29},{6,30},{7,31},{8,0},{9,1... | collective-permute-start | bytes 614408 | tf_op jit(solution)/shard_map/ppermute | solution.py:278
  43.2 0.0 collective-permute-done.3
  43.2 2.8 %collective-permute-done.4 = bf16[4,200,128]{2,1,0:T(8,128)(2,1)S(1)} collective-permute-done((bf16[4,200,128]{2,1,0:T(8,128)(2,1)S(1)}, bf16[4,200,128]{2,1,0:T(8,128)(2,1)S(1)}, u32[]{:S(2)}, u32[]{:S(2)}) %collective-permute-start.4) | collective-permute-done | bytes 204832 | tf_op jit(solution)/shard_map/ppermute | solution.py:278
  46.1 0.0 copy-start
  46.1 2.0 %collective-permute-done.5 = bf16[4,200,128]{2,1,0:T(8,128)(2,1)S(1)} collective-permute-done((bf16[4,200,128]{2,1,0:T(8,128)(2,1)S(1)}, bf16[4,200,128]{2,1,0:T(8,128)(2,1)S(1)}, u32[]{:S(2)}, u32[]{:S(2)}) %collective-permute-start.5) | collective-permute-done | bytes 204832 | tf_op jit(solution)/shard_map/ppermute | solution.py:278
  48.2 1.9 %collective-permute-start.6 = (bf16[16,200,128]{2,1,0:T(8,128)(2,1)S(1)}, bf16[16,200,128]{2,1,0:T(8,128)(2,1)S(1)}, u32[]{:S(2)}, u32[]{:S(2)}) collective-permute-start(bf16[16,200,128]{2,1,0:T(8,128)(2,1)S(1)} %constant_dynamic-update-slice_fusion.lm_ref), channel_id=1, source_target_pairs={{0,1},{1,0},{2,3},{3,2},{4,5},{5,4},{6,7},{7,6},{8,9},{9,8},{10,11... | collective-permute-start | bytes 2457608 | tf_op jit(solution)/shard_map/ppermute | solution.py:280
  50.1 0.0 copy-done
  50.1 0.2 copy.7
  50.4 0.1 pad_add_fusion.at_ref
  50.5 1.9 %collective-permute-done.6.lo_ref = bf16[16,200,128]{2,1,0:T(8,128)(2,1)S(1)} collective-permute-done((bf16[16,200,128]{2,1,0:T(8,128)(2,1)S(1)}, bf16[16,200,128]{2,1,0:T(8,128)(2,1)S(1)}, u32[]{:S(2)}, u32[]{:S(2)}) %collective-permute-start.6) | collective-permute-done | bytes 819232 | tf_op jit(solution)/shard_map/ppermute | solution.py:280
  52.4 1.6 %all-to-all-done.r_ref = bf16[16,200,128]{2,1,0:T(8,128)(2,1)S(1)} async-done(((bf16[16,200,128]{2,1,0:T(8,128)(2,1)}), bf16[16,200,128]{2,1,0:T(8,128)(2,1)S(1)}, u32[]{:S(2)}, u32[]{:S(2)}) %all-to-all-start) | async-done | bytes 819232 | tf_op jit(solution)/shard_map/all_to_all | solution.py:276
  54.0 3.7 %shard_map.65 = (bf16[4,288,128]{2,1,0:T(8,128)(2,1)S(1)}, f32[1,128]{1,0:T(1,128)S(1)}) custom-call(s32[3]{0:T(128)S(1)} %pad_add_fusion.at_ref, bf16[16,200,128]{2,1,0:T(8,128)(2,1)S(1)} %all-to-all-done.r_ref, bf16[512,256]{1,0:T(8,128)(2,1)S(1)} %bitcast.15, bf16[16,200,128]{2,1,0:T(8,128)(2,1)S(1)} %constant_dynamic-update-slice_fusion.lm_ref, ...), custom_call_target="tpu_custom_call" | custom-call | flops 3221225472 | bytes 4194304 | tf_op jit(solution)/shard_map/pallas_call | solution.py:282
  57.7 10.0 %all_to_all.10.pair_ref = bf16[4,288,128]{2,1,0:T(8,128)(2,1)S(1)} all-to-all(bf16[4,288,128]{2,1,0:T(8,128)(2,1)S(1)} %get-tuple-element.15), channel_id=1, replica_groups=mesh['y'=8,'zl'=2,'x'=4,'zh'=4,'core'=2] {'x'}, dimensions={0} | all-to-all | bytes 589824 | tf_op jit(solution)/shard_map/all_to_all | solution.py:295
  67.7 0.9 %shard_map.66 = f32[12,96,128]{2,1,0:T(8,128)} custom-call(bf16[4,288,128]{2,1,0:T(8,128)(2,1)S(1)} %all_to_all.10.pair_ref, f32[1,128]{1,0:T(1,128)S(1)} %get-tuple-element.16.offset_ref), custom_call_target="tpu_custom_call" | custom-call | tf_op jit(solution)/shard_map/pallas_call | solution.py:296
  (8 shorter events, 0.2 us)
Async XLA Ops:
  2.0 18.7 %collective-permute-start.1 = (bf16[1,200,128]{2,1,0:T(8,128)(2,1)S(1)}, bf16[1,200,128]{2,1,0:T(8,128)(2,1)S(1)}, u32[]{:S(2)}, u32[]{:S(2)}) collective-permute-start(bf16[1,200,128]{2,1,0:T(8,128)(2,1)S(1)} %get-tuple-element.13), channel_id=1, source_target_pairs={{0,4},{1,5},{2,6},{3,7},{4,0},{5,1},{6,2},{7,3},{8,12},{9,13},{10,... | collective-permute-start | bytes 153608 | tf_op jit(solution)/shard_map/ppermute | solution.py:272
  12.9 11.3 %collective-permute-start = (bf16[320,128]{1,0:T(8,128)(2,1)S(1)}, bf16[320,128]{1,0:T(8,128)(2,1)S(1)}, u32[]{:S(2)}, u32[]{:S(2)}) collective-permute-start(bf16[320,128]{1,0:T(8,128)(2,1)S(1)} %get-tuple-element.11), channel_id=1, source_target_pairs={{0,256},{1,192},{2,352},{3,160},{4,480},{5,32},{6,384},{7,64},{8,2... | collective-permute-start | bytes 245768 | tf_op jit(solution)/shard_map/ppermute | solution.py:270
  20.7 12.0 %collective-permute-start.2 = (bf16[2,200,128]{2,1,0:T(8,128)(2,1)S(1)}, bf16[2,200,128]{2,1,0:T(8,128)(2,1)S(1)}, u32[]{:S(2)}, u32[]{:S(2)}) collective-permute-start(bf16[2,200,128]{2,1,0:T(8,128)(2,1)S(1)} %constant_dynamic-update-slice_fusion.4), channel_id=1, source_target_pairs={{0,2},{1,3},{2,0},{3,1},{4,6},{5,7},{6,4},{7,5},{8,10},{9,11},{10,... | collective-permute-start | bytes 307208 | tf_op jit(solution)/shard_map/ppermute | solution.py:274
  25.2 28.8 %all-to-all-start = ((bf16[16,200,128]{2,1,0:T(8,128)(2,1)}), bf16[16,200,128]{2,1,0:T(8,128)(2,1)S(1)}, u32[]{:S(2)}, u32[]{:S(2)}) async-start(bf16[16,200,128]{2,1,0:T(8,128)(2,1)} %broadcast_in_dim.2), calls=%async_computation | async-start | bytes 1638400 | tf_op jit(solution)/shard_map/all_to_all | solution.py:276
  32.7 10.5 %collective-permute-start.3 = (bf16[4,200,128]{2,1,0:T(8,128)(2,1)S(1)}, bf16[4,200,128]{2,1,0:T(8,128)(2,1)S(1)}, u32[]{:S(2)}, u32[]{:S(2)}) collective-permute-start(bf16[4,200,128]{2,1,0:T(8,128)(2,1)S(1)} %pad_maximum_fusion), channel_id=1, source_target_pairs={{0,8},{1,9},{2,10},{3,11},{4,12},{5,13},{6,14},{7,15},{8,16},{9,17... | collective-permute-start | bytes 614408 | tf_op jit(solution)/shard_map/ppermute | solution.py:278
  36.1 10.0 %collective-permute-start.4 = (bf16[4,200,128]{2,1,0:T(8,128)(2,1)S(1)}, bf16[4,200,128]{2,1,0:T(8,128)(2,1)S(1)}, u32[]{:S(2)}, u32[]{:S(2)}) collective-permute-start(bf16[4,200,128]{2,1,0:T(8,128)(2,1)S(1)} %pad_maximum_fusion), channel_id=1, source_target_pairs={{0,16},{1,17},{2,18},{3,19},{4,20},{5,21},{6,22},{7,23},{8,24},{9,... | collective-permute-start | bytes 614408 | tf_op jit(solution)/shard_map/ppermute | solution.py:278
  39.1 9.0 %collective-permute-start.5 = (bf16[4,200,128]{2,1,0:T(8,128)(2,1)S(1)}, bf16[4,200,128]{2,1,0:T(8,128)(2,1)S(1)}, u32[]{:S(2)}, u32[]{:S(2)}) collective-permute-start(bf16[4,200,128]{2,1,0:T(8,128)(2,1)S(1)} %pad_maximum_fusion), channel_id=1, source_target_pairs={{0,24},{1,25},{2,26},{3,27},{4,28},{5,29},{6,30},{7,31},{8,0},{9,1... | collective-permute-start | bytes 614408 | tf_op jit(solution)/shard_map/ppermute | solution.py:278
  46.1 4.0 %copy-start = (bf16[1024,128]{1,0:T(8,128)(2,1)S(1)}, bf16[1024,128]{1,0:T(8,128)(2,1)}, u32[]{:S(2)}) copy-start(bf16[1024,128]{1,0:T(8,128)(2,1)} %param.10) | copy-start | bytes 786436
  48.2 4.2 %collective-permute-start.6 = (bf16[16,200,128]{2,1,0:T(8,128)(2,1)S(1)}, bf16[16,200,128]{2,1,0:T(8,128)(2,1)S(1)}, u32[]{:S(2)}, u32[]{:S(2)}) collective-permute-start(bf16[16,200,128]{2,1,0:T(8,128)(2,1)S(1)} %constant_dynamic-update-slice_fusion.lm_ref), channel_id=1, source_target_pairs={{0,1},{1,0},{2,3},{3,2},{4,5},{5,4},{6,7},{7,6},{8,9},{9,8},{10,11... | collective-permute-start | bytes 2457608 | tf_op jit(solution)/shard_map/ppermute | solution.py:280

commit v8 on v6

--- a/solution.py
+++ b/solution.py
@@ -145,7 +145,7 @@
             ],
             axis=0,
         )
-        outer = [dot(rt[zl], rhs) for zl in range(2)]
+        outer = [dot(rt[zl], rhs).astype(BF16) for zl in range(2)]
         for n in range(2):
             left_rows = []
             for g in range(3 * n, 3 * n + 3):
@@ -154,7 +154,6 @@
                 for q in range(4):
                     a = [
                         jnp.concatenate([o[e * 24 : e * 24 + 24, cols] for o in outer], axis=0)
-                        .astype(BF16)
                         for e in range(4 * q, 4 * q + 4)
                     ]
                     r02 = pltpu.roll(jnp.where(half, a[2], a[0]), 64, 1)

time: 68.9 us -> 68.9 us (level)
  no operation moved by 1% of the time
where the time goes in v8:
time: 68.9 us; the launch traced here: 68.4 us
  starting transfers between devices  41.3 us (60%)
  blocking collectives  10 us (15%)
  waiting for transfers between devices  9.14 us (13%)
  Pallas kernels  6.25 us (9%)
  local copies, waits for them, and re-layouts  1.42 us (2%)
    ppermute x1, starting transfers between devices, local(): lax.ppermute(left, AXES, ACROSS_ZH[2])  10.9 us
    ppermute x3, starting transfers between devices, local(): along = {k: lax.ppermute(left, AXES, ALONG_X[k]) for k in (2, 3, 1)}  10.5 us
    all_to_all x1, blocking collectives, local(): pairs = lax.all_to_all(pairs, 'x', 0, 0, tiled=True)  10 us
    ppermute x1, starting transfers between devices, local(): right = lax.ppermute(right, AXES, TRANSPOSE)  7.74 us
    all_to_all x1, starting transfers between devices, local(): right = lax.all_to_all(right, ('y', 'zl'), 0, 0, tiled=True)  6.77 us
    ppermute x3, waiting for transfers between devices, local(): along = {k: lax.ppermute(left, AXES, ALONG_X[k]) for k in (2, 3, 1)}  5.54 us
    ppermute x1, starting transfers between devices, local(): left = jnp.concatenate([left, lax.ppermute(left, AXES, ACROSS_ZH[1])])  3.49 us
    pallas_call x1, Pallas kernels, local(): call(pair_kernel, [jax.ShapeDtypeStruct((4, 288, 128), BF16), jax.ShapeDt...  3.45 us
  transfers between devices with their start and end apart: 8, of which 4 were waited for; matrix products, arithmetic and copies ran while one was open for 2% of the time, Pallas kernels for 0%

profile of v8, /device:TPU:2, one launch (start us, length us, event | category | flops | bytes accessed | tf_op | source)
XLA Modules:
  0.0 68.4 jit_solution(11730560333825665747)
XLA Ops:
  0.0 1.9 %shard_map.64 = (bf16[1,208,128]{2,1,0:T(8,128)(2,1)S(1)}, bf16[208,128]{1,0:T(8,128)(2,1)S(1)}) custom-call(bf16[12,64,256]{2,1,0:T(8,128)(2,1)} %bitcast.17, s32[12,64]{1,0:T(8,128)} %bitcast.21, bf16[32,256]{1,0:T(8,128)(2,1)} %bitcast.19, bf16[32,256]{1,0:T(8,128)(2,1)} %bitcast.20, f32[1,128]{1,0:T(1,128)} %bitcast.22), custom_call_target="tpu_custom_call" | custom-call | tf_op jit(solution)/shard_map/pallas_call | solution.py:231
  2.0 10.9 %collective-permute-start.1 = (bf16[1,208,128]{2,1,0:T(8,128)(2,1)S(1)}, bf16[1,208,128]{2,1,0:T(8,128)(2,1)S(1)}, u32[]{:S(2)}, u32[]{:S(2)}) collective-permute-start(bf16[1,208,128]{2,1,0:T(8,128)(2,1)S(1)} %get-tuple-element.11), channel_id=1, source_target_pairs={{0,4},{1,5},{2,6},{3,7},{4,0},{5,1},{6,2},{7,3},{8,12},{9,13},{10,... | collective-permute-start | bytes 159752 | tf_op jit(solution)/shard_map/ppermute | solution.py:254
  12.9 7.7 %collective-permute-start = (bf16[208,128]{1,0:T(8,128)(2,1)S(1)}, bf16[208,128]{1,0:T(8,128)(2,1)S(1)}, u32[]{:S(2)}, u32[]{:S(2)}) collective-permute-start(bf16[208,128]{1,0:T(8,128)(2,1)S(1)} %get-tuple-element.10), channel_id=1, source_target_pairs={{0,256},{1,192},{2,352},{3,160},{4,480},{5,32},{6,384},{7,64},{8,2... | collective-permute-start | bytes 159752 | tf_op jit(solution)/shard_map/ppermute | solution.py:251
  20.6 0.0 collective-permute-done.1
  20.7 3.5 %collective-permute-start.2 = (bf16[2,208,128]{2,1,0:T(8,128)(2,1)S(1)}, bf16[2,208,128]{2,1,0:T(8,128)(2,1)S(1)}, u32[]{:S(2)}, u32[]{:S(2)}) collective-permute-start(bf16[2,208,128]{2,1,0:T(8,128)(2,1)S(1)} %pad_maximum_fusion.1), channel_id=1, source_target_pairs={{0,2},{1,3},{2,0},{3,1},{4,6},{5,7},{6,4},{7,5},{8,10},{9,11},{10,... | collective-permute-start | bytes 319496 | tf_op jit(solution)/shard_map/ppermute | solution.py:256
  24.2 0.0 collective-permute-done
  24.2 1.0 %broadcast_in_dim.2 = bf16[16,208,128]{2,1,0:T(8,128)(2,1)} broadcast(bf16[208,128]{1,0:T(8,128)(2,1)S(1)} %collective-permute-done), dimensions={1,2} | broadcast | bytes 905216 | tf_op jit(solution)/shard_map/broadcast_in_dim | solution.py:252
  25.2 6.8 %all-to-all-start = ((bf16[16,208,128]{2,1,0:T(8,128)(2,1)}), bf16[16,208,128]{2,1,0:T(8,128)(2,1)S(1)}, u32[]{:S(2)}, u32[]{:S(2)}) async-start(bf16[16,208,128]{2,1,0:T(8,128)(2,1)} %broadcast_in_dim.2), calls=%async_computation | async-start | bytes 1703936 | tf_op jit(solution)/shard_map/all_to_all | solution.py:258
  32.0 0.0 collective-permute-done.2
  32.0 3.4 %collective-permute-start.3 = (bf16[4,208,128]{2,1,0:T(8,128)(2,1)S(1)}, bf16[4,208,128]{2,1,0:T(8,128)(2,1)S(1)}, u32[]{:S(2)}, u32[]{:S(2)}) collective-permute-start(bf16[4,208,128]{2,1,0:T(8,128)(2,1)S(1)} %pad_maximum_fusion), channel_id=1, source_target_pairs={{0,8},{1,9},{2,10},{3,11},{4,12},{5,13},{6,14},{7,15},{8,16},{9,17... | collective-permute-start | bytes 638984 | tf_op jit(solution)/shard_map/ppermute | solution.py:259
  35.4 3.0 %collective-permute-start.4 = (bf16[4,208,128]{2,1,0:T(8,128)(2,1)S(1)}, bf16[4,208,128]{2,1,0:T(8,128)(2,1)S(1)}, u32[]{:S(2)}, u32[]{:S(2)}) collective-permute-start(bf16[4,208,128]{2,1,0:T(8,128)(2,1)S(1)} %pad_maximum_fusion), channel_id=1, source_target_pairs={{0,16},{1,17},{2,18},{3,19},{4,20},{5,21},{6,22},{7,23},{8,24},{9,... | collective-permute-start | bytes 638984 | tf_op jit(solution)/shard_map/ppermute | solution.py:259
  38.5 4.1 %collective-permute-start.5 = (bf16[4,208,128]{2,1,0:T(8,128)(2,1)S(1)}, bf16[4,208,128]{2,1,0:T(8,128)(2,1)S(1)}, u32[]{:S(2)}, u32[]{:S(2)}) collective-permute-start(bf16[4,208,128]{2,1,0:T(8,128)(2,1)S(1)} %pad_maximum_fusion), channel_id=1, source_target_pairs={{0,24},{1,25},{2,26},{3,27},{4,28},{5,29},{6,30},{7,31},{8,0},{9,1... | collective-permute-start | bytes 638984 | tf_op jit(solution)/shard_map/ppermute | solution.py:259
  42.5 0.0 collective-permute-done.3
  42.6 3.4 %collective-permute-done.4 = bf16[4,208,128]{2,1,0:T(8,128)(2,1)S(1)} collective-permute-done((bf16[4,208,128]{2,1,0:T(8,128)(2,1)S(1)}, bf16[4,208,128]{2,1,0:T(8,128)(2,1)S(1)}, u32[]{:S(2)}, u32[]{:S(2)}) %collective-permute-start.4) | collective-permute-done | bytes 213024 | tf_op jit(solution)/shard_map/ppermute | solution.py:259
  46.0 0.0 copy-start
  46.0 2.1 %collective-permute-done.5 = bf16[4,208,128]{2,1,0:T(8,128)(2,1)S(1)} collective-permute-done((bf16[4,208,128]{2,1,0:T(8,128)(2,1)S(1)}, bf16[4,208,128]{2,1,0:T(8,128)(2,1)S(1)}, u32[]{:S(2)}, u32[]{:S(2)}) %collective-permute-start.5) | collective-permute-done | bytes 213024 | tf_op jit(solution)/shard_map/ppermute | solution.py:259
  48.2 1.9 %collective-permute-start.6 = (bf16[16,208,128]{2,1,0:T(8,128)(2,1)S(1)}, bf16[16,208,128]{2,1,0:T(8,128)(2,1)S(1)}, u32[]{:S(2)}, u32[]{:S(2)}) collective-permute-start(bf16[16,208,128]{2,1,0:T(8,128)(2,1)S(1)} %constant_dynamic-update-slice_fusion.lm_ref), channel_id=1, source_target_pairs={{0,1},{1,0},{2,3},{3,2},{4,5},{5,4},{6,7},{7,6},{8,9},{9,8},{10,11... | collective-permute-start | bytes 2555912 | tf_op jit(solution)/shard_map/ppermute | solution.py:261
  50.1 0.0 copy-done
  50.2 0.2 copy.7
  50.4 0.1 pad_add_fusion.at_ref
  50.5 2.0 %collective-permute-done.6.lo_ref = bf16[16,208,128]{2,1,0:T(8,128)(2,1)S(1)} collective-permute-done((bf16[16,208,128]{2,1,0:T(8,128)(2,1)S(1)}, bf16[16,208,128]{2,1,0:T(8,128)(2,1)S(1)}, u32[]{:S(2)}, u32[]{:S(2)}) %collective-permute-start.6) | collective-permute-done | bytes 852000 | tf_op jit(solution)/shard_map/ppermute | solution.py:261
  52.5 1.6 %all-to-all-done.r_ref = bf16[16,208,128]{2,1,0:T(8,128)(2,1)S(1)} async-done(((bf16[16,208,128]{2,1,0:T(8,128)(2,1)}), bf16[16,208,128]{2,1,0:T(8,128)(2,1)S(1)}, u32[]{:S(2)}, u32[]{:S(2)}) %all-to-all-start) | async-done | bytes 852000 | tf_op jit(solution)/shard_map/all_to_all | solution.py:258
  54.1 3.5 %shard_map.65 = (bf16[4,288,128]{2,1,0:T(8,128)(2,1)S(1)}, f32[1,128]{1,0:T(1,128)S(1)}) custom-call(s32[3]{0:T(128)S(1)} %pad_add_fusion.at_ref, bf16[16,208,128]{2,1,0:T(8,128)(2,1)S(1)} %all-to-all-done.r_ref, bf16[512,256]{1,0:T(8,128)(2,1)S(1)} %bitcast.15, bf16[16,208,128]{2,1,0:T(8,128)(2,1)S(1)} %constant_dynamic-update-slice_fusion.lm_ref, ...), custom_call_target="tpu_custom_call" | custom-call | flops 3221225472 | bytes 4194304 | tf_op jit(solution)/shard_map/pallas_call | solution.py:263
  57.6 10.0 %all_to_all.10.pair_ref = bf16[4,288,128]{2,1,0:T(8,128)(2,1)S(1)} all-to-all(bf16[4,288,128]{2,1,0:T(8,128)(2,1)S(1)} %get-tuple-element.13), channel_id=1, replica_groups=mesh['y'=8,'zl'=2,'x'=4,'zh'=4,'core'=2] {'x'}, dimensions={0} | all-to-all | bytes 589824 | tf_op jit(solution)/shard_map/all_to_all | solution.py:276
  67.6 0.9 %shard_map.66 = f32[12,96,128]{2,1,0:T(8,128)} custom-call(bf16[4,288,128]{2,1,0:T(8,128)(2,1)S(1)} %all_to_all.10.pair_ref, f32[1,128]{1,0:T(1,128)S(1)} %get-tuple-element.14.offset_ref), custom_call_target="tpu_custom_call" | custom-call | tf_op jit(solution)/shard_map/pallas_call | solution.py:277
  (7 shorter events, 0.2 us)
Async XLA Ops:
  2.0 18.7 %collective-permute-start.1 = (bf16[1,208,128]{2,1,0:T(8,128)(2,1)S(1)}, bf16[1,208,128]{2,1,0:T(8,128)(2,1)S(1)}, u32[]{:S(2)}, u32[]{:S(2)}) collective-permute-start(bf16[1,208,128]{2,1,0:T(8,128)(2,1)S(1)} %get-tuple-element.11), channel_id=1, source_target_pairs={{0,4},{1,5},{2,6},{3,7},{4,0},{5,1},{6,2},{7,3},{8,12},{9,13},{10,... | collective-permute-start | bytes 159752 | tf_op jit(solution)/shard_map/ppermute | solution.py:254
  12.9 11.3 %collective-permute-start = (bf16[208,128]{1,0:T(8,128)(2,1)S(1)}, bf16[208,128]{1,0:T(8,128)(2,1)S(1)}, u32[]{:S(2)}, u32[]{:S(2)}) collective-permute-start(bf16[208,128]{1,0:T(8,128)(2,1)S(1)} %get-tuple-element.10), channel_id=1, source_target_pairs={{0,256},{1,192},{2,352},{3,160},{4,480},{5,32},{6,384},{7,64},{8,2... | collective-permute-start | bytes 159752 | tf_op jit(solution)/shard_map/ppermute | solution.py:251
  20.7 11.3 %collective-permute-start.2 = (bf16[2,208,128]{2,1,0:T(8,128)(2,1)S(1)}, bf16[2,208,128]{2,1,0:T(8,128)(2,1)S(1)}, u32[]{:S(2)}, u32[]{:S(2)}) collective-permute-start(bf16[2,208,128]{2,1,0:T(8,128)(2,1)S(1)} %pad_maximum_fusion.1), channel_id=1, source_target_pairs={{0,2},{1,3},{2,0},{3,1},{4,6},{5,7},{6,4},{7,5},{8,10},{9,11},{10,... | collective-permute-start | bytes 319496 | tf_op jit(solution)/shard_map/ppermute | solution.py:256
  25.2 28.9 %all-to-all-start = ((bf16[16,208,128]{2,1,0:T(8,128)(2,1)}), bf16[16,208,128]{2,1,0:T(8,128)(2,1)S(1)}, u32[]{:S(2)}, u32[]{:S(2)}) async-start(bf16[16,208,128]{2,1,0:T(8,128)(2,1)} %broadcast_in_dim.2), calls=%async_computation | async-start | bytes 1703936 | tf_op jit(solution)/shard_map/all_to_all | solution.py:258
  32.0 10.5 %collective-permute-start.3 = (bf16[4,208,128]{2,1,0:T(8,128)(2,1)S(1)}, bf16[4,208,128]{2,1,0:T(8,128)(2,1)S(1)}, u32[]{:S(2)}, u32[]{:S(2)}) collective-permute-start(bf16[4,208,128]{2,1,0:T(8,128)(2,1)S(1)} %pad_maximum_fusion), channel_id=1, source_target_pairs={{0,8},{1,9},{2,10},{3,11},{4,12},{5,13},{6,14},{7,15},{8,16},{9,17... | collective-permute-start | bytes 638984 | tf_op jit(solution)/shard_map/ppermute | solution.py:259
  35.4 10.6 %collective-permute-start.4 = (bf16[4,208,128]{2,1,0:T(8,128)(2,1)S(1)}, bf16[4,208,128]{2,1,0:T(8,128)(2,1)S(1)}, u32[]{:S(2)}, u32[]{:S(2)}) collective-permute-start(bf16[4,208,128]{2,1,0:T(8,128)(2,1)S(1)} %pad_maximum_fusion), channel_id=1, source_target_pairs={{0,16},{1,17},{2,18},{3,19},{4,20},{5,21},{6,22},{7,23},{8,24},{9,... | collective-permute-start | bytes 638984 | tf_op jit(solution)/shard_map/ppermute | solution.py:259
  38.5 9.7 %collective-permute-start.5 = (bf16[4,208,128]{2,1,0:T(8,128)(2,1)S(1)}, bf16[4,208,128]{2,1,0:T(8,128)(2,1)S(1)}, u32[]{:S(2)}, u32[]{:S(2)}) collective-permute-start(bf16[4,208,128]{2,1,0:T(8,128)(2,1)S(1)} %pad_maximum_fusion), channel_id=1, source_target_pairs={{0,24},{1,25},{2,26},{3,27},{4,28},{5,29},{6,30},{7,31},{8,0},{9,1... | collective-permute-start | bytes 638984 | tf_op jit(solution)/shard_map/ppermute | solution.py:259
  46.0 4.1 %copy-start = (bf16[1024,128]{1,0:T(8,128)(2,1)S(1)}, bf16[1024,128]{1,0:T(8,128)(2,1)}, u32[]{:S(2)}) copy-start(bf16[1024,128]{1,0:T(8,128)(2,1)} %param.10) | copy-start | bytes 786436
  48.2 4.3 %collective-permute-start.6 = (bf16[16,208,128]{2,1,0:T(8,128)(2,1)S(1)}, bf16[16,208,128]{2,1,0:T(8,128)(2,1)S(1)}, u32[]{:S(2)}, u32[]{:S(2)}) collective-permute-start(bf16[16,208,128]{2,1,0:T(8,128)(2,1)S(1)} %constant_dynamic-update-slice_fusion.lm_ref), channel_id=1, source_target_pairs={{0,1},{1,0},{2,3},{3,2},{4,5},{5,4},{6,7},{7,6},{8,9},{9,8},{10,11... | collective-permute-start | bytes 2555912 | tf_op jit(solution)/shard_map/ppermute | solution.py:261
